TPU v7x, 256 devices: a whole 4x4x8 slice. The times are simulated.
256 devices in a mesh: dp: 16 (over x, z_lo), ctx: 16 (over z_hi, y, core).
Axes of the slice: x: 4, y: 4, z: 8 (z_hi: 2, z_lo: 4; z = z_hi * 4 + z_lo), core: 2. Of those that a mesh axis runs over, the one named last changes fastest.
Arguments:
- normed_layer_input: bfloat16 [32768, 4096], P(('dp', 'ctx')), may hold values from -6 to 6
- saved_query_state: bfloat16 [32768, 2048], P(('dp', 'ctx')), may hold values from -105 to 105
- saved_key_state: bfloat16 [32768, 512], P(('dp', 'ctx')), may hold values from -3.8 to 3.8
- saved_value_state: bfloat16 [32768, 512], P(('dp', 'ctx')), may hold values from -6 to 6
- output_cotangent: bfloat16 [32768, 2048], P(('dp', 'ctx')), may hold values from -0.5 to 0.5
- document_lengths: int32 [16, 8], P('dp'), may hold values from 1 to 1024, 2048 in all within a row
- span_order: int32 [32], replicated, may hold values from 0 to 31, each once
Outputs:
- grad_query_weight: float32 [4096, 2048], P('ctx')
- grad_key_weight: float32 [4096, 512], P('ctx')
- grad_value_weight: float32 [4096, 512], P('ctx')
Inputs may be any that keep to these rules, and one draw needn't show every extreme that they name: `document_lengths`: each sequence's 8 lengths sum to 2048, and one of them is exactly 1024. `span_order`: a permutation: every position block of a sequence is stored once.
All inputs are finite; a program needn't handle non-finite values.
Results may differ from a plain program's by a relative error of at most 0.024.
Values may be sent and summed in bfloat16 or wider, within the bound.
No kernel may reach another device: no remote copies, remote signals or barrier semaphores. Data moves between devices by JAX's collectives and lax.ppermute only.
A program may use at most 64 MiB of HBM per device.

v0:
```python
import math

import jax
import jax.numpy as jnp
from jax import lax
from jax.sharding import PartitionSpec as P

QUERY_HEADS = 16
KEY_VALUE_HEADS = 4
HEAD_WIDTH = 128


def shards(
    normed_layer_input,
    saved_query_state,
    saved_key_state,
    saved_value_state,
    output_cotangent,
    document_lengths,
    span_order,
):
    ctx_size = lax.axis_size("ctx")
    device_index = lax.axis_index("ctx")
    count_rows = saved_query_state.shape[0]
    half_rows = count_rows // 2
    sequence_rows = count_rows * ctx_size
    group_width = QUERY_HEADS // KEY_VALUE_HEADS
    score_scale = 1.0 / math.sqrt(HEAD_WIDTH)
    key_all, value_all = (
        lax.all_gather(saved_key_state, "ctx", axis=0, tiled=True),
        lax.all_gather(saved_value_state, "ctx", axis=0, tiled=True),
    )
    row_index = jnp.arange(sequence_rows, dtype=jnp.int32)
    span_ids = jnp.arange(span_order.shape[0], dtype=jnp.int32)
    span_start = jnp.sum(
        jnp.where((row_index // half_rows)[:, None] == span_ids[None, :], span_order[None, :], 0),
        axis=1,
        dtype=jnp.int32,
    )
    positions = span_start * half_rows + row_index % half_rows
    doc_ends = jnp.cumsum(document_lengths[0], dtype=jnp.int32)
    documents = jnp.sum(
        (positions[:, None] >= doc_ends[None, :]).astype(jnp.int32), axis=1, dtype=jnp.int32
    )
    first_row = device_index * count_rows
    query_pos = lax.dynamic_slice_in_dim(positions, first_row, count_rows)
    query_doc = lax.dynamic_slice_in_dim(documents, first_row, count_rows)
    visible = (positions[None, :] <= query_pos[:, None]) & (
        documents[None, :] == query_doc[:, None]
    )

    def head_cluster(head_index):
        query_group = lax.dynamic_slice_in_dim(
            saved_query_state, head_index * group_width * HEAD_WIDTH, group_width * HEAD_WIDTH, 1
        )
        query_group = query_group.reshape(count_rows, group_width, HEAD_WIDTH)
        out_group = lax.dynamic_slice_in_dim(
            output_cotangent, head_index * group_width * HEAD_WIDTH, group_width * HEAD_WIDTH, 1
        )
        out_group = out_group.reshape(count_rows, group_width, HEAD_WIDTH)
        key_group = lax.dynamic_slice_in_dim(key_all, head_index * HEAD_WIDTH, HEAD_WIDTH, 1)
        value_group = lax.dynamic_slice_in_dim(value_all, head_index * HEAD_WIDTH, HEAD_WIDTH, 1)
        scores = (
            jnp.einsum("tgd,sd->gts", query_group, key_group, preferred_element_type=jnp.float32)
            * score_scale
        )
        masked = jnp.where(visible[None], scores, -jnp.inf)
        row_max = jnp.max(masked, axis=2, keepdims=True)
        weights = jnp.where(visible[None], jnp.exp(masked - row_max), 0.0)
        probability = weights / jnp.sum(weights, axis=2, keepdims=True)
        prob_half = probability.astype(jnp.bfloat16)
        prob_grad = jnp.einsum(
            "tgd,sd->gts", out_group, value_group, preferred_element_type=jnp.float32
        )
        row_delta = jnp.sum(probability * prob_grad, axis=2, keepdims=True)
        score_grad = (probability * (prob_grad - row_delta)).astype(jnp.bfloat16)
        query_gradient = (
            jnp.einsum("gts,sd->tgd", score_grad, key_group, preferred_element_type=jnp.float32)
            * score_scale
        )
        key_portion = (
            jnp.einsum("gts,tgd->sd", score_grad, query_group, preferred_element_type=jnp.float32)
            * score_scale
        )
        value_portion = jnp.einsum(
            "gts,tgd->sd", prob_half, out_group, preferred_element_type=jnp.float32
        )
        return (
            query_gradient.reshape(count_rows, group_width * HEAD_WIDTH),
            key_portion.astype(jnp.bfloat16),
            value_portion.astype(jnp.bfloat16),
        )

    query_pile, key_pile, value_pile = lax.map(
        head_cluster, jnp.arange(KEY_VALUE_HEADS, dtype=jnp.int32)
    )
    query_gradient = (
        query_pile.transpose(1, 0, 2)
        .reshape(count_rows, QUERY_HEADS * HEAD_WIDTH)
        .astype(jnp.bfloat16)
    )
    key_portion = key_pile.transpose(1, 0, 2).reshape(sequence_rows, KEY_VALUE_HEADS * HEAD_WIDTH)
    value_portion = value_pile.transpose(1, 0, 2).reshape(
        sequence_rows, KEY_VALUE_HEADS * HEAD_WIDTH
    )
    input_cols = lax.all_to_all(normed_layer_input, "ctx", split_axis=1, concat_axis=0, tiled=True)

    def add_rows(piece_rows):
        return jnp.einsum("td,tc->dc", input_cols, piece_rows, preferred_element_type=jnp.float32)

    query_term = add_rows(lax.all_gather(query_gradient, "ctx", axis=0, tiled=True))
    key_row_block, value_row_block = (
        lax.psum_scatter(key_portion, "ctx", scatter_dimension=0, tiled=True).astype(jnp.float32),
        lax.psum_scatter(value_portion, "ctx", scatter_dimension=0, tiled=True).astype(jnp.float32),
    )
    kv_local = jnp.concatenate(
        [key_row_block.astype(jnp.bfloat16), value_row_block.astype(jnp.bfloat16)], axis=1
    )
    kv_term = add_rows(lax.all_gather(kv_local, "ctx", axis=0, tiled=True))
    query_matrix, key_value_weight = (
        lax.psum(query_term.astype(jnp.bfloat16), "dp").astype(jnp.float32),
        lax.psum(kv_term.astype(jnp.bfloat16), "dp").astype(jnp.float32),
    )
    return (
        query_matrix,
        key_value_weight[:, : KEY_VALUE_HEADS * HEAD_WIDTH],
        key_value_weight[:, KEY_VALUE_HEADS * HEAD_WIDTH :],
    )


def solution(mesh):
    return jax.shard_map(
        shards,
        mesh=mesh,
        in_specs=(
            P(("dp", "ctx"), None),
            P(("dp", "ctx"), None),
            P(("dp", "ctx"), None),
            P(("dp", "ctx"), None),
            P(("dp", "ctx"), None),
            P("dp", None),
            P(),
        ),
        out_specs=(P("ctx", None), P("ctx", None), P("ctx", None)),
        check_vma=False,
    )
```

profile of v0, /device:TPU:56, one launch (start us, length us, event | category | flops | bytes accessed | tf_op | source)
XLA Modules:
  0.0 791.9 jit_solution(15448741681854335847)
XLA Ops:
  10.6 64.2 %all-gather.5.cloned.1.call-done = bf16[2048,512]{1,0:T(8,128)(2,1)} async-done(((bf16[128,512]{1,0:T(8,128)(2,1)}), bf16[2048,512]{1,0:T(8,128)(2,1)}) %all-gather.5.cloned.1.call-update) | async-done | bytes 2097168 | tf_op jit(solution)/shard_map/all_gather | solution.py:30
  74.8 61.3 %all-gather.7.cloned.1.call-done = bf16[2048,512]{1,0:T(8,128)(2,1)} async-done(((bf16[128,512]{1,0:T(8,128)(2,1)}), bf16[2048,512]{1,0:T(8,128)(2,1)}) %all-gather.7.cloned.1.call-update) | async-done | bytes 2097168 | tf_op jit(solution)/shard_map/all_gather | solution.py:31
  136.2 93.1 %while.17 = (s32[]{:T(128)}, bf16[4,128,512]{1,2,0:T(8,128)(2,1)}, bf16[4,2048,128]{1,2,0:T(8,128)(2,1)}, bf16[4,2048,128]{1,2,0:T(8,128)(2,1)}, s32[4]{0:T(128)...) while((s32[]{:T(128)}, bf16[4,128,512]{1,2,0:T(8,128)(2,1)}, ...), condition=%wide.region_7.8_spmd.clone, body=%wide.region_3.7_spmd.clone.sunk | while | flops 1358562816 | bytes 57833796 | solution.py:94
  140.4 4.6 fusion.86
  146.1 3.2 fusion.87
  151.3 3.7 fusion.89
  163.7 4.6 fusion.86
  169.4 3.2 fusion.87
  174.5 3.7 fusion.89
  187.0 4.6 fusion.86
  192.7 3.2 fusion.87
  197.8 3.7 fusion.89
  210.3 4.6 fusion.86
  215.9 3.2 fusion.87
  221.1 3.7 fusion.89
  229.2 4.1 copy.80
  236.0 79.9 %reduce-scatter.7.cloned.1.call-done = bf16[128,512]{1,0:T(8,128)(2,1)} async-done(((bf16[2048,512]{1,0:T(8,128)(2,1)}), bf16[128,512]{1,0:T(8,128)(2,1)}) %reduce-scatter.7.cloned.1.call-update) | async-done | bytes 131088
  316.9 87.2 %reduce-scatter.9.cloned.1.call-done = bf16[128,512]{1,0:T(8,128)(2,1)} async-done(((bf16[2048,512]{1,0:T(8,128)(2,1)}), bf16[128,512]{1,0:T(8,128)(2,1)}) %reduce-scatter.9.cloned.1.call-update) | async-done | bytes 131088
  407.1 39.9 %all_to_all.19 = bf16[128,16,256]{0,2,1:T(8,128)(2,1)S(1)} all-to-all(bf16[128,16,256]{0,2,1:T(8,128)(2,1)S(1)} %bitcast.135), channel_id=1, replica_groups=mesh['dp'=16,'ctx'=16] {'ctx'}, dimensions={1} | all-to-all | bytes 2097152 | tf_op jit(solution)/shard_map/all_to_all | solution.py:106
  447.6 46.1 %all-gather.11.cloned.1.call-done = bf16[2048,1024]{0,1:T(8,128)(2,1)} async-done(((bf16[128,1024]{0,1:T(8,128)(2,1)}), bf16[2048,1024]{0,1:T(8,128)(2,1)}) %all-gather.11.cloned.1.call-update) | async-done | bytes 4194320 | tf_op jit(solution)/shard_map/all_gather | solution.py:119
  493.7 4.2 fusion.40
  497.9 108.1 %all-gather.9.cloned.1.call-done = bf16[2048,2048]{0,1:T(8,128)(2,1)} async-done(((bf16[128,2048]{0,1:T(8,128)(2,1)}), bf16[2048,2048]{0,1:T(8,128)(2,1)}) %all-gather.9.cloned.1.call-update) | async-done | bytes 8388624 | tf_op jit(solution)/shard_map/all_gather | solution.py:111
  606.0 6.7 fusion.39
  612.7 166.7 %all-reduce.3.cloned.1.call-done = (bf16[256,2048]{0,1:T(8,128)(2,1)}, bf16[256,1024]{0,1:T(8,128)(2,1)}) async-done(((bf16[256,2048]{0,1:T(8,128)(2,1)}, bf16[256,1024]{0,1:T(8,128)(2,1)}), (bf16[256,2048]{0,1:T(8,128)(2,1)}, bf16[256,1024]{0,1:T(8,128)(2,1)})) %all-reduce.3.cloned.1.call-update) | async-done | bytes 1572880 | tf_op jit(solution)/shard_map/psum | solution.py:121
  (99 shorter events, 57.5 us)
Async XLA Ops:
  7.2 67.7 %all-gather.5.cloned.1.call-start = ((), (), s32[]{:S(2)}) async-start(), calls=%async_computation.3 | async-start | bytes 2228224 | tf_op jit(solution)/shard_map/all_gather | solution.py:30
  7.9 128.3 %all-gather.7.cloned.1.call-start = ((), (), s32[]{:S(2)}) async-start(), calls=%async_computation.4 | async-start | bytes 2228224 | tf_op jit(solution)/shard_map/all_gather | solution.py:31
  8.6 307.2 %reduce-scatter.7.cloned.1.call-start = ((), (), s32[]{:S(2)}) async-start(), calls=%async_computation.7 | async-start | bytes 2228224
  146.1 3.6 copy-start
  169.4 3.6 copy-start
  192.7 3.6 copy-start
  215.9 3.6 copy-start
  229.2 4.1 copy-start.1
  233.3 173.1 %copy-start.2 = (bf16[128,4096]{1,0:T(8,128)(2,1)S(1)}, bf16[128,4096]{1,0:T(8,128)(2,1)}, u32[]{:S(2)}) copy-start(bf16[128,4096]{1,0:T(8,128)(2,1)} %param.9) | copy-start | bytes 3145732
  233.3 170.7 %reduce-scatter.9.cloned.1.call-start = ((), (), s32[]{:S(2)}) async-start(), calls=%async_computation.8 | async-start | bytes 2228224
  235.9 257.7 %all-gather.11.cloned.1.call-start = ((), (), s32[]{:S(2)}) async-start(), calls=%async_computation.6 | async-start | bytes 4456448 | tf_op jit(solution)/shard_map/all_gather | solution.py:119
  405.8 200.2 %all-gather.9.cloned.1.call-start = ((), (), s32[]{:S(2)}) async-start(), calls=%async_computation.5 | async-start | bytes 8912896 | tf_op jit(solution)/shard_map/all_gather | solution.py:111
  406.4 373.0 %all-reduce.3.cloned.1.call-start = ((), (), s32[]{:S(2)}) async-start(), calls=%async_computation.9 | async-start | bytes 3145728 | tf_op jit(solution)/shard_map/psum | solution.py:121
Sparse Core Ops, SparseCore 0:
  10.7 64.0 all-gather.4
  77.6 58.5 all-gather.6
  233.4 82.3 reduce-scatter.6
  320.5 83.4 reduce-scatter.8
  407.0 86.5 all-gather.10
  496.6 109.2 all-gather.8
  612.8 166.5 all-reduce.2
where the time goes:
time: 795 us; the launch traced here: 792 us
  waiting for transfers between devices  615 us (77%)
  matrix products  66 us (8%)
  local copies, waits for them, and re-layouts  40.5 us (5%)
  blocking collectives  39.9 us (5%)
  between operations  14.2 us (2%)
  other arithmetic  10 us (1%)
    unnamed x9, waiting for transfers between devices  169 us
    psum x1, waiting for transfers between devices, shards(): lax.psum(query_term.astype(jnp.bfloat16), 'dp').astype(jnp.float32)  167 us
    all_gather x1, waiting for transfers between devices, shards(): lax.all_gather(query_gradient, 'ctx', axis=0, tiled=True)  108 us
    all_gather x1, waiting for transfers between devices, shards(): lax.all_gather(saved_key_state, 'ctx', axis=0, tiled=True)  64.2 us
    all_gather x1, waiting for transfers between devices, shards(): lax.all_gather(saved_value_state, 'ctx', axis=0, tiled=True)  61.3 us
    all_gather x1, waiting for transfers between devices, shards(): kv_term = add_rows(lax.all_gather(kv_local, 'ctx', axis=0, tiled=True))  46.1 us
    all_to_all x1, blocking collectives, shards(): lax.all_to_all(normed_layer_input, 'ctx', split_axis=1, concat_axis=0, ti...  39.9 us
    sub x4, matrix products, head_cluster(): weights = jnp.where(visible[None], jnp.exp(masked - row_max), 0.0)  18.6 us
  transfers between devices with their start and end apart: 7, of which 7 were waited for; matrix products, arithmetic and copies ran while one was open for 1% of the time, Pallas kernels for 0%

commit v1 on v0

v1 whole, which is shorter than its diff:
```python
import functools
import math

import jax
import jax.numpy as jnp
from jax import lax
from jax.experimental import pallas as pl
from jax.experimental.pallas import tpu as pltpu
from jax.sharding import Mesh, PartitionSpec as P

HEAD = 128
KV_HEADS = 4
HALF = 64
SPANS = 32
SEQ = 2048
NX, NZL, NZH, NY, NC = 4, 4, 2, 4, 2
ROWS = 128
OWN = ROWS * NY * NC
FEATS = 256
SCALE = 1.0 / math.sqrt(HEAD)
LOG2E = math.log2(math.e)
TILE = 256
VMEM = 56 * 1024 * 1024
AXES = ("x", "zl", "zh", "y", "c")


def nt(a, b):
    return lax.dot_general(a, b, (((1,), (1,)), ((), ())), preferred_element_type=jnp.float32)


def tn(a, b):
    return lax.dot_general(a, b, (((0,), (0,)), ((), ())), preferred_element_type=jnp.float32)


def nn(a, b):
    return lax.dot_general(a, b, (((1,), (0,)), ((), ())), preferred_element_type=jnp.float32)


def attention_kernel(ids, span, lens, own, other, dq_ref, dkv_ref, ks, vs, dk, dv):
    zh, core = ids[0], ids[1]
    blocks = OWN // HALF
    for j in range(blocks):
        rows = slice((j % 2) * HALF, (j % 2) * HALF + HALF)
        at = pl.ds(pl.multiple_of(span[zh * blocks + j] * HALF, HALF), HALF)
        ks[at, :] = own[j // 2, rows, 4 * HEAD : 5 * HEAD]
        vs[at, :] = own[j // 2, rows, 5 * HEAD : 6 * HEAD]
        at = pl.ds(pl.multiple_of(span[(1 - zh) * blocks + j] * HALF, HALF), HALF)
        ks[at, :] = other[j // 2, rows, :HEAD]
        vs[at, :] = other[j // 2, rows, HEAD:]
    dk[...] = jnp.zeros_like(dk)
    dv[...] = jnp.zeros_like(dv)
    ends = []
    total = jnp.int32(0)
    for d in range(lens.shape[1]):
        total = total + lens[0, d]
        ends.append(total)
    lane = lax.broadcasted_iota(jnp.int32, (1, 2 * HALF), 1) % HALF

    def block(j, carry):
        first = span[zh * blocks + j] * HALF
        low = jnp.int32(0)
        for e in ends:
            low = jnp.where(e <= first, e, low)
        high = pl.cdiv(first + HALF, 2 * HALF) * (2 * HALF)
        tiles = pl.cdiv(high - low, TILE)
        half, part = j // 2, pl.multiple_of((j % 2) * HALF, HALF)
        q = jnp.concatenate(
            [own[half, pl.ds(part, HALF), :HEAD], own[half, pl.ds(part, HALF), HEAD : 2 * HEAD]], axis=0
        )
        do = jnp.concatenate(
            [own[half, pl.ds(part, HALF), 2 * HEAD : 3 * HEAD], own[half, pl.ds(part, HALF), 3 * HEAD : 4 * HEAD]],
            axis=0,
        )
        pos = first + lane
        doc = jnp.zeros_like(pos)
        for e in ends:
            doc = jnp.where(e <= pos, e, doc)

        def work(n):
            keys = n * TILE
            start = pl.multiple_of(jnp.maximum(high - keys, 0), 2 * HALF)
            at = pl.ds(start, keys)
            k, v = ks[at, :], vs[at, :]
            row = lax.broadcasted_iota(jnp.int32, (keys, 2 * HALF), 0)
            seen = (row >= doc - start) & (row <= pos - start)
            s = jnp.where(seen, nt(k, q), -1e30)
            top = jnp.max(s, axis=0, keepdims=True)
            p = jnp.exp2((s - top) * (SCALE * LOG2E))
            p = p * (1.0 / jnp.sum(p, axis=0, keepdims=True))
            dp = nt(v, do)
            delta = jnp.sum(p * dp, axis=0, keepdims=True)
            ds = (p * (dp - delta)).astype(jnp.bfloat16)
            dv[at, :] += nn(p.astype(jnp.bfloat16), do)
            dk[at, :] += nn(ds, q)
            g = (tn(ds, k) * SCALE).astype(jnp.bfloat16)
            out = pl.ds(pl.multiple_of(j * HALF, HALF), HALF)
            dq_ref[out, :HEAD] = g[:HALF]
            dq_ref[out, HEAD:] = g[HALF:]

        for n in range(1, 6):
            pl.when(tiles == n)(functools.partial(work, n))
        return carry

    lax.fori_loop(0, blocks, block, 0)
    for j in range(blocks):
        for side, base in ((zh, 0), (1 - zh, OWN)):
            at = pl.ds(pl.multiple_of(span[side * blocks + j] * HALF, HALF), HALF)
            to = slice(base + j * HALF, base + (j + 1) * HALF)
            dkv_ref[core, to, :] = (dk[at, :] * SCALE).astype(jnp.bfloat16)
            dkv_ref[1 - core, to, :] = dv[at, :].astype(jnp.bfloat16)


def attention(ids, span, lens, own, other):
    smem = pl.BlockSpec(memory_space=pltpu.SMEM)
    vmem = pl.BlockSpec(memory_space=pltpu.VMEM)
    return pl.pallas_call(
        attention_kernel,
        out_shape=(
            jax.ShapeDtypeStruct((OWN, 2 * HEAD), jnp.bfloat16),
            jax.ShapeDtypeStruct((2, SEQ, HEAD), jnp.bfloat16),
        ),
        in_specs=[smem, smem, smem, vmem, vmem],
        out_specs=(vmem, vmem),
        scratch_shapes=[
            pltpu.VMEM((SEQ, HEAD), jnp.bfloat16),
            pltpu.VMEM((SEQ, HEAD), jnp.bfloat16),
            pltpu.VMEM((SEQ, HEAD), jnp.float32),
            pltpu.VMEM((SEQ, HEAD), jnp.float32),
        ],
        compiler_params=pltpu.CompilerParams(vmem_limit_bytes=VMEM),
        name="attention_backward",
    )(ids, span, lens, own, other)


def weight_kernel(x_ref, g_ref, out_ref):
    r = tn(x_ref[...], g_ref[...]).astype(jnp.bfloat16)
    out_ref[:, 0, 0] = r.reshape(out_ref.shape[0], out_ref.shape[3], out_ref.shape[4])


def weight_term(x, g):
    cols = g.shape[1]
    return pl.pallas_call(
        weight_kernel,
        grid=(NZH * NY,),
        out_shape=jax.ShapeDtypeStruct((NX, NY, NZH, FEATS // NX, cols), jnp.bfloat16),
        in_specs=[
            pl.BlockSpec((OWN, FEATS), lambda i: (0, i)),
            pl.BlockSpec((OWN, cols), lambda i: (0, 0)),
        ],
        out_specs=pl.BlockSpec((NX, 1, 1, FEATS // NX, cols), lambda i: (0, i % NY, i // NY, 0, 0)),
        compiler_params=pltpu.CompilerParams(vmem_limit_bytes=VMEM),
        name="weight_term",
    )(x, g)


def finish_kernel(ids, a, b, c, d, q_ref, k_ref, v_ref):
    x, zl = ids[0], ids[1]
    sub = FEATS // (NX * NZL)
    cols = KV_HEADS * HEAD
    for sx, piece in enumerate((a, b, c, d)):
        for sz in range(NZL):
            row = lax.rem(x - sx + NX, NX) * (FEATS // NX) + lax.rem(zl - sz + NZL, NZL) * sub
            at = pl.ds(pl.multiple_of(row, sub), sub)
            for y in range(NY):
                got = piece[sz, y].astype(jnp.float32)
                q_ref[at, y * cols : (y + 1) * cols] = got[:, :cols]
                k_ref[at, y * HEAD : (y + 1) * HEAD] = got[:, cols : cols + HEAD]
                v_ref[at, y * HEAD : (y + 1) * HEAD] = got[:, cols + HEAD :]


def finish(ids, pieces):
    smem = pl.BlockSpec(memory_space=pltpu.SMEM)
    vmem = pl.BlockSpec(memory_space=pltpu.VMEM)
    cols = KV_HEADS * HEAD
    return pl.pallas_call(
        finish_kernel,
        out_shape=(
            jax.ShapeDtypeStruct((FEATS, NY * cols), jnp.float32),
            jax.ShapeDtypeStruct((FEATS, cols), jnp.float32),
            jax.ShapeDtypeStruct((FEATS, cols), jnp.float32),
        ),
        in_specs=[smem, vmem, vmem, vmem, vmem],
        out_specs=(vmem, vmem, vmem),
        compiler_params=pltpu.CompilerParams(vmem_limit_bytes=VMEM),
        name="finish",
    )(ids, *pieces)


def shift(value, axis, n, s):
    return lax.ppermute(value, axis, [(i, (i + s) % n) for i in range(n)])


def by_head(value, copies):
    return jnp.broadcast_to(value.reshape(ROWS, KV_HEADS, 1, HEAD), (ROWS, KV_HEADS, copies, HEAD)).reshape(
        ROWS, KV_HEADS * copies, HEAD
    )


def in_order(first, mine, got, axis):
    return jnp.where(
        first, jnp.concatenate([mine, got], axis=axis), jnp.concatenate([got, mine], axis=axis)
    )


def reduce_term(term):
    cols = term.shape[-1]
    sub = FEATS // (NX * NZL)
    got = lax.all_to_all(term.reshape(NX * NY, NZH * FEATS // NX, cols), ("x", "y"), 0, 0, tiled=True)
    got = got.reshape(NX, NY, NZH, NZL, sub, cols)
    part = jnp.sum(got.astype(jnp.float32), axis=0).astype(jnp.bfloat16)
    part = part.transpose(1, 2, 0, 3, 4).reshape(NZH * NZL, NY * sub, cols)
    got = lax.all_to_all(part, ("zh", "zl"), 0, 0, tiled=True).reshape(NZH * NZL, NY, sub, cols)
    return jnp.sum(got.astype(jnp.float32), axis=0).astype(jnp.bfloat16)


def shards(x, q, k, v, do, lens, span):
    ix, izl, izh, core = (lax.axis_index(a) for a in ("x", "zl", "zh", "c"))
    first = core == 0
    groups = NY * NC

    kv_other = shift(jnp.concatenate([k, v], axis=1), "zh", NZH, 1)
    send = jnp.concatenate(
        [
            q.reshape(ROWS, groups, 2 * HEAD),
            do.reshape(ROWS, groups, 2 * HEAD),
            by_head(k, NC),
            by_head(v, NC),
        ],
        axis=2,
    ).transpose(1, 0, 2)
    own = lax.all_to_all(send, ("y", "c"), 0, 0, tiled=True)
    k_o, v_o = kv_other[:, : KV_HEADS * HEAD], kv_other[:, KV_HEADS * HEAD :]
    send = jnp.concatenate([by_head(k_o, NC), by_head(v_o, NC)], axis=2).transpose(1, 0, 2)
    other = lax.all_to_all(send, ("y", "c"), 0, 0, tiled=True)

    by_class = x.reshape(ROWS, NZH * NY, NC, FEATS)
    keep = jnp.where(first, by_class[:, :, 0], by_class[:, :, 1]).reshape(ROWS, -1)
    give = jnp.where(first, by_class[:, :, 1], by_class[:, :, 0]).reshape(ROWS, -1)
    pair = in_order(first, keep, shift(give, "c", NC, 1), 0)
    x_all = lax.all_gather(pair, "y", axis=0, tiled=True)

    dq, dkv = attention(jnp.stack([izh, core]).astype(jnp.int32), span, lens, own, other)

    gq = in_order(first, dq, shift(dq, "c", NC, 1), 1)
    got = shift(dkv[1], "c", NC, 1)
    both = dkv[0].astype(jnp.float32) + got.astype(jnp.float32)
    got = shift(both[OWN:].astype(jnp.bfloat16), "zh", NZH, 1)
    mine = (both[:OWN] + got.astype(jnp.float32)).astype(jnp.bfloat16)
    gkv = in_order(first, mine, shift(mine, "c", NC, 1), 1)

    piece = jnp.concatenate(
        [reduce_term(weight_term(x_all, gq)), reduce_term(weight_term(x_all, gkv))], axis=2
    )
    line = jnp.stack([piece] + [shift(piece, "zl", NZL, s) for s in range(1, NZL)])
    pieces = [line] + [shift(line, "x", NX, s) for s in range(1, NX)]
    return finish(jnp.stack([ix, izl]).astype(jnp.int32), pieces)


def solution(mesh):
    fine = Mesh(mesh.devices.reshape(NX, NZL, NZH, NY, NC), AXES)
    rows = P(AXES, None)
    out = P(("zh", "y", "c"), None)
    return jax.shard_map(
        shards,
        mesh=fine,
        in_specs=(rows, rows, rows, rows, rows, P(("x", "zl"), None), P()),
        out_specs=(out, out, out),
        check_vma=False,
    )
```

time: 795 us -> 265 us (0.33)
  waiting for transfers between devices: 615 us -> 134 us
  matrix products: 66 us -> 0 us
  starting transfers between devices: 0.28 us -> 60.5 us
  blocking collectives: 39.9 us -> 0 us
  Pallas kernels: 0 us -> 33.5 us
  local copies, waits for them, and re-layouts: 40.5 us -> 9.39 us
    all_gather x4 -> x1, waiting for transfers between devices: 280 us -> 0.01 us  [shards(): x_all = lax.all_gather(pair, 'y', axis=0, tiled=True)]
    unnamed x9 -> x1, waiting for transfers between devices: 169 us -> 0.02 us
    psum x1 -> x0, waiting for transfers between devices: 167 us -> none  [shards(): lax.psum(query_term.astype(jnp.bfloat16), 'dp').astype(jnp.float32)]
    all_to_all x0 -> x6, waiting for transfers between devices: none -> 88.1 us  [the longest x1 29.8 us: shards(): own = lax.all_to_all(send, ('y', 'c'), 0, 0, tiled=True)]
    dot_general x18 -> x0, matrix products: 47.5 us -> none  [the longest x4 14.8 us: head_cluster(): jnp.einsum('gts,tgd->sd', prob_half, out_group, preferred_element_type=jn...]
    ppermute x0 -> x12, waiting for transfers between devices: none -> 46 us  [shift(): return lax.ppermute(value, axis, [(i, (i + s) % n) for i in range(n)])]
    all_to_all x1 -> x0, blocking collectives: 39.9 us -> none  [shards(): lax.all_to_all(normed_layer_input, 'ctx', split_axis=1, concat_axis=0, ti...]
    all_to_all x0 -> x6, starting transfers between devices: none -> 37.3 us  [the longest x2 13.6 us: reduce_term(): lax.all_to_all(term.reshape(NX * NY, NZH * FEATS // NX, cols), ('x', 'y')...]
  transfers between devices with their start and end apart: 7 -> 19, of which waited for: 7 -> 18; matrix products, arithmetic and copies ran while one was open for 1% -> 4% of each run, Pallas kernels for 0% -> 9%
where the time goes in v1:
time: 265 us; the launch traced here: 261 us
  waiting for transfers between devices  134 us (51%)
  starting transfers between devices  60.5 us (23%)
  Pallas kernels  33.5 us (13%)
  between operations  14.4 us (5%)
  local copies, waits for them, and re-layouts  9.39 us (4%)
  other arithmetic  9.04 us (3%)
    ppermute x12, waiting for transfers between devices, shift(): return lax.ppermute(value, axis, [(i, (i + s) % n) for i in range(n)])  46 us
    all_to_all x1, waiting for transfers between devices, shards(): own = lax.all_to_all(send, ('y', 'c'), 0, 0, tiled=True)  29.8 us
    all_to_all x2, waiting for transfers between devices, reduce_term(): lax.all_to_all(term.reshape(NX * NY, NZH * FEATS // NX, cols), ('x', 'y')...  28.1 us
    ppermute x12, starting transfers between devices, shift(): return lax.ppermute(value, axis, [(i, (i + s) % n) for i in range(n)])  23.2 us
    all_to_all x2, waiting for transfers between devices, reduce_term(): lax.all_to_all(part, ('zh', 'zl'), 0, 0, tiled=True)  18.5 us
    pallas_call x2, Pallas kernels, weight_term(): pl.pallas_call(weight_kernel, grid=(NZH * NY,), out_shape=jax.ShapeDtypeS...  15.4 us
    pallas_call x1, Pallas kernels, attention(): pl.pallas_call(attention_kernel, out_shape=(jax.ShapeDtypeStruct((OWN, 2...  14.8 us
    all_to_all x2, starting transfers between devices, reduce_term(): lax.all_to_all(term.reshape(NX * NY, NZH * FEATS // NX, cols), ('x', 'y')...  13.6 us
  transfers between devices with their start and end apart: 19, of which 18 were waited for; matrix products, arithmetic and copies ran while one was open for 4% of the time, Pallas kernels for 9%

profile of v1, /device:TPU:56, one launch (start us, length us, event | category | flops | bytes accessed | tf_op | source)
XLA Modules:
  0.0 260.9 jit_solution(11494065007343293941)
XLA Ops:
  14.2 6.4 %collective-permute-start.1 = (bf16[128,1024]{1,0:T(8,128)(2,1)S(1)}, bf16[128,1024]{1,0:T(8,128)(2,1)S(1)}, u32[]{:S(2)}, u32[]{:S(2)}) collective-permute-start(bf16[128,1024]{1,0:T(8,128)(2,1)S(1)} %pad_maximum_fusion.1), channel_id=1, source_target_pairs={{0,8},{8,0},{1,9},{9,1},{2,10},{10,2},{3,11},{11,3},{4,12},{12,4},... | collective-permute-start | bytes 786440 | tf_op jit(solution)/shard_map/ppermute | solution.py:190
  20.6 12.3 %collective-permute-done.1 = bf16[128,1024]{1,0:T(8,128)(2,1)S(1)} collective-permute-done((bf16[128,1024]{1,0:T(8,128)(2,1)S(1)}, bf16[128,1024]{1,0:T(8,128)(2,1)S(1)}, u32[]{:S(2)}, u32[]{:S(2)}) %collective-permute-start.1) | collective-permute-done | bytes 262176 | tf_op jit(solution)/shard_map/ppermute | solution.py:190
  33.9 4.7 %all-to-all-start.1 = ((bf16[8,128,256]{2,1,0:T(8,128)(2,1)}), bf16[8,128,256]{2,1,0:T(8,128)(2,1)S(1)}, u32[]{:S(2)}, u32[]{:S(2)}) async-start(bf16[8,128,256]{2,1,0:T(8,128)(2,1)} %maximum_bitcast_fusion.1), calls=%async_computation.1 | async-start | bytes 1048576 | tf_op jit(solution)/shard_map/all_to_all | solution.py:234
  41.1 11.8 %all-to-all-done.1.other = bf16[8,128,256]{2,1,0:T(8,128)(2,1)S(1)} async-done(((bf16[8,128,256]{2,1,0:T(8,128)(2,1)}), bf16[8,128,256]{2,1,0:T(8,128)(2,1)S(1)}, u32[]{:S(2)}, u32[]{:S(2)}) %all-to-all-start.1) | async-done | bytes 524320 | tf_op jit(solution)/shard_map/all_to_all | solution.py:234
  52.8 5.6 %all-to-all-start = ((bf16[8,128,768]{2,1,0:T(8,128)(2,1)}), bf16[8,128,768]{2,1,0:T(8,128)(2,1)S(1)}, u32[]{:S(2)}, u32[]{:S(2)}) async-start(bf16[8,128,768]{2,1,0:T(8,128)(2,1)} %maximum_bitcast_fusion), calls=%async_computation | async-start | bytes 3145728 | tf_op jit(solution)/shard_map/all_to_all | solution.py:231
  59.0 29.8 %all-to-all-done.own = bf16[8,128,768]{2,1,0:T(8,128)(2,1)S(1)} async-done(((bf16[8,128,768]{2,1,0:T(8,128)(2,1)}), bf16[8,128,768]{2,1,0:T(8,128)(2,1)S(1)}, u32[]{:S(2)}, u32[]{:S(2)}) %all-to-all-start) | async-done | bytes 1572896 | tf_op jit(solution)/shard_map/all_to_all | solution.py:231
  90.0 14.8 %attention_backward.1 = (bf16[1024,256]{1,0:T(8,128)(2,1)}, bf16[2,2048,128]{2,1,0:T(8,128)(2,1)}) custom-call(s32[2]{0:T(128)} %pad_add_fusion.1.ids, s32[32]{0:T(128)} %span.1, s32[1,8]{1,0:T(1,128)} %lens.1, bf16[8,128,768]{2,1,0:T(8,128)(2,1)} %copy-done, bf16[8,128,256]{2,1,0:T(8,128)(2,1)} %copy-done.1), custom_call_target="tpu_custom_call" | custom-call | tf_op jit(solution)/shard_map/attention_backward/pallas_call | solution.py:116
  109.1 4.6 %collective-permute-start.4 = (bf16[1024,128]{1,0:T(8,128)(2,1)S(1)}, bf16[1024,128]{1,0:T(8,128)(2,1)S(1)}, u32[]{:S(2)}, u32[]{:S(2)}) collective-permute-start(bf16[1024,128]{1,0:T(8,128)(2,1)S(1)} %slice.49), channel_id=1, source_target_pairs={{0,8},{8,0},{1,9},{9,1},{2,10},{10,2},{3,11},{11,3},{4,12},{12,4},... | collective-permute-start | bytes 786440 | tf_op jit(solution)/shard_map/ppermute | solution.py:190
  113.7 12.9 %collective-permute-done.4 = bf16[1024,128]{1,0:T(8,128)(2,1)S(1)} collective-permute-done((bf16[1024,128]{1,0:T(8,128)(2,1)S(1)}, bf16[1024,128]{1,0:T(8,128)(2,1)S(1)}, u32[]{:S(2)}, u32[]{:S(2)}) %collective-permute-start.4) | collective-permute-done | bytes 262176 | tf_op jit(solution)/shard_map/ppermute | solution.py:190
  129.2 7.3 %weight_term.3 = bf16[4,4,2,64,256]{4,3,2,1,0:T(8,128)(2,1)} custom-call(bf16[1024,2048]{1,0:T(8,128)(2,1)} %all-gather.2.cloned.1.call-done.x_ref, bf16[1024,256]{1,0:T(8,128)(2,1)} %maximum_select_fusion.2.g_ref), custom_call_target="tpu_custom_call" | custom-call | tf_op jit(solution)/shard_map/weight_term/pallas_call | solution.py:142
  136.5 7.0 %all-to-all-start.4 = ((bf16[16,128,256]{2,1,0:T(8,128)(2,1)}), bf16[16,128,256]{2,1,0:T(8,128)(2,1)S(1)}, u32[]{:S(2)}, u32[]{:S(2)}) async-start(bf16[16,128,256]{2,1,0:T(8,128)(2,1)} %bitcast.63), calls=%async_computation.4 | async-start | bytes 2097152 | tf_op jit(solution)/shard_map/all_to_all | solution.py:208
  147.0 8.1 %weight_term.2 = bf16[4,4,2,64,512]{4,3,2,1,0:T(8,128)(2,1)} custom-call(bf16[1024,2048]{1,0:T(8,128)(2,1)} %all-gather.2.cloned.1.call-done.x_ref, bf16[1024,512]{1,0:T(8,128)(2,1)} %maximum_select_fusion.1.g_ref), custom_call_target="tpu_custom_call" | custom-call | tf_op jit(solution)/shard_map/weight_term/pallas_call | solution.py:142
  155.2 3.5 %all-to-all-done.4 = bf16[16,128,256]{2,1,0:T(8,128)(2,1)S(1)} async-done(((bf16[16,128,256]{2,1,0:T(8,128)(2,1)}), bf16[16,128,256]{2,1,0:T(8,128)(2,1)S(1)}, u32[]{:S(2)}, u32[]{:S(2)}) %all-to-all-start.4) | async-done | bytes 1048608 | tf_op jit(solution)/shard_map/all_to_all | solution.py:208
  158.7 6.6 %all-to-all-start.2 = ((bf16[16,128,512]{2,1,0:T(8,128)(2,1)}), bf16[16,128,512]{2,1,0:T(8,128)(2,1)S(1)}, u32[]{:S(2)}, u32[]{:S(2)}) async-start(bf16[16,128,512]{2,1,0:T(8,128)(2,1)} %bitcast.60), calls=%async_computation.2 | async-start | bytes 4194304 | tf_op jit(solution)/shard_map/all_to_all | solution.py:208
  166.2 24.5 %all-to-all-done.2 = bf16[16,128,512]{2,1,0:T(8,128)(2,1)S(1)} async-done(((bf16[16,128,512]{2,1,0:T(8,128)(2,1)}), bf16[16,128,512]{2,1,0:T(8,128)(2,1)S(1)}, u32[]{:S(2)}, u32[]{:S(2)}) %all-to-all-start.2) | async-done | bytes 2097184 | tf_op jit(solution)/shard_map/all_to_all | solution.py:208
  190.7 8.1 %all-to-all-start.5 = ((bf16[8,64,256]{2,1,0:T(8,128)(2,1)}), bf16[8,64,256]{2,1,0:T(8,128)(2,1)S(1)}, u32[]{:S(2)}, u32[]{:S(2)}) async-start(bf16[8,64,256]{2,1,0:T(8,128)(2,1)} %bitcast.22), calls=%async_computation.5 | async-start | bytes 524288 | tf_op jit(solution)/shard_map/all_to_all | solution.py:212
  200.1 7.3 %all-to-all-done.5 = bf16[8,64,256]{2,1,0:T(8,128)(2,1)S(1)} async-done(((bf16[8,64,256]{2,1,0:T(8,128)(2,1)}), bf16[8,64,256]{2,1,0:T(8,128)(2,1)S(1)}, u32[]{:S(2)}, u32[]{:S(2)}) %all-to-all-start.5) | async-done | bytes 262176 | tf_op jit(solution)/shard_map/all_to_all | solution.py:212
  207.5 5.3 %all-to-all-start.3 = ((bf16[8,64,512]{2,1,0:T(8,128)(2,1)}), bf16[8,64,512]{2,1,0:T(8,128)(2,1)S(1)}, u32[]{:S(2)}, u32[]{:S(2)}) async-start(bf16[8,64,512]{2,1,0:T(8,128)(2,1)} %bitcast.15), calls=%async_computation.3 | async-start | bytes 1048576 | tf_op jit(solution)/shard_map/all_to_all | solution.py:212
  212.8 11.1 %all-to-all-done.3 = bf16[8,64,512]{2,1,0:T(8,128)(2,1)S(1)} async-done(((bf16[8,64,512]{2,1,0:T(8,128)(2,1)}), bf16[8,64,512]{2,1,0:T(8,128)(2,1)S(1)}, u32[]{:S(2)}, u32[]{:S(2)}) %all-to-all-start.3) | async-done | bytes 524320 | tf_op jit(solution)/shard_map/all_to_all | solution.py:212
  226.5 3.6 %collective-permute-start.7 = (bf16[4,16,768]{2,1,0:T(8,128)(2,1)S(1)}, bf16[4,16,768]{2,1,0:T(8,128)(2,1)S(1)}, u32[]{:S(2)}, u32[]{:S(2)}) collective-permute-start(bf16[4,16,768]{2,1,0:T(8,128)(2,1)S(1)} %get-tuple-element.14), channel_id=1, source_target_pairs={{0,32},{16,48},{32,0},{48,16},{1,33},{17,49},{33,1},{49,17},{2,34}... | collective-permute-start | bytes 294920 | tf_op jit(solution)/shard_map/ppermute | solution.py:190
  230.3 3.5 %collective-permute-done.7 = bf16[4,16,768]{2,1,0:T(8,128)(2,1)S(1)} collective-permute-done((bf16[4,16,768]{2,1,0:T(8,128)(2,1)S(1)}, bf16[4,16,768]{2,1,0:T(8,128)(2,1)S(1)}, u32[]{:S(2)}, u32[]{:S(2)}) %collective-permute-start.7) | collective-permute-done | bytes 98336 | tf_op jit(solution)/shard_map/ppermute | solution.py:190
  237.4 3.2 %collective-permute-start.11 = (bf16[4,4,16,768]{3,2,1,0:T(8,128)(2,1)S(1)}, bf16[4,4,16,768]{3,2,1,0:T(8,128)(2,1)S(1)}, u32[]{:S(2)}, u32[]{:S(2)}) collective-permute-start(bf16[4,4,16,768]{3,2,1,0:T(8,128)(2,1)S(1)} %pad_maximum_fusion.a), channel_id=1, source_target_pairs={{0,192},{64,0},{128,64},{192,128},{1,193},{65,1},{129,65},{193,129... | collective-permute-start | bytes 1179656 | tf_op jit(solution)/shard_map/ppermute | solution.py:190
  241.3 3.3 %collective-permute-done.10.c = bf16[4,4,16,768]{3,2,1,0:T(8,128)(2,1)S(1)} collective-permute-done((bf16[4,4,16,768]{3,2,1,0:T(8,128)(2,1)S(1)}, bf16[4,4,16,768]{3,2,1,0:T(8,128)(2,1)S(1)}, u32[]{:S(2)}, u32[]{:S(2)}) %collective-permute-start.10) | collective-permute-done | bytes 393248 | tf_op jit(solution)/shard_map/ppermute | solution.py:190
  244.6 4.7 %collective-permute-done.11.d = bf16[4,4,16,768]{3,2,1,0:T(8,128)(2,1)S(1)} collective-permute-done((bf16[4,4,16,768]{3,2,1,0:T(8,128)(2,1)S(1)}, bf16[4,4,16,768]{3,2,1,0:T(8,128)(2,1)S(1)}, u32[]{:S(2)}, u32[]{:S(2)}) %collective-permute-start.11) | collective-permute-done | bytes 393248 | tf_op jit(solution)/shard_map/ppermute | solution.py:190
  (78 shorter events, 36.4 us)
Async XLA Ops:
  7.2 122.1 %all-gather.2.cloned.1.call-start = ((), (), s32[]{:S(2)}) async-start(), calls=%async_computation.6 | async-start | bytes 5242880 | tf_op jit(solution)/shard_map/all_gather | solution.py:240
  10.8 2.0 collective-permute-start
  14.2 24.5 %copy-start.4 = (bf16[128,2048]{1,0:T(8,128)(2,1)S(1)}, bf16[128,2048]{1,0:T(8,128)(2,1)}, u32[]{:S(2)}) copy-start(bf16[128,2048]{1,0:T(8,128)(2,1)} %param.8) | copy-start | bytes 1572868
  14.2 18.7 %collective-permute-start.1 = (bf16[128,1024]{1,0:T(8,128)(2,1)S(1)}, bf16[128,1024]{1,0:T(8,128)(2,1)S(1)}, u32[]{:S(2)}, u32[]{:S(2)}) collective-permute-start(bf16[128,1024]{1,0:T(8,128)(2,1)S(1)} %pad_maximum_fusion.1), channel_id=1, source_target_pairs={{0,8},{8,0},{1,9},{9,1},{2,10},{10,2},{3,11},{11,3},{4,12},{12,4},... | collective-permute-start | bytes 786440 | tf_op jit(solution)/shard_map/ppermute | solution.py:190
  33.1 6.1 %copy-start.5 = (bf16[128,2048]{1,0:T(8,128)(2,1)S(1)}, bf16[128,2048]{1,0:T(8,128)(2,1)}, u32[]{:S(2)}) copy-start(bf16[128,2048]{1,0:T(8,128)(2,1)} %param.11) | copy-start | bytes 1572868
  33.9 18.9 %all-to-all-start.1 = ((bf16[8,128,256]{2,1,0:T(8,128)(2,1)}), bf16[8,128,256]{2,1,0:T(8,128)(2,1)S(1)}, u32[]{:S(2)}, u32[]{:S(2)}) async-start(bf16[8,128,256]{2,1,0:T(8,128)(2,1)} %maximum_bitcast_fusion.1), calls=%async_computation.1 | async-start | bytes 1048576 | tf_op jit(solution)/shard_map/all_to_all | solution.py:234
  52.8 36.0 %copy-start.1 = (bf16[8,128,256]{2,1,0:T(8,128)(2,1)}, bf16[8,128,256]{2,1,0:T(8,128)(2,1)S(1)}, u32[]{:S(2)}) copy-start(bf16[8,128,256]{2,1,0:T(8,128)(2,1)S(1)} %all-to-all-done.1.other) | copy-start | bytes 1572868
  52.8 36.0 %all-to-all-start = ((bf16[8,128,768]{2,1,0:T(8,128)(2,1)}), bf16[8,128,768]{2,1,0:T(8,128)(2,1)S(1)}, u32[]{:S(2)}, u32[]{:S(2)}) async-start(bf16[8,128,768]{2,1,0:T(8,128)(2,1)} %maximum_bitcast_fusion), calls=%async_computation | async-start | bytes 3145728 | tf_op jit(solution)/shard_map/all_to_all | solution.py:231
  105.9 2.0 collective-permute-start.3
  109.1 17.5 %collective-permute-start.4 = (bf16[1024,128]{1,0:T(8,128)(2,1)S(1)}, bf16[1024,128]{1,0:T(8,128)(2,1)S(1)}, u32[]{:S(2)}, u32[]{:S(2)}) collective-permute-start(bf16[1024,128]{1,0:T(8,128)(2,1)S(1)} %slice.49), channel_id=1, source_target_pairs={{0,8},{8,0},{1,9},{9,1},{2,10},{10,2},{3,11},{11,3},{4,12},{12,4},... | collective-permute-start | bytes 786440 | tf_op jit(solution)/shard_map/ppermute | solution.py:190
  126.6 1.6 collective-permute-start.5
  136.5 7.0 %copy-start.3 = (bf16[1024,256]{1,0:T(8,128)(2,1)S(1)}, bf16[1024,256]{1,0:T(8,128)(2,1)}, u32[]{:S(2)}) copy-start(bf16[1024,256]{1,0:T(8,128)(2,1)} %get-tuple-element.5) | copy-start | bytes 1572868
  136.5 22.2 %all-to-all-start.4 = ((bf16[16,128,256]{2,1,0:T(8,128)(2,1)}), bf16[16,128,256]{2,1,0:T(8,128)(2,1)S(1)}, u32[]{:S(2)}, u32[]{:S(2)}) async-start(bf16[16,128,256]{2,1,0:T(8,128)(2,1)} %bitcast.63), calls=%async_computation.4 | async-start | bytes 2097152 | tf_op jit(solution)/shard_map/all_to_all | solution.py:208
  143.6 2.2 collective-permute-start.2
  158.7 32.0 %all-to-all-start.2 = ((bf16[16,128,512]{2,1,0:T(8,128)(2,1)}), bf16[16,128,512]{2,1,0:T(8,128)(2,1)S(1)}, u32[]{:S(2)}, u32[]{:S(2)}) async-start(bf16[16,128,512]{2,1,0:T(8,128)(2,1)} %bitcast.60), calls=%async_computation.2 | async-start | bytes 4194304 | tf_op jit(solution)/shard_map/all_to_all | solution.py:208
  190.7 16.7 %all-to-all-start.5 = ((bf16[8,64,256]{2,1,0:T(8,128)(2,1)}), bf16[8,64,256]{2,1,0:T(8,128)(2,1)S(1)}, u32[]{:S(2)}, u32[]{:S(2)}) async-start(bf16[8,64,256]{2,1,0:T(8,128)(2,1)} %bitcast.22), calls=%async_computation.5 | async-start | bytes 524288 | tf_op jit(solution)/shard_map/all_to_all | solution.py:212
  207.5 16.4 %all-to-all-start.3 = ((bf16[8,64,512]{2,1,0:T(8,128)(2,1)}), bf16[8,64,512]{2,1,0:T(8,128)(2,1)S(1)}, u32[]{:S(2)}, u32[]{:S(2)}) async-start(bf16[8,64,512]{2,1,0:T(8,128)(2,1)} %bitcast.15), calls=%async_computation.3 | async-start | bytes 1048576 | tf_op jit(solution)/shard_map/all_to_all | solution.py:212
  224.0 6.2 %collective-permute-start.6 = (bf16[4,16,768]{2,1,0:T(8,128)(2,1)S(1)}, bf16[4,16,768]{2,1,0:T(8,128)(2,1)S(1)}, u32[]{:S(2)}, u32[]{:S(2)}) collective-permute-start(bf16[4,16,768]{2,1,0:T(8,128)(2,1)S(1)} %get-tuple-element.14), channel_id=1, source_target_pairs={{0,16},{16,32},{32,48},{48,0},{1,17},{17,33},{33,49},{49,1},{2,18}... | collective-permute-start | bytes 294920 | tf_op jit(solution)/shard_map/ppermute | solution.py:190
  226.5 7.3 %collective-permute-start.7 = (bf16[4,16,768]{2,1,0:T(8,128)(2,1)S(1)}, bf16[4,16,768]{2,1,0:T(8,128)(2,1)S(1)}, u32[]{:S(2)}, u32[]{:S(2)}) collective-permute-start(bf16[4,16,768]{2,1,0:T(8,128)(2,1)S(1)} %get-tuple-element.14), channel_id=1, source_target_pairs={{0,32},{16,48},{32,0},{48,16},{1,33},{17,49},{33,1},{49,17},{2,34}... | collective-permute-start | bytes 294920 | tf_op jit(solution)/shard_map/ppermute | solution.py:190
  230.0 5.0 %collective-permute-start.8 = (bf16[4,16,768]{2,1,0:T(8,128)(2,1)S(1)}, bf16[4,16,768]{2,1,0:T(8,128)(2,1)S(1)}, u32[]{:S(2)}, u32[]{:S(2)}) collective-permute-start(bf16[4,16,768]{2,1,0:T(8,128)(2,1)S(1)} %get-tuple-element.14), channel_id=1, source_target_pairs={{0,48},{16,0},{32,16},{48,32},{1,49},{17,1},{33,17},{49,33},{2,50}... | collective-permute-start | bytes 294920 | tf_op jit(solution)/shard_map/ppermute | solution.py:190
  235.0 15.1 %copy-start.2 = (bf16[4,4,16,768]{3,2,1,0:T(8,128)(2,1)}, bf16[4,4,16,768]{3,2,1,0:T(8,128)(2,1)S(1)}, u32[]{:S(2)}) copy-start(bf16[4,4,16,768]{3,2,1,0:T(8,128)(2,1)S(1)} %pad_maximum_fusion.a) | copy-start | bytes 1179652
  235.0 9.6 %collective-permute-start.10 = (bf16[4,4,16,768]{3,2,1,0:T(8,128)(2,1)S(1)}, bf16[4,4,16,768]{3,2,1,0:T(8,128)(2,1)S(1)}, u32[]{:S(2)}, u32[]{:S(2)}) collective-permute-start(bf16[4,4,16,768]{3,2,1,0:T(8,128)(2,1)S(1)} %pad_maximum_fusion.a), channel_id=1, source_target_pairs={{0,128},{64,192},{128,0},{192,64},{1,129},{65,193},{129,1},{193,65... | collective-permute-start | bytes 1179656 | tf_op jit(solution)/shard_map/ppermute | solution.py:190
  237.4 11.9 %collective-permute-start.11 = (bf16[4,4,16,768]{3,2,1,0:T(8,128)(2,1)S(1)}, bf16[4,4,16,768]{3,2,1,0:T(8,128)(2,1)S(1)}, u32[]{:S(2)}, u32[]{:S(2)}) collective-permute-start(bf16[4,4,16,768]{3,2,1,0:T(8,128)(2,1)S(1)} %pad_maximum_fusion.a), channel_id=1, source_target_pairs={{0,192},{64,0},{128,64},{192,128},{1,193},{65,1},{129,65},{193,129... | collective-permute-start | bytes 1179656 | tf_op jit(solution)/shard_map/ppermute | solution.py:190
  240.7 9.4 %collective-permute-start.9 = (bf16[4,4,16,768]{3,2,1,0:T(8,128)(2,1)S(1)}, bf16[4,4,16,768]{3,2,1,0:T(8,128)(2,1)S(1)}, u32[]{:S(2)}, u32[]{:S(2)}) collective-permute-start(bf16[4,4,16,768]{3,2,1,0:T(8,128)(2,1)S(1)} %pad_maximum_fusion.a), channel_id=1, source_target_pairs={{0,64},{64,128},{128,192},{192,0},{1,65},{65,129},{129,193},{193,1... | collective-permute-start | bytes 1179656 | tf_op jit(solution)/shard_map/ppermute | solution.py:190
  (6 other events, 14.6 us)
Sparse Core Ops, SparseCore 0:
  14.3 68.7 all-gather.1

commit v2 on v1

v2 whole, which is shorter than its diff:
```python
import functools
import math

import jax
import jax.numpy as jnp
from jax import lax
from jax.experimental import pallas as pl
from jax.experimental.pallas import tpu as pltpu
from jax.sharding import Mesh, PartitionSpec as P

HEAD = 128
KV_HEADS = 4
HALF = 64
SPANS = 32
SEQ = 2048
NX, NZL, NZH, NY, NC = 4, 4, 2, 4, 2
ROWS = 128
OWN = ROWS * NY * NC
FEATS = 256
SCALE = 1.0 / math.sqrt(HEAD)
LOG2E = math.log2(math.e)
TILE = 256
VMEM = 60 * 1024 * 1024
AXES = ("x", "zl", "zh", "y", "c")


def nt(a, b):
    return lax.dot_general(a, b, (((1,), (1,)), ((), ())), preferred_element_type=jnp.float32)


def tn(a, b):
    return lax.dot_general(a, b, (((0,), (0,)), ((), ())), preferred_element_type=jnp.float32)


def nn(a, b):
    return lax.dot_general(a, b, (((1,), (0,)), ((), ())), preferred_element_type=jnp.float32)


def cost(us):
    return pl.CostEstimate(flops=us * 1_000_000_000, bytes_accessed=us * 2_000_000, transcendentals=0)


def attention_kernel(ids, span, lens, own, kv, kv_got, dq_ref, keep_ref, give_ref, ks, vs, dk, dv):
    zh, core = ids[0], ids[1]
    blocks = OWN // HALF
    side = zh + core - 2 * zh * core
    for part, first in ((kv, side * blocks), (kv_got, (1 - side) * blocks)):
        for j in range(blocks):
            rows = slice((j % 2) * HALF, (j % 2) * HALF + HALF)
            at = pl.ds(pl.multiple_of(span[first + j] * HALF, HALF), HALF)
            ks[at, :] = part[j // 2, rows, :HEAD]
            vs[at, :] = part[j // 2, rows, HEAD:]
    dk[...] = jnp.zeros_like(dk)
    dv[...] = jnp.zeros_like(dv)
    ends = []
    total = jnp.int32(0)
    for d in range(lens.shape[1]):
        total = total + lens[0, d]
        ends.append(total)
    lane = lax.broadcasted_iota(jnp.int32, (1, 2 * HALF), 1) % HALF

    def block(j, carry):
        first = span[zh * blocks + j] * HALF
        low = jnp.int32(0)
        for e in ends:
            low = jnp.where(e <= first, e, low)
        high = pl.cdiv(first + HALF, 2 * HALF) * (2 * HALF)
        tiles = pl.cdiv(high - low, TILE)
        half, part = j // 2, pl.multiple_of((j % 2) * HALF, HALF)
        q = jnp.concatenate(
            [own[half, pl.ds(part, HALF), :HEAD], own[half, pl.ds(part, HALF), HEAD : 2 * HEAD]], axis=0
        )
        do = jnp.concatenate(
            [own[half, pl.ds(part, HALF), 2 * HEAD : 3 * HEAD], own[half, pl.ds(part, HALF), 3 * HEAD : 4 * HEAD]],
            axis=0,
        )
        pos = first + lane
        doc = jnp.zeros_like(pos)
        for e in ends:
            doc = jnp.where(e <= pos, e, doc)

        def work(n):
            keys = n * TILE
            start = pl.multiple_of(jnp.maximum(high - keys, 0), 2 * HALF)
            at = pl.ds(start, keys)
            k, v = ks[at, :], vs[at, :]
            row = lax.broadcasted_iota(jnp.int32, (keys, 2 * HALF), 0)
            seen = (row >= doc - start) & (row <= pos - start)
            s = jnp.where(seen, nt(k, q), -1e30)
            top = jnp.max(s, axis=0, keepdims=True)
            p = jnp.exp2((s - top) * (SCALE * LOG2E))
            p = p * (1.0 / jnp.sum(p, axis=0, keepdims=True))
            dp = nt(v, do)
            delta = jnp.sum(p * dp, axis=0, keepdims=True)
            ds = (p * (dp - delta)).astype(jnp.bfloat16)
            dv[at, :] += nn(p.astype(jnp.bfloat16), do)
            dk[at, :] += nn(ds, q)
            g = (tn(ds, k) * SCALE).astype(jnp.bfloat16)
            out = pl.ds(pl.multiple_of(j * HALF, HALF), HALF)
            dq_ref[out, :HEAD] = g[:HALF]
            dq_ref[out, HEAD:] = g[HALF:]

        for n in range(1, 6):
            pl.when(tiles == n)(functools.partial(work, n))
        return carry

    lax.fori_loop(0, blocks, block, 0)
    for which, a_ref, b_ref in ((0, keep_ref, give_ref), (1, give_ref, keep_ref)):

        @pl.when(core == which)
        def _(a_ref=a_ref, b_ref=b_ref):
            for j in range(blocks):
                for side, base in ((zh, 0), (1 - zh, OWN)):
                    at = pl.ds(pl.multiple_of(span[side * blocks + j] * HALF, HALF), HALF)
                    to = slice(base + j * HALF, base + (j + 1) * HALF)
                    a_ref[to, :] = (dk[at, :] * SCALE).astype(jnp.bfloat16)
                    b_ref[to, :] = dv[at, :].astype(jnp.bfloat16)


def attention(ids, span, lens, own, kv, kv_got):
    smem = pl.BlockSpec(memory_space=pltpu.SMEM)
    vmem = pl.BlockSpec(memory_space=pltpu.VMEM)
    return pl.pallas_call(
        attention_kernel,
        out_shape=(
            jax.ShapeDtypeStruct((OWN, 2 * HEAD), jnp.bfloat16),
            jax.ShapeDtypeStruct((SEQ, HEAD), jnp.bfloat16),
            jax.ShapeDtypeStruct((SEQ, HEAD), jnp.bfloat16),
        ),
        in_specs=[smem, smem, smem, vmem, vmem, vmem],
        out_specs=(vmem, vmem, vmem),
        cost_estimate=cost(14),
        scratch_shapes=[
            pltpu.VMEM((SEQ, HEAD), jnp.bfloat16),
            pltpu.VMEM((SEQ, HEAD), jnp.bfloat16),
            pltpu.VMEM((SEQ, HEAD), jnp.float32),
            pltpu.VMEM((SEQ, HEAD), jnp.float32),
        ],
        compiler_params=pltpu.CompilerParams(vmem_limit_bytes=VMEM),
        name="attention_backward",
    )(ids, span, lens, own, kv, kv_got)


def turn_kernel(ids, x_ref, keep, give, turned):
    core, x = ids[1], ids[2]
    rows = FEATS // NX
    for out, which in ((keep, core), (give, 1 - core)):
        for i in range(NZH * NY):
            turned[i % 2] = x_ref[:, pl.ds(pl.multiple_of((2 * i + which) * FEATS, FEATS), FEATS)].T
            for s in range(NX):
                at = pl.ds(pl.multiple_of(lax.rem(x + s, NX) * rows, rows), rows)
                out[s, i * rows : (i + 1) * rows, :] = turned[i % 2, at, :]


def turn(ids, x):
    smem = pl.BlockSpec(memory_space=pltpu.SMEM)
    vmem = pl.BlockSpec(memory_space=pltpu.VMEM)
    shape = jax.ShapeDtypeStruct((NX, NZH * NY * FEATS // NX, ROWS), jnp.bfloat16)
    return pl.pallas_call(
        turn_kernel,
        out_shape=(shape, shape),
        in_specs=[smem, vmem],
        out_specs=(vmem, vmem),
        scratch_shapes=[pltpu.VMEM((2, FEATS, ROWS), jnp.bfloat16)],
        compiler_params=pltpu.CompilerParams(vmem_limit_bytes=VMEM),
        name="turn",
    )(ids, x)


def weight_kernel(joined, ids, *refs):
    pieces, mine, got, out, g = refs[:8], refs[8 : 8 + NX], refs[8 + NX : 8 + 2 * NX], refs[-2], refs[-1]
    core, y = ids[1], ids[3]
    width = mine[0].shape[1]
    for i, s in enumerate((0, -1, 1, 2)):
        base = lax.rem(y + s + NY, NY) * (NC * ROWS)
        for t in range(NX):
            for half, which in enumerate((core, 1 - core)):
                at = pl.ds(pl.multiple_of(base + which * ROWS, ROWS), ROWS)
                to = slice((2 * t + half) * ROWS, (2 * t + half + 1) * ROWS)
                g[i, to, :width] = mine[t][at, :]
                g[i, to, width:] = got[t][at, :]
    sub = FEATS // (NX * NZL)
    first = 0
    if joined:
        before = refs[8 + 2 * NX]
        first = before.shape[-1]
        out[:, :, :, :, :first] = before[...]
    for zh in range(NZH):
        total = jnp.zeros((FEATS, 2 * width), jnp.float32)
        for i in range(NY):
            total += nn(pieces[4 * zh + i][...], g[i])
        total = total.astype(jnp.bfloat16)
        for y_to in range(NY):
            for zl in range(NZL):
                row = (y_to * NZL + zl) * sub
                out[zh, zl, y_to, :, first : first + 2 * width] = total[row : row + sub]


def weight_term(ids, xs, mine, got, before=None):
    width = mine[0].shape[1]
    cols = 2 * width + (before.shape[-1] if before is not None else 0)
    vmem = pl.BlockSpec(memory_space=pltpu.VMEM)
    more = [] if before is None else [before]
    return pl.pallas_call(
        functools.partial(weight_kernel, before is not None),
        out_shape=jax.ShapeDtypeStruct((NZH, NZL, NY, FEATS // (NX * NZL), cols), jnp.bfloat16),
        in_specs=[pl.BlockSpec(memory_space=pltpu.SMEM)] + [vmem] * (len(xs) + 2 * NX + len(more)),
        out_specs=vmem,
        scratch_shapes=[pltpu.VMEM((NY, OWN, 2 * width), jnp.bfloat16)],
        compiler_params=pltpu.CompilerParams(vmem_limit_bytes=VMEM),
        cost_estimate=cost(5),
        name="weight_term",
    )(ids, *xs, *mine, *got, *more)


def finish_kernel(ids, *refs):
    pieces, (q_ref, k_ref, v_ref) = refs[:NX], refs[NX:]
    core, x, zl = ids[1], ids[2], ids[4]
    sub = FEATS // (NX * NZL)
    for sx in range(NX):
        for sz in range(NZL):
            row = lax.rem(x - sx + NX, NX) * (FEATS // NX) + lax.rem(zl - sz + NZL, NZL) * sub
            at = pl.ds(pl.multiple_of(row, sub), sub)
            for y in range(NY):
                got = pieces[sx].at[sz, y]
                for i, which in enumerate((core, 1 - core)):
                    src = pl.ds(pl.multiple_of(which * 2 * HEAD, 2 * HEAD), 2 * HEAD)
                    to = slice((2 * y + i) * 2 * HEAD, (2 * y + i + 1) * 2 * HEAD)
                    q_ref[at, to] = got[:, src].astype(jnp.float32)
                    src = pl.ds(pl.multiple_of((4 + which) * HEAD, HEAD), HEAD)
                    (k_ref, v_ref)[i][at, y * HEAD : (y + 1) * HEAD] = got[:, src].astype(jnp.float32)


def finish(ids, pieces):
    smem = pl.BlockSpec(memory_space=pltpu.SMEM)
    vmem = pl.BlockSpec(memory_space=pltpu.VMEM)
    cols = KV_HEADS * HEAD
    return pl.pallas_call(
        finish_kernel,
        out_shape=(
            jax.ShapeDtypeStruct((FEATS, NY * cols), jnp.float32),
            jax.ShapeDtypeStruct((FEATS, cols), jnp.float32),
            jax.ShapeDtypeStruct((FEATS, cols), jnp.float32),
        ),
        in_specs=[smem] + [vmem] * len(pieces),
        out_specs=(vmem, vmem, vmem),
        compiler_params=pltpu.CompilerParams(vmem_limit_bytes=VMEM),
        name="finish",
    )(ids, *pieces)


def shift(value, axis, n, s):
    return lax.ppermute(value, axis, [(i, (i + s) % n) for i in range(n)])


def by_head(value, copies):
    return jnp.broadcast_to(value.reshape(ROWS, KV_HEADS, 1, HEAD), (ROWS, KV_HEADS, copies, HEAD)).reshape(
        ROWS, KV_HEADS * copies, HEAD
    )


def gather_x(value):
    return [value] + [shift(value, "x", NX, s) for s in range(1, NX)]


def other_core(values):
    rest = shift(jnp.concatenate(values[1:], axis=0), "c", NC, 1)
    n = values[0].shape[0]
    return [shift(values[0], "c", NC, 1)] + [rest[i * n : (i + 1) * n] for i in range(len(values) - 1)]


def shards(x, q, k, v, do, lens, span):
    ids = jnp.stack([lax.axis_index(a) for a in ("zh", "c", "x", "y", "zl")]).astype(jnp.int32)
    groups = NY * NC
    kv_rows = jnp.concatenate([k, v], axis=1)
    send = jnp.concatenate(
        [q.reshape(ROWS, groups, 2 * HEAD), do.reshape(ROWS, groups, 2 * HEAD)], axis=2
    ).transpose(1, 0, 2)
    kv_rows, x, send = lax.optimization_barrier((kv_rows, x, send))
    own = lax.all_to_all(send, ("y", "c"), 0, 0, tiled=True)
    far = shift(kv_rows, "zh", NZH, 1)

    keep, give = turn(ids, x)
    pair = jnp.concatenate([keep, shift(give, "c", NC, 1)], axis=2)
    quarters = [pair[0]] + [shift(pair[t], "x", NX, t) for t in range(1, NX)]
    xa, xb = (
        jnp.concatenate([t[h * FEATS : (h + 1) * FEATS] for t in quarters], axis=1) for h in range(NZH)
    )

    send = jnp.stack([kv_rows, far]).reshape(NC, ROWS, 2, KV_HEADS, HEAD)
    send = send.transpose(3, 0, 1, 2, 4).reshape(groups, ROWS, 2 * HEAD)
    own, send = lax.optimization_barrier((own, send))
    kv = lax.all_to_all(send, ("y", "c"), 0, 0, tiled=True)
    kv_got = shift(kv, "c", NC, 1)

    xa_up, xb_up = shift(xa, "y", NY, 1), shift(xb, "y", NY, 1)
    xa_down, xb_down = shift(xa, "y", NY, -1), shift(xb, "y", NY, -1)
    dq, kept, given = attention(ids, span, lens, own, kv, kv_got)
    dqs = gather_x(dq)
    both = kept.astype(jnp.float32) + shift(given, "c", NC, 1).astype(jnp.float32)
    got = shift(both[OWN:].astype(jnp.bfloat16), "zh", NZH, 1)
    got, xa_up, xb_down, xa_down, xb_up, *dqs = lax.optimization_barrier(
        (got, xa_up, xb_down, xa_down, xb_up, *dqs)
    )
    xa_far, xb_far = shift(xa_up, "y", NY, 1), shift(xb_down, "y", NY, -1)
    x_all = [xa, xa_up, xa_down, xa_far, xb, xb_up, xb_down, xb_far]
    mine = (both[:OWN] + got.astype(jnp.float32)).astype(jnp.bfloat16)
    mines = gather_x(mine)
    part = weight_term(ids, x_all, dqs, other_core(dqs))
    part, *mines = lax.optimization_barrier((part, *mines))
    part = weight_term(ids, x_all, mines, other_core(mines), part)
    sub, cols = part.shape[-2:]
    got = lax.all_to_all(part.reshape(NZH * NZL * NY, sub, cols), ("zh", "zl", "y"), 0, 0, tiled=True)
    got = got.reshape(NZH * NZL, NY, sub, cols)
    piece = jnp.sum(got.astype(jnp.float32), axis=0).astype(jnp.bfloat16)
    line = jnp.stack([piece] + [shift(piece, "zl", NZL, s) for s in range(1, NZL)])
    pieces = [line] + [shift(line, "x", NX, s) for s in range(1, NX)]
    return finish(ids, pieces)


def solution(mesh):
    fine = Mesh(mesh.devices.reshape(NX, NZL, NZH, NY, NC), AXES)
    rows = P(AXES, None)
    out = P(("zh", "y", "c"), None)
    return jax.shard_map(
        shards,
        mesh=fine,
        in_specs=(rows, rows, rows, rows, rows, P(("x", "zl"), None), P()),
        out_specs=(out, out, out),
        check_vma=False,
    )
```

time: 265 us -> 206 us (0.78); the launches traced: 261 us -> 205 us
  waiting for transfers between devices: 134 us -> 70.5 us
  blocking collectives: 0 us -> 32.3 us
  between operations: 14.4 us -> 1.08 us
  starting transfers between devices: 60.5 us -> 52.1 us
  other arithmetic: 9.04 us -> 3.42 us
  local copies, waits for them, and re-layouts: 9.39 us -> 12.7 us
    all_to_all x5 -> x1, waiting for transfers between devices: 58.3 us -> 6.73 us  [shards(): kv = lax.all_to_all(send, ('y', 'c'), 0, 0, tiled=True)]
    all_to_all x0 -> x1, blocking collectives: none -> 32.3 us  [shards(): lax.all_to_all(part.reshape(NZH * NZL * NY, sub, cols), ('zh', 'zl', 'y')...]
    all_to_all x1, waiting for transfers between devices: 29.8 us -> 0.01 us  [shards(): own = lax.all_to_all(send, ('y', 'c'), 0, 0, tiled=True)]
    all_to_all x5 -> x1, starting transfers between devices: 31.7 us -> 4.8 us  [shards(): kv = lax.all_to_all(send, ('y', 'c'), 0, 0, tiled=True)]
    ppermute x12 -> x30, starting transfers between devices: 23.2 us -> 42.5 us  [shift(): return lax.ppermute(value, axis, [(i, (i + s) % n) for i in range(n)])]
    ppermute x12 -> x30, waiting for transfers between devices: 46 us -> 63.7 us  [shift(): return lax.ppermute(value, axis, [(i, (i + s) % n) for i in range(n)])]
    select_n x4 -> x0, other arithmetic: 3.66 us -> none  [the longest x3 3.52 us: in_order(): jnp.where(first, jnp.concatenate([mine, got], axis=axis), jnp.concatenate...]
    unnamed x27 -> x57, local copies, waits for them, and re-layouts: 2.72 us -> 5.59 us
  transfers between devices with their start and end apart: 19 -> 32, of which waited for: 18 -> 15; matrix products, arithmetic and copies ran while one was open for 4% -> 4% of each run, Pallas kernels for 9% -> 11%
where the time goes in v2:
time: 206 us; the launch traced here: 205 us
  waiting for transfers between devices  70.5 us (34%)
  starting transfers between devices  52.1 us (25%)
  Pallas kernels  33.2 us (16%)
  blocking collectives  32.3 us (16%)
  local copies, waits for them, and re-layouts  12.7 us (6%)
  other arithmetic  3.42 us (2%)
    ppermute x30, waiting for transfers between devices, shift(): return lax.ppermute(value, axis, [(i, (i + s) % n) for i in range(n)])  63.7 us
    ppermute x30, starting transfers between devices, shift(): return lax.ppermute(value, axis, [(i, (i + s) % n) for i in range(n)])  42.5 us
    all_to_all x1, blocking collectives, shards(): lax.all_to_all(part.reshape(NZH * NZL * NY, sub, cols), ('zh', 'zl', 'y')...  32.3 us
    pallas_call x1, Pallas kernels, attention(): pl.pallas_call(attention_kernel, out_shape=(jax.ShapeDtypeStruct((OWN, 2...  15.8 us
    pallas_call x2, Pallas kernels, weight_term(): pl.pallas_call(functools.partial(weight_kernel, before is not None), out_...  11.6 us
    all_to_all x1, waiting for transfers between devices, shards(): kv = lax.all_to_all(send, ('y', 'c'), 0, 0, tiled=True)  6.73 us
    unnamed x57, local copies, waits for them, and re-layouts  5.59 us
    all_to_all x1, starting transfers between devices, shards(): kv = lax.all_to_all(send, ('y', 'c'), 0, 0, tiled=True)  4.8 us
  transfers between devices with their start and end apart: 32, of which 15 were waited for; matrix products, arithmetic and copies ran while one was open for 4% of the time, Pallas kernels for 11%

profile of v2, /device:TPU:56, one launch (start us, length us, event | category | flops | bytes accessed | tf_op | source)
XLA Modules:
  0.0 205.3 jit_solution(6393496623467025604)
XLA Ops:
  4.5 2.6 %turn.1 = (bf16[4,512,128]{2,1,0:T(8,128)(2,1)}, bf16[4,512,128]{2,1,0:T(8,128)(2,1)}) custom-call(s32[5]{0:T(128)} %stack.47.ids, bf16[128,4096]{1,0:T(8,128)(2,1)} %x_ref), custom_call_target="tpu_custom_call" | custom-call | tf_op jit(solution)/shard_map/turn/pallas_call | solution.py:159
  7.1 4.8 %all-to-all-start = ((bf16[8,128,512]{2,1,0:T(8,128)(2,1)}), bf16[8,128,512]{2,1,0:T(8,128)(2,1)S(1)}, u32[]{:S(2)}, u32[]{:S(2)}) async-start(bf16[8,128,512]{2,1,0:T(8,128)(2,1)} %maximum_bitcast_fusion), calls=%async_computation | async-start | bytes 2097152 | tf_op jit(solution)/shard_map/all_to_all | solution.py:280
  11.9 6.3 %collective-permute-start.4 = (bf16[128,1024]{1,0:T(8,128)(2,1)S(1)}, bf16[128,1024]{1,0:T(8,128)(2,1)}, u32[]{:S(2)}, u32[]{:S(2)}) collective-permute-start(bf16[128,1024]{1,0:T(8,128)(2,1)S(1)} %pad_maximum_fusion.5), channel_id=1, source_target_pairs={{0,8},{8,0},{1,9},{9,1},{2,10},{10,2},{3,11},{11,3},{4,12},{12,4},... | collective-permute-start | bytes 786440 | tf_op jit(solution)/shard_map/ppermute | solution.py:253
  19.7 10.9 %collective-permute-done.4 = bf16[128,1024]{1,0:T(8,128)(2,1)} collective-permute-done((bf16[128,1024]{1,0:T(8,128)(2,1)S(1)}, bf16[128,1024]{1,0:T(8,128)(2,1)}, u32[]{:S(2)}, u32[]{:S(2)}) %collective-permute-start.4) | collective-permute-done | bytes 262176 | tf_op jit(solution)/shard_map/ppermute | solution.py:253
  36.3 2.7 %collective-permute-start.2 = (bf16[512,256]{1,0:T(8,128)(2,1)}, bf16[512,256]{1,0:T(8,128)(2,1)S(1)}, u32[]{:S(2)}, u32[]{:S(2)}) collective-permute-start(bf16[512,256]{1,0:T(8,128)(2,1)} %get-tuple-element.58), channel_id=1, source_target_pairs={{0,128},{64,192},{128,0},{192,64},{1,129},{65,193},{129,1},{193,65... | collective-permute-start | bytes 786440 | tf_op jit(solution)/shard_map/ppermute | solution.py:253
  39.0 4.8 %all-to-all-start.1 = ((bf16[8,128,256]{2,1,0:T(8,128)(2,1)}), bf16[8,128,256]{2,1,0:T(8,128)(2,1)S(1)}, u32[]{:S(2)}, u32[]{:S(2)}) async-start(bf16[8,128,256]{2,1,0:T(8,128)(2,1)} %reshape.30), calls=%async_computation.1 | async-start | bytes 1048576 | tf_op jit(solution)/shard_map/all_to_all | solution.py:293
  45.4 6.7 %all-to-all-done.1.kv = bf16[8,128,256]{2,1,0:T(8,128)(2,1)S(1)} async-done(((bf16[8,128,256]{2,1,0:T(8,128)(2,1)}), bf16[8,128,256]{2,1,0:T(8,128)(2,1)S(1)}, u32[]{:S(2)}, u32[]{:S(2)}) %all-to-all-start.1) | async-done | bytes 524320 | tf_op jit(solution)/shard_map/all_to_all | solution.py:293
  54.7 15.8 %attention_backward.1 = (bf16[1024,256]{1,0:T(8,128)(2,1)}, bf16[2048,128]{1,0:T(8,128)(2,1)}, bf16[2048,128]{1,0:T(8,128)(2,1)}) custom-call(s32[5]{0:T(128)} %stack.47.ids, s32[32]{0:T(128)} %span.1, s32[1,8]{1,0:T(1,128)} %lens.1, bf16[8,128,512]{2,1,0:T(8,128)(2,1)} %copy-done.1, bf16[8,128,256]{2,1,0:T(8,128)(2,1)} %copy-done.5, ...), custom_call_target="tpu_custom_call" | custom-call | flops 14000000000 | bytes 28000000 | tf_op jit(solution)/shard_map/attention_backward/pallas_call | solution.py:123
  74.0 3.2 %collective-permute-start.13 = (bf16[1024,256]{1,0:T(8,128)(2,1)}, bf16[1024,256]{1,0:T(8,128)(2,1)S(1)}, u32[]{:S(2)}, u32[]{:S(2)}) collective-permute-start(bf16[1024,256]{1,0:T(8,128)(2,1)} %get-tuple-element.41.refs_8_), channel_id=1, source_target_pairs={{0,128},{64,192},{128,0},{192,64},{1,129},{65,193},{129,1},{193,65... | collective-permute-start | bytes 1572872 | tf_op jit(solution)/shard_map/ppermute | solution.py:253
  78.7 7.6 %collective-permute-done.10.refs_2_ = bf16[256,1024]{1,0:T(8,128)(2,1)S(1)} collective-permute-done((bf16[256,1024]{1,0:T(8,128)(2,1)S(1)}, bf16[256,1024]{1,0:T(8,128)(2,1)S(1)}, u32[]{:S(2)}, u32[]{:S(2)}) %collective-permute-start.10) | collective-permute-done | bytes 524320 | tf_op jit(solution)/shard_map/ppermute | solution.py:253
  86.2 4.3 %collective-permute-start.7 = (bf16[1024,128]{1,0:T(8,128)(2,1)S(1)}, bf16[1024,128]{1,0:T(8,128)(2,1)S(1)}, u32[]{:S(2)}, u32[]{:S(2)}) collective-permute-start(bf16[1024,128]{1,0:T(8,128)(2,1)S(1)} %slice.116), channel_id=1, source_target_pairs={{0,8},{8,0},{1,9},{9,1},{2,10},{10,2},{3,11},{11,3},{4,12},{12,4},... | collective-permute-start | bytes 786440 | tf_op jit(solution)/shard_map/ppermute | solution.py:253
  90.6 9.9 %collective-permute-done.13.refs_10_ = bf16[1024,256]{1,0:T(8,128)(2,1)S(1)} collective-permute-done((bf16[1024,256]{1,0:T(8,128)(2,1)}, bf16[1024,256]{1,0:T(8,128)(2,1)S(1)}, u32[]{:S(2)}, u32[]{:S(2)}) %collective-permute-start.13) | collective-permute-done | bytes 524320 | tf_op jit(solution)/shard_map/ppermute | solution.py:253
  105.3 3.2 %collective-permute-start.20 = (bf16[1024,128]{1,0:T(8,128)(2,1)S(1)}, bf16[1024,128]{1,0:T(8,128)(2,1)S(1)}, u32[]{:S(2)}, u32[]{:S(2)}) collective-permute-start(bf16[1024,128]{1,0:T(8,128)(2,1)S(1)} %fusion.refs_8_), channel_id=1, source_target_pairs={{0,128},{64,192},{128,0},{192,64},{1,129},{65,193},{129,1},{193,65... | collective-permute-start | bytes 786440 | tf_op jit(solution)/shard_map/ppermute | solution.py:253
  109.7 6.6 %collective-permute-done.15.refs_3_ = bf16[256,1024]{1,0:T(8,128)(2,1)S(1)} collective-permute-done((bf16[256,1024]{1,0:T(8,128)(2,1)S(1)}, bf16[256,1024]{1,0:T(8,128)(2,1)S(1)}, u32[]{:S(2)}, u32[]{:S(2)}) %collective-permute-start.15) | collective-permute-done | bytes 524320 | tf_op jit(solution)/shard_map/ppermute | solution.py:253
  116.3 2.6 %collective-permute-start.21 = (bf16[1024,128]{1,0:T(8,128)(2,1)S(1)}, bf16[1024,128]{1,0:T(8,128)(2,1)S(1)}, u32[]{:S(2)}, u32[]{:S(2)}) collective-permute-start(bf16[1024,128]{1,0:T(8,128)(2,1)S(1)} %fusion.refs_8_), channel_id=1, source_target_pairs={{0,192},{64,0},{128,64},{192,128},{1,193},{65,1},{129,65},{193,129... | collective-permute-start | bytes 786440 | tf_op jit(solution)/shard_map/ppermute | solution.py:253
  119.9 6.5 %weight_term.2.refs_16_ = bf16[2,4,4,16,512]{4,3,2,1,0:T(8,128)(2,1)} custom-call(s32[5]{0:T(128)} %stack.47.ids, bf16[256,1024]{1,0:T(8,128)(2,1)} %copy-done.4, bf16[256,1024]{1,0:T(8,128)(2,1)} %copy-done.21, bf16[256,1024]{1,0:T(8,128)(2,1)} %copy-done.20, bf16[256,1024]{1,0:T(8,128)(2,1)} %copy-done.23, bf16[256,1024]{1,0:T(8,128)(2,1)} %copy-done.3, ...), custom_call_target="tpu_custom_call" | custom-call | flops 5000000000 | bytes 10000000 | tf_op jit(solution)/shard_map/weight_term/pallas_call | solution.py:204
  130.6 5.1 %weight_term.3 = bf16[2,4,4,16,768]{4,3,2,1,0:T(8,128)(2,1)} custom-call(s32[5]{0:T(128)} %stack.47.ids, bf16[256,1024]{1,0:T(8,128)(2,1)} %copy-done.4, bf16[256,1024]{1,0:T(8,128)(2,1)} %copy-done.21, bf16[256,1024]{1,0:T(8,128)(2,1)} %copy-done.20, bf16[256,1024]{1,0:T(8,128)(2,1)} %copy-done.23, bf16[256,1024]{1,0:T(8,128)(2,1)} %copy-done.3, ...), custom_call_target="tpu_custom_call" | custom-call | flops 5000000000 | bytes 10000000 | tf_op jit(solution)/shard_map/weight_term/pallas_call | solution.py:204
  135.7 32.3 %all_to_all.15 = bf16[32,16,768]{2,1,0:T(8,128)(2,1)S(1)} all-to-all(bf16[32,16,768]{2,1,0:T(8,128)(2,1)} %bitcast.30), channel_id=1, replica_groups=mesh['x'=4,'zl'=4,'zh'=2,'y'=4,'c'=2] {'zh','zl','y'}, dimensions={0} | all-to-all | bytes 1572864 | tf_op jit(solution)/shard_map/all_to_all | solution.py:313
  168.3 3.7 %collective-permute-start.25 = (bf16[4,16,768]{2,1,0:T(8,128)(2,1)S(1)}, bf16[4,16,768]{2,1,0:T(8,128)(2,1)S(1)}, u32[]{:S(2)}, u32[]{:S(2)}) collective-permute-start(bf16[4,16,768]{2,1,0:T(8,128)(2,1)S(1)} %reduce_sum.12), channel_id=1, source_target_pairs={{0,32},{16,48},{32,0},{48,16},{1,33},{17,49},{33,1},{49,17},{2,34}... | collective-permute-start | bytes 294920 | tf_op jit(solution)/shard_map/ppermute | solution.py:253
  173.9 2.8 %collective-permute-done.25 = bf16[4,16,768]{2,1,0:T(8,128)(2,1)S(1)} collective-permute-done((bf16[4,16,768]{2,1,0:T(8,128)(2,1)S(1)}, bf16[4,16,768]{2,1,0:T(8,128)(2,1)S(1)}, u32[]{:S(2)}, u32[]{:S(2)}) %collective-permute-start.25) | collective-permute-done | bytes 98336 | tf_op jit(solution)/shard_map/ppermute | solution.py:253
  176.7 2.8 %collective-permute-done.26 = bf16[4,16,768]{2,1,0:T(8,128)(2,1)S(1)} collective-permute-done((bf16[4,16,768]{2,1,0:T(8,128)(2,1)S(1)}, bf16[4,16,768]{2,1,0:T(8,128)(2,1)S(1)}, u32[]{:S(2)}, u32[]{:S(2)}) %collective-permute-start.26) | collective-permute-done | bytes 98336 | tf_op jit(solution)/shard_map/ppermute | solution.py:253
  179.8 2.8 %collective-permute-start.28 = (bf16[4,4,16,768]{3,2,1,0:T(8,128)(2,1)S(1)}, bf16[4,4,16,768]{3,2,1,0:T(8,128)(2,1)S(1)}, u32[]{:S(2)}, u32[]{:S(2)}) collective-permute-start(bf16[4,4,16,768]{3,2,1,0:T(8,128)(2,1)S(1)} %pad_maximum_fusion.4.refs_0_), channel_id=1, source_target_pairs={{0,128},{64,192},{128,0},{192,64},{1,129},{65,193},{129,1},{193,65... | collective-permute-start | bytes 1179656 | tf_op jit(solution)/shard_map/ppermute | solution.py:253
  183.9 16.5 %collective-permute-done.27.refs_1_ = bf16[4,4,16,768]{3,2,1,0:T(8,128)(2,1)S(1)} collective-permute-done((bf16[4,4,16,768]{3,2,1,0:T(8,128)(2,1)S(1)}, bf16[4,4,16,768]{3,2,1,0:T(8,128)(2,1)S(1)}, u32[]{:S(2)}, u32[]{:S(2)}) %collective-permute-start.27) | collective-permute-done | bytes 393248 | tf_op jit(solution)/shard_map/ppermute | solution.py:253
  202.0 3.3 %finish.1 = (f32[256,2048]{1,0:T(8,128)}, f32[256,512]{1,0:T(8,128)}, f32[256,512]{1,0:T(8,128)}) custom-call(s32[5]{0:T(128)} %stack.47.ids, bf16[4,4,16,768]{3,2,1,0:T(8,128)(2,1)} %copy-done, bf16[4,4,16,768]{3,2,1,0:T(8,128)(2,1)} %copy-done.9, bf16[4,4,16,768]{3,2,1,0:T(8,128)(2,1)} %copy-done.10, bf16[4,4,16,768]{3,2,1,0:T(8,128)(2,1)} %copy-done.11), custom_call_target="tpu_custom_call" | custom-call | tf_op jit(solution)/shard_map/finish/pallas_call | solution.py:238
  (131 shorter events, 36.4 us)
Async XLA Ops:
  7.1 24.9 %collective-permute-start = (bf16[4,512,128]{2,1,0:T(8,128)(2,1)}, bf16[4,512,128]{2,1,0:T(8,128)(2,1)S(1)}, u32[]{:S(2)}, u32[]{:S(2)}) collective-permute-start(bf16[4,512,128]{2,1,0:T(8,128)(2,1)} %get-tuple-element.29), channel_id=1, source_target_pairs={{0,1},{1,0},{2,3},{3,2},{4,5},{5,4},{6,7},{7,6},{8,9},{9,8},{10,11... | collective-permute-start | bytes 1572872 | tf_op jit(solution)/shard_map/ppermute | solution.py:253
  7.1 32.0 %all-to-all-start = ((bf16[8,128,512]{2,1,0:T(8,128)(2,1)}), bf16[8,128,512]{2,1,0:T(8,128)(2,1)S(1)}, u32[]{:S(2)}, u32[]{:S(2)}) async-start(bf16[8,128,512]{2,1,0:T(8,128)(2,1)} %maximum_bitcast_fusion), calls=%async_computation | async-start | bytes 2097152 | tf_op jit(solution)/shard_map/all_to_all | solution.py:280
  11.9 18.7 %collective-permute-start.4 = (bf16[128,1024]{1,0:T(8,128)(2,1)S(1)}, bf16[128,1024]{1,0:T(8,128)(2,1)}, u32[]{:S(2)}, u32[]{:S(2)}) collective-permute-start(bf16[128,1024]{1,0:T(8,128)(2,1)S(1)} %pad_maximum_fusion.5), channel_id=1, source_target_pairs={{0,8},{8,0},{1,9},{9,1},{2,10},{10,2},{3,11},{11,3},{4,12},{12,4},... | collective-permute-start | bytes 786440 | tf_op jit(solution)/shard_map/ppermute | solution.py:253
  33.0 12.4 %collective-permute-start.1 = (bf16[512,256]{1,0:T(8,128)(2,1)}, bf16[512,256]{1,0:T(8,128)(2,1)S(1)}, u32[]{:S(2)}, u32[]{:S(2)}) collective-permute-start(bf16[512,256]{1,0:T(8,128)(2,1)} %get-tuple-element.56), channel_id=1, source_target_pairs={{0,64},{64,128},{128,192},{192,0},{1,65},{65,129},{129,193},{193,1... | collective-permute-start | bytes 786440 | tf_op jit(solution)/shard_map/ppermute | solution.py:253
  36.3 15.8 %collective-permute-start.2 = (bf16[512,256]{1,0:T(8,128)(2,1)}, bf16[512,256]{1,0:T(8,128)(2,1)S(1)}, u32[]{:S(2)}, u32[]{:S(2)}) collective-permute-start(bf16[512,256]{1,0:T(8,128)(2,1)} %get-tuple-element.58), channel_id=1, source_target_pairs={{0,128},{64,192},{128,0},{192,64},{1,129},{65,193},{129,1},{193,65... | collective-permute-start | bytes 786440 | tf_op jit(solution)/shard_map/ppermute | solution.py:253
  39.0 13.1 %all-to-all-start.1 = ((bf16[8,128,256]{2,1,0:T(8,128)(2,1)}), bf16[8,128,256]{2,1,0:T(8,128)(2,1)S(1)}, u32[]{:S(2)}, u32[]{:S(2)}) async-start(bf16[8,128,256]{2,1,0:T(8,128)(2,1)} %reshape.30), calls=%async_computation.1 | async-start | bytes 1048576 | tf_op jit(solution)/shard_map/all_to_all | solution.py:293
  43.9 8.6 %collective-permute-start.3 = (bf16[512,256]{1,0:T(8,128)(2,1)}, bf16[512,256]{1,0:T(8,128)(2,1)S(1)}, u32[]{:S(2)}, u32[]{:S(2)}) collective-permute-start(bf16[512,256]{1,0:T(8,128)(2,1)} %get-tuple-element.57), channel_id=1, source_target_pairs={{0,192},{64,0},{128,64},{192,128},{1,193},{65,1},{129,65},{193,129... | collective-permute-start | bytes 786440 | tf_op jit(solution)/shard_map/ppermute | solution.py:253
  52.6 21.3 %collective-permute-start.11 = (bf16[256,1024]{1,0:T(8,128)(2,1)S(1)}, bf16[256,1024]{1,0:T(8,128)(2,1)S(1)}, u32[]{:S(2)}, u32[]{:S(2)}) collective-permute-start(bf16[256,1024]{1,0:T(8,128)(2,1)S(1)} %pad_maximum_fusion.3.refs_4_), channel_id=1, source_target_pairs={{0,2},{2,4},{4,6},{6,0},{1,3},{3,5},{5,7},{7,1},{8,10},{10,12},{12... | collective-permute-start | bytes 1572872 | tf_op jit(solution)/shard_map/ppermute | solution.py:253
  54.4 19.5 %collective-permute-start.9 = (bf16[256,1024]{1,0:T(8,128)(2,1)S(1)}, bf16[256,1024]{1,0:T(8,128)(2,1)S(1)}, u32[]{:S(2)}, u32[]{:S(2)}) collective-permute-start(bf16[256,1024]{1,0:T(8,128)(2,1)S(1)} %pad_maximum_fusion.3.refs_4_), channel_id=1, source_target_pairs={{0,6},{2,0},{4,2},{6,4},{1,7},{3,1},{5,3},{7,5},{8,14},{10,8},{12,... | collective-permute-start | bytes 1572872 | tf_op jit(solution)/shard_map/ppermute | solution.py:253
  70.6 15.6 %collective-permute-start.10 = (bf16[256,1024]{1,0:T(8,128)(2,1)S(1)}, bf16[256,1024]{1,0:T(8,128)(2,1)S(1)}, u32[]{:S(2)}, u32[]{:S(2)}) collective-permute-start(bf16[256,1024]{1,0:T(8,128)(2,1)S(1)} %pad_maximum_fusion.2.refs_0_), channel_id=1, source_target_pairs={{0,6},{2,0},{4,2},{6,4},{1,7},{3,1},{5,3},{7,5},{8,14},{10,8},{12,... | collective-permute-start | bytes 1572872 | tf_op jit(solution)/shard_map/ppermute | solution.py:253
  71.6 19.0 %collective-permute-start.8 = (bf16[256,1024]{1,0:T(8,128)(2,1)S(1)}, bf16[256,1024]{1,0:T(8,128)(2,1)S(1)}, u32[]{:S(2)}, u32[]{:S(2)}) collective-permute-start(bf16[256,1024]{1,0:T(8,128)(2,1)S(1)} %pad_maximum_fusion.2.refs_0_), channel_id=1, source_target_pairs={{0,2},{2,4},{4,6},{6,0},{1,3},{3,5},{5,7},{7,1},{8,10},{10,12},{12... | collective-permute-start | bytes 1572872 | tf_op jit(solution)/shard_map/ppermute | solution.py:253
  73.9 16.6 %collective-permute-start.12 = (bf16[1024,256]{1,0:T(8,128)(2,1)}, bf16[1024,256]{1,0:T(8,128)(2,1)S(1)}, u32[]{:S(2)}, u32[]{:S(2)}) collective-permute-start(bf16[1024,256]{1,0:T(8,128)(2,1)} %get-tuple-element.41.refs_8_), channel_id=1, source_target_pairs={{0,64},{64,128},{128,192},{192,0},{1,65},{65,129},{129,193},{193,1... | collective-permute-start | bytes 1572872 | tf_op jit(solution)/shard_map/ppermute | solution.py:253
  74.0 26.5 %collective-permute-start.13 = (bf16[1024,256]{1,0:T(8,128)(2,1)}, bf16[1024,256]{1,0:T(8,128)(2,1)S(1)}, u32[]{:S(2)}, u32[]{:S(2)}) collective-permute-start(bf16[1024,256]{1,0:T(8,128)(2,1)} %get-tuple-element.41.refs_8_), channel_id=1, source_target_pairs={{0,128},{64,192},{128,0},{192,64},{1,129},{65,193},{129,1},{193,65... | collective-permute-start | bytes 1572872 | tf_op jit(solution)/shard_map/ppermute | solution.py:253
  77.2 23.9 %collective-permute-start.14 = (bf16[1024,256]{1,0:T(8,128)(2,1)}, bf16[1024,256]{1,0:T(8,128)(2,1)S(1)}, u32[]{:S(2)}, u32[]{:S(2)}) collective-permute-start(bf16[1024,256]{1,0:T(8,128)(2,1)} %get-tuple-element.41.refs_8_), channel_id=1, source_target_pairs={{0,192},{64,0},{128,64},{192,128},{1,193},{65,1},{129,65},{193,129... | collective-permute-start | bytes 1572872 | tf_op jit(solution)/shard_map/ppermute | solution.py:253
  86.2 15.4 %collective-permute-start.7 = (bf16[1024,128]{1,0:T(8,128)(2,1)S(1)}, bf16[1024,128]{1,0:T(8,128)(2,1)S(1)}, u32[]{:S(2)}, u32[]{:S(2)}) collective-permute-start(bf16[1024,128]{1,0:T(8,128)(2,1)S(1)} %slice.116), channel_id=1, source_target_pairs={{0,8},{8,0},{1,9},{9,1},{2,10},{10,2},{3,11},{11,3},{4,12},{12,4},... | collective-permute-start | bytes 786440 | tf_op jit(solution)/shard_map/ppermute | solution.py:253
  102.0 14.3 %collective-permute-start.15 = (bf16[256,1024]{1,0:T(8,128)(2,1)S(1)}, bf16[256,1024]{1,0:T(8,128)(2,1)S(1)}, u32[]{:S(2)}, u32[]{:S(2)}) collective-permute-start(bf16[256,1024]{1,0:T(8,128)(2,1)S(1)} %collective-permute-done.8.refs_1_), channel_id=1, source_target_pairs={{0,2},{2,4},{4,6},{6,0},{1,3},{3,5},{5,7},{7,1},{8,10},{10,12},{12... | collective-permute-start | bytes 1572872 | tf_op jit(solution)/shard_map/ppermute | solution.py:253
  103.8 15.2 %collective-permute-start.16 = (bf16[256,1024]{1,0:T(8,128)(2,1)S(1)}, bf16[256,1024]{1,0:T(8,128)(2,1)S(1)}, u32[]{:S(2)}, u32[]{:S(2)}) collective-permute-start(bf16[256,1024]{1,0:T(8,128)(2,1)S(1)} %collective-permute-done.9.refs_6_), channel_id=1, source_target_pairs={{0,6},{2,0},{4,2},{6,4},{1,7},{3,1},{5,3},{7,5},{8,14},{10,8},{12,... | collective-permute-start | bytes 1572872 | tf_op jit(solution)/shard_map/ppermute | solution.py:253
  104.1 14.9 %collective-permute-start.17 = (bf16[1024,256]{1,0:T(8,128)(2,1)S(1)}, bf16[1024,256]{1,0:T(8,128)(2,1)S(1)}, u32[]{:S(2)}, u32[]{:S(2)}) collective-permute-start(bf16[1024,256]{1,0:T(8,128)(2,1)S(1)} %copy-done.22), channel_id=1, source_target_pairs={{0,1},{1,0},{2,3},{3,2},{4,5},{5,4},{6,7},{7,6},{8,9},{9,8},{10,11... | collective-permute-start | bytes 1572872 | tf_op jit(solution)/shard_map/ppermute | solution.py:253
  104.1 22.3 %collective-permute-start.19 = (bf16[1024,128]{1,0:T(8,128)(2,1)S(1)}, bf16[1024,128]{1,0:T(8,128)(2,1)S(1)}, u32[]{:S(2)}, u32[]{:S(2)}) collective-permute-start(bf16[1024,128]{1,0:T(8,128)(2,1)S(1)} %fusion.refs_8_), channel_id=1, source_target_pairs={{0,64},{64,128},{128,192},{192,0},{1,65},{65,129},{129,193},{193,1... | collective-permute-start | bytes 786440 | tf_op jit(solution)/shard_map/ppermute | solution.py:253
  105.3 21.1 %collective-permute-start.20 = (bf16[1024,128]{1,0:T(8,128)(2,1)S(1)}, bf16[1024,128]{1,0:T(8,128)(2,1)S(1)}, u32[]{:S(2)}, u32[]{:S(2)}) collective-permute-start(bf16[1024,128]{1,0:T(8,128)(2,1)S(1)} %fusion.refs_8_), channel_id=1, source_target_pairs={{0,128},{64,192},{128,0},{192,64},{1,129},{65,193},{129,1},{193,65... | collective-permute-start | bytes 786440 | tf_op jit(solution)/shard_map/ppermute | solution.py:253
  116.3 10.2 %collective-permute-start.21 = (bf16[1024,128]{1,0:T(8,128)(2,1)S(1)}, bf16[1024,128]{1,0:T(8,128)(2,1)S(1)}, u32[]{:S(2)}, u32[]{:S(2)}) collective-permute-start(bf16[1024,128]{1,0:T(8,128)(2,1)S(1)} %fusion.refs_8_), channel_id=1, source_target_pairs={{0,192},{64,0},{128,64},{192,128},{1,193},{65,1},{129,65},{193,129... | collective-permute-start | bytes 786440 | tf_op jit(solution)/shard_map/ppermute | solution.py:253
  179.6 20.8 %collective-permute-start.27 = (bf16[4,4,16,768]{3,2,1,0:T(8,128)(2,1)S(1)}, bf16[4,4,16,768]{3,2,1,0:T(8,128)(2,1)S(1)}, u32[]{:S(2)}, u32[]{:S(2)}) collective-permute-start(bf16[4,4,16,768]{3,2,1,0:T(8,128)(2,1)S(1)} %pad_maximum_fusion.4.refs_0_), channel_id=1, source_target_pairs={{0,64},{64,128},{128,192},{192,0},{1,65},{65,129},{129,193},{193,1... | collective-permute-start | bytes 1179656 | tf_op jit(solution)/shard_map/ppermute | solution.py:253
  179.8 20.5 %collective-permute-start.28 = (bf16[4,4,16,768]{3,2,1,0:T(8,128)(2,1)S(1)}, bf16[4,4,16,768]{3,2,1,0:T(8,128)(2,1)S(1)}, u32[]{:S(2)}, u32[]{:S(2)}) collective-permute-start(bf16[4,4,16,768]{3,2,1,0:T(8,128)(2,1)S(1)} %pad_maximum_fusion.4.refs_0_), channel_id=1, source_target_pairs={{0,128},{64,192},{128,0},{192,64},{1,129},{65,193},{129,1},{193,65... | collective-permute-start | bytes 1179656 | tf_op jit(solution)/shard_map/ppermute | solution.py:253
  182.7 18.3 %collective-permute-start.29 = (bf16[4,4,16,768]{3,2,1,0:T(8,128)(2,1)S(1)}, bf16[4,4,16,768]{3,2,1,0:T(8,128)(2,1)S(1)}, u32[]{:S(2)}, u32[]{:S(2)}) collective-permute-start(bf16[4,4,16,768]{3,2,1,0:T(8,128)(2,1)S(1)} %pad_maximum_fusion.4.refs_0_), channel_id=1, source_target_pairs={{0,192},{64,0},{128,64},{192,128},{1,193},{65,1},{129,65},{193,129... | collective-permute-start | bytes 1179656 | tf_op jit(solution)/shard_map/ppermute | solution.py:253
  (35 other events, 295.6 us)

commit v3 on v2

--- a/solution.py
+++ b/solution.py
@@ -283,26 +283,28 @@
     keep, give = turn(ids, x)
     pair = jnp.concatenate([keep, shift(give, "c", NC, 1)], axis=2)
     quarters = [pair[0]] + [shift(pair[t], "x", NX, t) for t in range(1, NX)]
+    send = jnp.stack([kv_rows, far]).reshape(NC, ROWS, 2, KV_HEADS, HEAD)
+    send = send.transpose(3, 0, 1, 2, 4).reshape(groups, ROWS, 2 * HEAD)
+    own, send, *quarters = lax.optimization_barrier((own, send, *quarters))
     xa, xb = (
         jnp.concatenate([t[h * FEATS : (h + 1) * FEATS] for t in quarters], axis=1) for h in range(NZH)
     )
-
-    send = jnp.stack([kv_rows, far]).reshape(NC, ROWS, 2, KV_HEADS, HEAD)
-    send = send.transpose(3, 0, 1, 2, 4).reshape(groups, ROWS, 2 * HEAD)
-    own, send = lax.optimization_barrier((own, send))
     kv = lax.all_to_all(send, ("y", "c"), 0, 0, tiled=True)
     kv_got = shift(kv, "c", NC, 1)
 
     xa_up, xb_up = shift(xa, "y", NY, 1), shift(xb, "y", NY, 1)
     xa_down, xb_down = shift(xa, "y", NY, -1), shift(xb, "y", NY, -1)
     dq, kept, given = attention(ids, span, lens, own, kv, kv_got)
+    dq, kept, given, xa_up, xb_down, xa_down, xb_up = lax.optimization_barrier(
+        (dq, kept, given, xa_up, xb_down, xa_down, xb_up)
+    )
     dqs = gather_x(dq)
     both = kept.astype(jnp.float32) + shift(given, "c", NC, 1).astype(jnp.float32)
+    both, xa_up, xb_down = lax.optimization_barrier((both, xa_up, xb_down))
+    xa_far, xb_far = shift(xa_up, "y", NY, 1), shift(xb_down, "y", NY, -1)
     got = shift(both[OWN:].astype(jnp.bfloat16), "zh", NZH, 1)
-    got, xa_up, xb_down, xa_down, xb_up, *dqs = lax.optimization_barrier(
-        (got, xa_up, xb_down, xa_down, xb_up, *dqs)
-    )
-    xa_far, xb_far = shift(xa_up, "y", NY, 1), shift(xb_down, "y", NY, -1)
+    got, *dqs = lax.optimization_barrier((got, *dqs))
+    xa_far, xb_far, *dqs = lax.optimization_barrier((xa_far, xb_far, *dqs))
     x_all = [xa, xa_up, xa_down, xa_far, xb, xb_up, xb_down, xb_far]
     mine = (both[:OWN] + got.astype(jnp.float32)).astype(jnp.bfloat16)
     mines = gather_x(mine)

time: 206 us -> 203 us (0.985)
  blocking collectives: 32.3 us -> 41.3 us
  starting transfers between devices: 52.1 us -> 46.2 us
  waiting for transfers between devices: 70.5 us -> 65 us
    all_to_all x0 -> x1, blocking collectives: none -> 12.9 us  [shards(): kv = lax.all_to_all(send, ('y', 'c'), 0, 0, tiled=True)]
    all_to_all x1 -> x0, waiting for transfers between devices: 6.73 us -> none  [shards(): kv = lax.all_to_all(send, ('y', 'c'), 0, 0, tiled=True)]
    all_to_all x1 -> x0, starting transfers between devices: 4.8 us -> none  [shards(): kv = lax.all_to_all(send, ('y', 'c'), 0, 0, tiled=True)]
    all_to_all x1, blocking collectives: 32.3 us -> 28.4 us  [shards(): lax.all_to_all(part.reshape(NZH * NZL * NY, sub, cols), ('zh', 'zl', 'y')...]
    unnamed x57 -> x61, local copies, waits for them, and re-layouts: 5.59 us -> 7.65 us
  transfers between devices with their start and end apart: 32 -> 31, of which waited for: 15 -> 16; matrix products, arithmetic and copies ran while one was open for 4% -> 3% of each run, Pallas kernels for 11% -> 11%
where the time goes in v3:
time: 203 us; the launch traced here: 202 us
  waiting for transfers between devices  65 us (32%)
  starting transfers between devices  46.2 us (23%)
  blocking collectives  41.3 us (20%)
  Pallas kernels  32.2 us (16%)
  local copies, waits for them, and re-layouts  13 us (6%)
  other arithmetic  3.42 us (2%)
    ppermute x30, waiting for transfers between devices, shift(): return lax.ppermute(value, axis, [(i, (i + s) % n) for i in range(n)])  65 us
    ppermute x30, starting transfers between devices, shift(): return lax.ppermute(value, axis, [(i, (i + s) % n) for i in range(n)])  41.4 us
    all_to_all x1, blocking collectives, shards(): lax.all_to_all(part.reshape(NZH * NZL * NY, sub, cols), ('zh', 'zl', 'y')...  28.4 us
    pallas_call x1, Pallas kernels, attention(): pl.pallas_call(attention_kernel, out_shape=(jax.ShapeDtypeStruct((OWN, 2...  14.7 us
    all_to_all x1, blocking collectives, shards(): kv = lax.all_to_all(send, ('y', 'c'), 0, 0, tiled=True)  12.9 us
    pallas_call x2, Pallas kernels, weight_term(): pl.pallas_call(functools.partial(weight_kernel, before is not None), out_...  11.6 us
    unnamed x61, local copies, waits for them, and re-layouts  7.65 us
    all_to_all x1, starting transfers between devices, shards(): own = lax.all_to_all(send, ('y', 'c'), 0, 0, tiled=True)  4.84 us
  transfers between devices with their start and end apart: 31, of which 16 were waited for; matrix products, arithmetic and copies ran while one was open for 3% of the time, Pallas kernels for 11%

profile of v3, /device:TPU:56, one launch (start us, length us, event | category | flops | bytes accessed | tf_op | source)
XLA Modules:
  0.0 202.2 jit_solution(11547211857295990825)
XLA Ops:
  4.5 2.6 %turn.1 = (bf16[4,512,128]{2,1,0:T(8,128)(2,1)}, bf16[4,512,128]{2,1,0:T(8,128)(2,1)}) custom-call(s32[5]{0:T(128)} %stack.47.ids, bf16[128,4096]{1,0:T(8,128)(2,1)} %x_ref), custom_call_target="tpu_custom_call" | custom-call | tf_op jit(solution)/shard_map/turn/pallas_call | solution.py:159
  7.1 4.8 %all-to-all-start = ((bf16[8,128,512]{2,1,0:T(8,128)(2,1)}), bf16[8,128,512]{2,1,0:T(8,128)(2,1)S(1)}, u32[]{:S(2)}, u32[]{:S(2)}) async-start(bf16[8,128,512]{2,1,0:T(8,128)(2,1)} %maximum_bitcast_fusion), calls=%async_computation | async-start | bytes 2097152 | tf_op jit(solution)/shard_map/all_to_all | solution.py:280
  11.9 6.3 %collective-permute-start = (bf16[128,1024]{1,0:T(8,128)(2,1)S(1)}, bf16[128,1024]{1,0:T(8,128)(2,1)S(1)}, u32[]{:S(2)}, u32[]{:S(2)}) collective-permute-start(bf16[128,1024]{1,0:T(8,128)(2,1)S(1)} %pad_maximum_fusion.5), channel_id=1, source_target_pairs={{0,8},{8,0},{1,9},{9,1},{2,10},{10,2},{3,11},{11,3},{4,12},{12,4},... | collective-permute-start | bytes 786440 | tf_op jit(solution)/shard_map/ppermute | solution.py:253
  20.8 2.7 %collective-permute-start.3 = (bf16[512,256]{1,0:T(8,128)(2,1)}, bf16[512,256]{1,0:T(8,128)(2,1)S(1)}, u32[]{:S(2)}, u32[]{:S(2)}) collective-permute-start(bf16[512,256]{1,0:T(8,128)(2,1)} %get-tuple-element.87), channel_id=1, source_target_pairs={{0,128},{64,192},{128,0},{192,64},{1,129},{65,193},{129,1},{193,65... | collective-permute-start | bytes 786440 | tf_op jit(solution)/shard_map/ppermute | solution.py:253
  25.4 5.1 %collective-permute-done = bf16[128,1024]{1,0:T(8,128)(2,1)S(1)} collective-permute-done((bf16[128,1024]{1,0:T(8,128)(2,1)S(1)}, bf16[128,1024]{1,0:T(8,128)(2,1)S(1)}, u32[]{:S(2)}, u32[]{:S(2)}) %collective-permute-start) | collective-permute-done | bytes 262176 | tf_op jit(solution)/shard_map/ppermute | solution.py:253
  32.0 3.5 %collective-permute-done.3 = bf16[512,256]{1,0:T(8,128)(2,1)S(1)} collective-permute-done((bf16[512,256]{1,0:T(8,128)(2,1)}, bf16[512,256]{1,0:T(8,128)(2,1)S(1)}, u32[]{:S(2)}, u32[]{:S(2)}) %collective-permute-start.3) | collective-permute-done | bytes 262176 | tf_op jit(solution)/shard_map/ppermute | solution.py:253
  35.4 12.9 %all_to_all.15.kv = bf16[8,128,256]{2,1,0:T(8,128)(2,1)S(1)} all-to-all(bf16[8,128,256]{2,1,0:T(8,128)(2,1)S(1)} %reshape.28), channel_id=1, replica_groups=mesh['x'=4,'zl'=4,'zh'=2,'y'=4,'c'=2] {'y','c'}, dimensions={0} | all-to-all | bytes 1048576 | tf_op jit(solution)/shard_map/all_to_all | solution.py:292
  49.2 3.2 %collective-permute-start.9 = (bf16[256,1024]{1,0:T(8,128)(2,1)S(1)}, bf16[256,1024]{1,0:T(8,128)(2,1)S(1)}, u32[]{:S(2)}, u32[]{:S(2)}) collective-permute-start(bf16[256,1024]{1,0:T(8,128)(2,1)S(1)} %pad_maximum_fusion.3.refs_4_), channel_id=1, source_target_pairs={{0,2},{2,4},{4,6},{6,0},{1,3},{3,5},{5,7},{7,1},{8,10},{10,12},{12... | collective-permute-start | bytes 1572872 | tf_op jit(solution)/shard_map/ppermute | solution.py:253
  55.4 14.7 %attention_backward.1 = (bf16[1024,256]{1,0:T(8,128)(2,1)}, bf16[2048,128]{1,0:T(8,128)(2,1)}, bf16[2048,128]{1,0:T(8,128)(2,1)}) custom-call(s32[5]{0:T(128)} %stack.47.ids, s32[32]{0:T(128)} %span.1, s32[1,8]{1,0:T(1,128)} %lens.1, bf16[8,128,512]{2,1,0:T(8,128)(2,1)} %copy-done.1, bf16[8,128,256]{2,1,0:T(8,128)(2,1)} %copy-done.5, ...), custom_call_target="tpu_custom_call" | custom-call | flops 14000000000 | bytes 28000000 | tf_op jit(solution)/shard_map/attention_backward/pallas_call | solution.py:123
  70.1 4.5 %collective-permute-done.6.refs_1_ = bf16[256,1024]{1,0:T(8,128)(2,1)S(1)} collective-permute-done((bf16[256,1024]{1,0:T(8,128)(2,1)S(1)}, bf16[256,1024]{1,0:T(8,128)(2,1)S(1)}, u32[]{:S(2)}, u32[]{:S(2)}) %collective-permute-start.6) | collective-permute-done | bytes 524320 | tf_op jit(solution)/shard_map/ppermute | solution.py:253
  81.8 3.2 %collective-permute-start.11 = (bf16[256,1024]{1,0:T(8,128)(2,1)S(1)}, bf16[256,1024]{1,0:T(8,128)(2,1)S(1)}, u32[]{:S(2)}, u32[]{:S(2)}) collective-permute-start(bf16[256,1024]{1,0:T(8,128)(2,1)S(1)} %collective-permute-done.6.refs_1_), channel_id=1, source_target_pairs={{0,2},{2,4},{4,6},{6,0},{1,3},{3,5},{5,7},{7,1},{8,10},{10,12},{12... | collective-permute-start | bytes 1572872 | tf_op jit(solution)/shard_map/ppermute | solution.py:253
  85.1 6.1 %collective-permute-done.14.refs_9_ = bf16[1024,256]{1,0:T(8,128)(2,1)S(1)} collective-permute-done((bf16[1024,256]{1,0:T(8,128)(2,1)}, bf16[1024,256]{1,0:T(8,128)(2,1)S(1)}, u32[]{:S(2)}, u32[]{:S(2)}) %collective-permute-start.14) | collective-permute-done | bytes 524320 | tf_op jit(solution)/shard_map/ppermute | solution.py:253
  93.3 9.6 %collective-permute-done.15.refs_10_ = bf16[1024,256]{1,0:T(8,128)(2,1)S(1)} collective-permute-done((bf16[1024,256]{1,0:T(8,128)(2,1)}, bf16[1024,256]{1,0:T(8,128)(2,1)S(1)}, u32[]{:S(2)}, u32[]{:S(2)}) %collective-permute-start.15) | collective-permute-done | bytes 524320 | tf_op jit(solution)/shard_map/ppermute | solution.py:253
  103.0 5.6 %collective-permute-done.13 = bf16[1024,128]{1,0:T(8,128)(2,1)S(1)} collective-permute-done((bf16[1024,128]{1,0:T(8,128)(2,1)S(1)}, bf16[1024,128]{1,0:T(8,128)(2,1)S(1)}, u32[]{:S(2)}, u32[]{:S(2)}) %collective-permute-start.13) | collective-permute-done | bytes 262176 | tf_op jit(solution)/shard_map/ppermute | solution.py:253
  116.9 6.5 %weight_term.2.refs_16_ = bf16[2,4,4,16,512]{4,3,2,1,0:T(8,128)(2,1)} custom-call(s32[5]{0:T(128)} %stack.47.ids, bf16[256,1024]{1,0:T(8,128)(2,1)} %copy-done.4, bf16[256,1024]{1,0:T(8,128)(2,1)} %copy-done.21, bf16[256,1024]{1,0:T(8,128)(2,1)} %copy-done.22, bf16[256,1024]{1,0:T(8,128)(2,1)} %copy-done.23, bf16[256,1024]{1,0:T(8,128)(2,1)} %copy-done.3, ...), custom_call_target="tpu_custom_call" | custom-call | flops 5000000000 | bytes 10000000 | tf_op jit(solution)/shard_map/weight_term/pallas_call | solution.py:204
  130.7 5.1 %weight_term.3 = bf16[2,4,4,16,768]{4,3,2,1,0:T(8,128)(2,1)} custom-call(s32[5]{0:T(128)} %stack.47.ids, bf16[256,1024]{1,0:T(8,128)(2,1)} %copy-done.4, bf16[256,1024]{1,0:T(8,128)(2,1)} %copy-done.21, bf16[256,1024]{1,0:T(8,128)(2,1)} %copy-done.22, bf16[256,1024]{1,0:T(8,128)(2,1)} %copy-done.23, bf16[256,1024]{1,0:T(8,128)(2,1)} %copy-done.3, ...), custom_call_target="tpu_custom_call" | custom-call | flops 5000000000 | bytes 10000000 | tf_op jit(solution)/shard_map/weight_term/pallas_call | solution.py:204
  135.8 28.4 %all_to_all.16 = bf16[32,16,768]{2,1,0:T(8,128)(2,1)S(1)} all-to-all(bf16[32,16,768]{2,1,0:T(8,128)(2,1)} %bitcast.28), channel_id=1, replica_groups=mesh['x'=4,'zl'=4,'zh'=2,'y'=4,'c'=2] {'zh','zl','y'}, dimensions={0} | all-to-all | bytes 1572864 | tf_op jit(solution)/shard_map/all_to_all | solution.py:315
  164.5 3.7 %collective-permute-start.25 = (bf16[4,16,768]{2,1,0:T(8,128)(2,1)S(1)}, bf16[4,16,768]{2,1,0:T(8,128)(2,1)S(1)}, u32[]{:S(2)}, u32[]{:S(2)}) collective-permute-start(bf16[4,16,768]{2,1,0:T(8,128)(2,1)S(1)} %reduce_sum.12), channel_id=1, source_target_pairs={{0,32},{16,48},{32,0},{48,16},{1,33},{17,49},{33,1},{49,17},{2,34}... | collective-permute-start | bytes 294920 | tf_op jit(solution)/shard_map/ppermute | solution.py:253
  170.1 2.8 %collective-permute-done.25 = bf16[4,16,768]{2,1,0:T(8,128)(2,1)S(1)} collective-permute-done((bf16[4,16,768]{2,1,0:T(8,128)(2,1)S(1)}, bf16[4,16,768]{2,1,0:T(8,128)(2,1)S(1)}, u32[]{:S(2)}, u32[]{:S(2)}) %collective-permute-start.25) | collective-permute-done | bytes 98336 | tf_op jit(solution)/shard_map/ppermute | solution.py:253
  172.9 2.8 %collective-permute-done.26 = bf16[4,16,768]{2,1,0:T(8,128)(2,1)S(1)} collective-permute-done((bf16[4,16,768]{2,1,0:T(8,128)(2,1)S(1)}, bf16[4,16,768]{2,1,0:T(8,128)(2,1)S(1)}, u32[]{:S(2)}, u32[]{:S(2)}) %collective-permute-start.26) | collective-permute-done | bytes 98336 | tf_op jit(solution)/shard_map/ppermute | solution.py:253
  176.9 3.1 %collective-permute-start.28 = (bf16[4,4,16,768]{3,2,1,0:T(8,128)(2,1)S(1)}, bf16[4,4,16,768]{3,2,1,0:T(8,128)(2,1)S(1)}, u32[]{:S(2)}, u32[]{:S(2)}) collective-permute-start(bf16[4,4,16,768]{3,2,1,0:T(8,128)(2,1)S(1)} %pad_maximum_fusion.4.refs_0_), channel_id=1, source_target_pairs={{0,128},{64,192},{128,0},{192,64},{1,129},{65,193},{129,1},{193,65... | collective-permute-start | bytes 1179656 | tf_op jit(solution)/shard_map/ppermute | solution.py:253
  180.2 8.1 %collective-permute-done.27.refs_1_ = bf16[4,4,16,768]{3,2,1,0:T(8,128)(2,1)S(1)} collective-permute-done((bf16[4,4,16,768]{3,2,1,0:T(8,128)(2,1)S(1)}, bf16[4,4,16,768]{3,2,1,0:T(8,128)(2,1)S(1)}, u32[]{:S(2)}, u32[]{:S(2)}) %collective-permute-start.27) | collective-permute-done | bytes 393248 | tf_op jit(solution)/shard_map/ppermute | solution.py:253
  188.2 9.2 %collective-permute-done.28.refs_2_ = bf16[4,4,16,768]{3,2,1,0:T(8,128)(2,1)S(1)} collective-permute-done((bf16[4,4,16,768]{3,2,1,0:T(8,128)(2,1)S(1)}, bf16[4,4,16,768]{3,2,1,0:T(8,128)(2,1)S(1)}, u32[]{:S(2)}, u32[]{:S(2)}) %collective-permute-start.28) | collective-permute-done | bytes 393248 | tf_op jit(solution)/shard_map/ppermute | solution.py:253
  198.9 3.3 %finish.1 = (f32[256,2048]{1,0:T(8,128)}, f32[256,512]{1,0:T(8,128)}, f32[256,512]{1,0:T(8,128)}) custom-call(s32[5]{0:T(128)} %stack.47.ids, bf16[4,4,16,768]{3,2,1,0:T(8,128)(2,1)} %copy-done, bf16[4,4,16,768]{3,2,1,0:T(8,128)(2,1)} %copy-done.10, bf16[4,4,16,768]{3,2,1,0:T(8,128)(2,1)} %copy-done.11, bf16[4,4,16,768]{3,2,1,0:T(8,128)(2,1)} %copy-done.12), custom_call_target="tpu_custom_call" | custom-call | tf_op jit(solution)/shard_map/finish/pallas_call | solution.py:238
  (132 shorter events, 43.3 us)
Async XLA Ops:
  7.0 11.2 %collective-permute-start.1 = (bf16[4,512,128]{2,1,0:T(8,128)(2,1)}, bf16[4,512,128]{2,1,0:T(8,128)(2,1)S(1)}, u32[]{:S(2)}, u32[]{:S(2)}) collective-permute-start(bf16[4,512,128]{2,1,0:T(8,128)(2,1)} %get-tuple-element.47), channel_id=1, source_target_pairs={{0,1},{1,0},{2,3},{3,2},{4,5},{5,4},{6,7},{7,6},{8,9},{9,8},{10,11... | collective-permute-start | bytes 1572872 | tf_op jit(solution)/shard_map/ppermute | solution.py:253
  7.1 28.4 %all-to-all-start = ((bf16[8,128,512]{2,1,0:T(8,128)(2,1)}), bf16[8,128,512]{2,1,0:T(8,128)(2,1)S(1)}, u32[]{:S(2)}, u32[]{:S(2)}) async-start(bf16[8,128,512]{2,1,0:T(8,128)(2,1)} %maximum_bitcast_fusion), calls=%async_computation | async-start | bytes 2097152 | tf_op jit(solution)/shard_map/all_to_all | solution.py:280
  11.9 18.6 %collective-permute-start = (bf16[128,1024]{1,0:T(8,128)(2,1)S(1)}, bf16[128,1024]{1,0:T(8,128)(2,1)S(1)}, u32[]{:S(2)}, u32[]{:S(2)}) collective-permute-start(bf16[128,1024]{1,0:T(8,128)(2,1)S(1)} %pad_maximum_fusion.5), channel_id=1, source_target_pairs={{0,8},{8,0},{1,9},{9,1},{2,10},{10,2},{3,11},{11,3},{4,12},{12,4},... | collective-permute-start | bytes 786440 | tf_op jit(solution)/shard_map/ppermute | solution.py:253
  19.3 12.6 %collective-permute-start.2 = (bf16[512,256]{1,0:T(8,128)(2,1)}, bf16[512,256]{1,0:T(8,128)(2,1)S(1)}, u32[]{:S(2)}, u32[]{:S(2)}) collective-permute-start(bf16[512,256]{1,0:T(8,128)(2,1)} %get-tuple-element.88), channel_id=1, source_target_pairs={{0,64},{64,128},{128,192},{192,0},{1,65},{65,129},{129,193},{193,1... | collective-permute-start | bytes 786440 | tf_op jit(solution)/shard_map/ppermute | solution.py:253
  20.8 14.6 %collective-permute-start.3 = (bf16[512,256]{1,0:T(8,128)(2,1)}, bf16[512,256]{1,0:T(8,128)(2,1)S(1)}, u32[]{:S(2)}, u32[]{:S(2)}) collective-permute-start(bf16[512,256]{1,0:T(8,128)(2,1)} %get-tuple-element.87), channel_id=1, source_target_pairs={{0,128},{64,192},{128,0},{192,64},{1,129},{65,193},{129,1},{193,65... | collective-permute-start | bytes 786440 | tf_op jit(solution)/shard_map/ppermute | solution.py:253
  23.6 11.9 %collective-permute-start.4 = (bf16[512,256]{1,0:T(8,128)(2,1)}, bf16[512,256]{1,0:T(8,128)(2,1)S(1)}, u32[]{:S(2)}, u32[]{:S(2)}) collective-permute-start(bf16[512,256]{1,0:T(8,128)(2,1)} %get-tuple-element.86), channel_id=1, source_target_pairs={{0,192},{64,0},{128,64},{192,128},{1,193},{65,1},{129,65},{193,129... | collective-permute-start | bytes 786440 | tf_op jit(solution)/shard_map/ppermute | solution.py:253
  49.2 20.9 %collective-permute-start.7 = (bf16[256,1024]{1,0:T(8,128)(2,1)S(1)}, bf16[256,1024]{1,0:T(8,128)(2,1)S(1)}, u32[]{:S(2)}, u32[]{:S(2)}) collective-permute-start(bf16[256,1024]{1,0:T(8,128)(2,1)S(1)} %pad_maximum_fusion.3.refs_4_), channel_id=1, source_target_pairs={{0,6},{2,0},{4,2},{6,4},{1,7},{3,1},{5,3},{7,5},{8,14},{10,8},{12,... | collective-permute-start | bytes 1572872 | tf_op jit(solution)/shard_map/ppermute | solution.py:253
  49.2 21.0 %collective-permute-start.9 = (bf16[256,1024]{1,0:T(8,128)(2,1)S(1)}, bf16[256,1024]{1,0:T(8,128)(2,1)S(1)}, u32[]{:S(2)}, u32[]{:S(2)}) collective-permute-start(bf16[256,1024]{1,0:T(8,128)(2,1)S(1)} %pad_maximum_fusion.3.refs_4_), channel_id=1, source_target_pairs={{0,2},{2,4},{4,6},{6,0},{1,3},{3,5},{5,7},{7,1},{8,10},{10,12},{12... | collective-permute-start | bytes 1572872 | tf_op jit(solution)/shard_map/ppermute | solution.py:253
  52.5 22.2 %collective-permute-start.6 = (bf16[256,1024]{1,0:T(8,128)(2,1)S(1)}, bf16[256,1024]{1,0:T(8,128)(2,1)S(1)}, u32[]{:S(2)}, u32[]{:S(2)}) collective-permute-start(bf16[256,1024]{1,0:T(8,128)(2,1)S(1)} %pad_maximum_fusion.2.refs_0_), channel_id=1, source_target_pairs={{0,2},{2,4},{4,6},{6,0},{1,3},{3,5},{5,7},{7,1},{8,10},{10,12},{12... | collective-permute-start | bytes 1572872 | tf_op jit(solution)/shard_map/ppermute | solution.py:253
  53.4 22.0 %collective-permute-start.8 = (bf16[256,1024]{1,0:T(8,128)(2,1)S(1)}, bf16[256,1024]{1,0:T(8,128)(2,1)S(1)}, u32[]{:S(2)}, u32[]{:S(2)}) collective-permute-start(bf16[256,1024]{1,0:T(8,128)(2,1)S(1)} %pad_maximum_fusion.2.refs_0_), channel_id=1, source_target_pairs={{0,6},{2,0},{4,2},{6,4},{1,7},{3,1},{5,3},{7,5},{8,14},{10,8},{12,... | collective-permute-start | bytes 1572872 | tf_op jit(solution)/shard_map/ppermute | solution.py:253
  75.4 15.8 %collective-permute-start.14 = (bf16[1024,256]{1,0:T(8,128)(2,1)}, bf16[1024,256]{1,0:T(8,128)(2,1)S(1)}, u32[]{:S(2)}, u32[]{:S(2)}) collective-permute-start(bf16[1024,256]{1,0:T(8,128)(2,1)} %get-tuple-element.73.refs_8_), channel_id=1, source_target_pairs={{0,64},{64,128},{128,192},{192,0},{1,65},{65,129},{129,193},{193,1... | collective-permute-start | bytes 1572872 | tf_op jit(solution)/shard_map/ppermute | solution.py:253
  76.7 26.1 %collective-permute-start.15 = (bf16[1024,256]{1,0:T(8,128)(2,1)}, bf16[1024,256]{1,0:T(8,128)(2,1)S(1)}, u32[]{:S(2)}, u32[]{:S(2)}) collective-permute-start(bf16[1024,256]{1,0:T(8,128)(2,1)} %get-tuple-element.73.refs_8_), channel_id=1, source_target_pairs={{0,128},{64,192},{128,0},{192,64},{1,129},{65,193},{129,1},{193,65... | collective-permute-start | bytes 1572872 | tf_op jit(solution)/shard_map/ppermute | solution.py:253
  79.1 23.9 %collective-permute-start.16 = (bf16[1024,256]{1,0:T(8,128)(2,1)}, bf16[1024,256]{1,0:T(8,128)(2,1)S(1)}, u32[]{:S(2)}, u32[]{:S(2)}) collective-permute-start(bf16[1024,256]{1,0:T(8,128)(2,1)} %get-tuple-element.73.refs_8_), channel_id=1, source_target_pairs={{0,192},{64,0},{128,64},{192,128},{1,193},{65,1},{129,65},{193,129... | collective-permute-start | bytes 1572872 | tf_op jit(solution)/shard_map/ppermute | solution.py:253
  81.8 26.8 %collective-permute-start.11 = (bf16[256,1024]{1,0:T(8,128)(2,1)S(1)}, bf16[256,1024]{1,0:T(8,128)(2,1)S(1)}, u32[]{:S(2)}, u32[]{:S(2)}) collective-permute-start(bf16[256,1024]{1,0:T(8,128)(2,1)S(1)} %collective-permute-done.6.refs_1_), channel_id=1, source_target_pairs={{0,2},{2,4},{4,6},{6,0},{1,3},{3,5},{5,7},{7,1},{8,10},{10,12},{12... | collective-permute-start | bytes 1572872 | tf_op jit(solution)/shard_map/ppermute | solution.py:253
  85.1 24.4 %collective-permute-start.12 = (bf16[256,1024]{1,0:T(8,128)(2,1)S(1)}, bf16[256,1024]{1,0:T(8,128)(2,1)S(1)}, u32[]{:S(2)}, u32[]{:S(2)}) collective-permute-start(bf16[256,1024]{1,0:T(8,128)(2,1)S(1)} %collective-permute-done.7.refs_6_), channel_id=1, source_target_pairs={{0,6},{2,0},{4,2},{6,4},{1,7},{3,1},{5,3},{7,5},{8,14},{10,8},{12,... | collective-permute-start | bytes 1572872 | tf_op jit(solution)/shard_map/ppermute | solution.py:253
  91.2 17.5 %collective-permute-start.13 = (bf16[1024,128]{1,0:T(8,128)(2,1)S(1)}, bf16[1024,128]{1,0:T(8,128)(2,1)S(1)}, u32[]{:S(2)}, u32[]{:S(2)}) collective-permute-start(bf16[1024,128]{1,0:T(8,128)(2,1)S(1)} %slice.98), channel_id=1, source_target_pairs={{0,8},{8,0},{1,9},{9,1},{2,10},{10,2},{3,11},{11,3},{4,12},{12,4},... | collective-permute-start | bytes 786440 | tf_op jit(solution)/shard_map/ppermute | solution.py:253
  110.8 15.1 %collective-permute-start.19 = (bf16[1024,128]{1,0:T(8,128)(2,1)S(1)}, bf16[1024,128]{1,0:T(8,128)(2,1)S(1)}, u32[]{:S(2)}, u32[]{:S(2)}) collective-permute-start(bf16[1024,128]{1,0:T(8,128)(2,1)S(1)} %add_convert_fusion.refs_8_), channel_id=1, source_target_pairs={{0,64},{64,128},{128,192},{192,0},{1,65},{65,129},{129,193},{193,1... | collective-permute-start | bytes 786440 | tf_op jit(solution)/shard_map/ppermute | solution.py:253
  111.0 14.9 %collective-permute-start.20 = (bf16[1024,128]{1,0:T(8,128)(2,1)S(1)}, bf16[1024,128]{1,0:T(8,128)(2,1)S(1)}, u32[]{:S(2)}, u32[]{:S(2)}) collective-permute-start(bf16[1024,128]{1,0:T(8,128)(2,1)S(1)} %add_convert_fusion.refs_8_), channel_id=1, source_target_pairs={{0,128},{64,192},{128,0},{192,64},{1,129},{65,193},{129,1},{193,65... | collective-permute-start | bytes 786440 | tf_op jit(solution)/shard_map/ppermute | solution.py:253
  113.4 13.2 %collective-permute-start.21 = (bf16[1024,128]{1,0:T(8,128)(2,1)S(1)}, bf16[1024,128]{1,0:T(8,128)(2,1)S(1)}, u32[]{:S(2)}, u32[]{:S(2)}) collective-permute-start(bf16[1024,128]{1,0:T(8,128)(2,1)S(1)} %add_convert_fusion.refs_8_), channel_id=1, source_target_pairs={{0,192},{64,0},{128,64},{192,128},{1,193},{65,1},{129,65},{193,129... | collective-permute-start | bytes 786440 | tf_op jit(solution)/shard_map/ppermute | solution.py:253
  164.5 8.5 %collective-permute-start.25 = (bf16[4,16,768]{2,1,0:T(8,128)(2,1)S(1)}, bf16[4,16,768]{2,1,0:T(8,128)(2,1)S(1)}, u32[]{:S(2)}, u32[]{:S(2)}) collective-permute-start(bf16[4,16,768]{2,1,0:T(8,128)(2,1)S(1)} %reduce_sum.12), channel_id=1, source_target_pairs={{0,32},{16,48},{32,0},{48,16},{1,33},{17,49},{33,1},{49,17},{2,34}... | collective-permute-start | bytes 294920 | tf_op jit(solution)/shard_map/ppermute | solution.py:253
  168.2 7.6 %collective-permute-start.26 = (bf16[4,16,768]{2,1,0:T(8,128)(2,1)S(1)}, bf16[4,16,768]{2,1,0:T(8,128)(2,1)S(1)}, u32[]{:S(2)}, u32[]{:S(2)}) collective-permute-start(bf16[4,16,768]{2,1,0:T(8,128)(2,1)S(1)} %reduce_sum.12), channel_id=1, source_target_pairs={{0,48},{16,0},{32,16},{48,32},{1,49},{17,1},{33,17},{49,33},{2,50}... | collective-permute-start | bytes 294920 | tf_op jit(solution)/shard_map/ppermute | solution.py:253
  175.8 12.4 %collective-permute-start.27 = (bf16[4,4,16,768]{3,2,1,0:T(8,128)(2,1)S(1)}, bf16[4,4,16,768]{3,2,1,0:T(8,128)(2,1)S(1)}, u32[]{:S(2)}, u32[]{:S(2)}) collective-permute-start(bf16[4,4,16,768]{3,2,1,0:T(8,128)(2,1)S(1)} %pad_maximum_fusion.4.refs_0_), channel_id=1, source_target_pairs={{0,64},{64,128},{128,192},{192,0},{1,65},{65,129},{129,193},{193,1... | collective-permute-start | bytes 1179656 | tf_op jit(solution)/shard_map/ppermute | solution.py:253
  176.9 20.5 %collective-permute-start.28 = (bf16[4,4,16,768]{3,2,1,0:T(8,128)(2,1)S(1)}, bf16[4,4,16,768]{3,2,1,0:T(8,128)(2,1)S(1)}, u32[]{:S(2)}, u32[]{:S(2)}) collective-permute-start(bf16[4,4,16,768]{3,2,1,0:T(8,128)(2,1)S(1)} %pad_maximum_fusion.4.refs_0_), channel_id=1, source_target_pairs={{0,128},{64,192},{128,0},{192,64},{1,129},{65,193},{129,1},{193,65... | collective-permute-start | bytes 1179656 | tf_op jit(solution)/shard_map/ppermute | solution.py:253
  180.0 17.4 %collective-permute-start.29 = (bf16[4,4,16,768]{3,2,1,0:T(8,128)(2,1)S(1)}, bf16[4,4,16,768]{3,2,1,0:T(8,128)(2,1)S(1)}, u32[]{:S(2)}, u32[]{:S(2)}) collective-permute-start(bf16[4,4,16,768]{3,2,1,0:T(8,128)(2,1)S(1)} %pad_maximum_fusion.4.refs_0_), channel_id=1, source_target_pairs={{0,192},{64,0},{128,64},{192,128},{1,193},{65,1},{129,65},{193,129... | collective-permute-start | bytes 1179656 | tf_op jit(solution)/shard_map/ppermute | solution.py:253
  (36 other events, 369.5 us)

commit v4 on v3

--- a/solution.py
+++ b/solution.py
@@ -300,11 +300,12 @@
     )
     dqs = gather_x(dq)
     both = kept.astype(jnp.float32) + shift(given, "c", NC, 1).astype(jnp.float32)
-    both, xa_up, xb_down = lax.optimization_barrier((both, xa_up, xb_down))
-    xa_far, xb_far = shift(xa_up, "y", NY, 1), shift(xb_down, "y", NY, -1)
+    both, xa_up = lax.optimization_barrier((both, xa_up))
+    xa_far = shift(xa_up, "y", NY, 1)
     got = shift(both[OWN:].astype(jnp.bfloat16), "zh", NZH, 1)
-    got, *dqs = lax.optimization_barrier((got, *dqs))
-    xa_far, xb_far, *dqs = lax.optimization_barrier((xa_far, xb_far, *dqs))
+    got, xb_down, *dqs = lax.optimization_barrier((got, xb_down, *dqs))
+    xb_far = shift(xb_down, "y", NY, -1)
+    xa_far, *dqs = lax.optimization_barrier((xa_far, *dqs))
     x_all = [xa, xa_up, xa_down, xa_far, xb, xb_up, xb_down, xb_far]
     mine = (both[:OWN] + got.astype(jnp.float32)).astype(jnp.bfloat16)
     mines = gather_x(mine)

time: 203 us -> 203 us (level)
  starting transfers between devices: 46.2 us -> 49 us
    ppermute x30, starting transfers between devices: 41.4 us -> 44.1 us  [shift(): return lax.ppermute(value, axis, [(i, (i + s) % n) for i in range(n)])]
    unnamed x61 -> x59, local copies, waits for them, and re-layouts: 7.65 us -> 7.02 us
  transfers between devices with their start and end apart: 31 -> 31, of which waited for: 16 -> 15; matrix products, arithmetic and copies ran while one was open for 3% -> 3% of each run, Pallas kernels for 11% -> 10%
where the time goes in v4:
time: 203 us
  waiting for transfers between devices  63.6 us (31%)
  starting transfers between devices  49 us (24%)
  blocking collectives  41.6 us (20%)
  Pallas kernels  31.6 us (16%)
  local copies, waits for them, and re-layouts  12.3 us (6%)
  other arithmetic  3.42 us (2%)
    ppermute x30, waiting for transfers between devices, shift(): return lax.ppermute(value, axis, [(i, (i + s) % n) for i in range(n)])  63.6 us
    ppermute x30, starting transfers between devices, shift(): return lax.ppermute(value, axis, [(i, (i + s) % n) for i in range(n)])  44.1 us
    all_to_all x1, blocking collectives, shards(): lax.all_to_all(part.reshape(NZH * NZL * NY, sub, cols), ('zh', 'zl', 'y')...  28.6 us
    pallas_call x1, Pallas kernels, attention(): pl.pallas_call(attention_kernel, out_shape=(jax.ShapeDtypeStruct((OWN, 2...  14.2 us
    all_to_all x1, blocking collectives, shards(): kv = lax.all_to_all(send, ('y', 'c'), 0, 0, tiled=True)  12.9 us
    pallas_call x2, Pallas kernels, weight_term(): pl.pallas_call(functools.partial(weight_kernel, before is not None), out_...  11.6 us
    unnamed x59, local copies, waits for them, and re-layouts  7.02 us
    all_to_all x1, starting transfers between devices, shards(): own = lax.all_to_all(send, ('y', 'c'), 0, 0, tiled=True)  4.84 us
  transfers between devices with their start and end apart: 31, of which 15 were waited for; matrix products, arithmetic and copies ran while one was open for 3% of the time, Pallas kernels for 10%

profile of v4, /device:TPU:56, one launch (start us, length us, event | category | flops | bytes accessed | tf_op | source)
XLA Modules:
  0.0 202.6 jit_solution(2745141316685064335)
XLA Ops:
  4.5 2.6 %turn.1 = (bf16[4,512,128]{2,1,0:T(8,128)(2,1)}, bf16[4,512,128]{2,1,0:T(8,128)(2,1)}) custom-call(s32[5]{0:T(128)} %stack.47.ids, bf16[128,4096]{1,0:T(8,128)(2,1)} %x_ref), custom_call_target="tpu_custom_call" | custom-call | tf_op jit(solution)/shard_map/turn/pallas_call | solution.py:159
  7.0 4.8 %all-to-all-start = ((bf16[8,128,512]{2,1,0:T(8,128)(2,1)}), bf16[8,128,512]{2,1,0:T(8,128)(2,1)S(1)}, u32[]{:S(2)}, u32[]{:S(2)}) async-start(bf16[8,128,512]{2,1,0:T(8,128)(2,1)} %maximum_bitcast_fusion), calls=%async_computation | async-start | bytes 2097152 | tf_op jit(solution)/shard_map/all_to_all | solution.py:280
  11.9 6.3 %collective-permute-start = (bf16[128,1024]{1,0:T(8,128)(2,1)S(1)}, bf16[128,1024]{1,0:T(8,128)(2,1)S(1)}, u32[]{:S(2)}, u32[]{:S(2)}) collective-permute-start(bf16[128,1024]{1,0:T(8,128)(2,1)S(1)} %pad_maximum_fusion.5), channel_id=1, source_target_pairs={{0,8},{8,0},{1,9},{9,1},{2,10},{10,2},{3,11},{11,3},{4,12},{12,4},... | collective-permute-start | bytes 786440 | tf_op jit(solution)/shard_map/ppermute | solution.py:253
  20.8 2.7 %collective-permute-start.3 = (bf16[512,256]{1,0:T(8,128)(2,1)}, bf16[512,256]{1,0:T(8,128)(2,1)S(1)}, u32[]{:S(2)}, u32[]{:S(2)}) collective-permute-start(bf16[512,256]{1,0:T(8,128)(2,1)} %get-tuple-element.85), channel_id=1, source_target_pairs={{0,128},{64,192},{128,0},{192,64},{1,129},{65,193},{129,1},{193,65... | collective-permute-start | bytes 786440 | tf_op jit(solution)/shard_map/ppermute | solution.py:253
  25.3 5.1 %collective-permute-done = bf16[128,1024]{1,0:T(8,128)(2,1)S(1)} collective-permute-done((bf16[128,1024]{1,0:T(8,128)(2,1)S(1)}, bf16[128,1024]{1,0:T(8,128)(2,1)S(1)}, u32[]{:S(2)}, u32[]{:S(2)}) %collective-permute-start) | collective-permute-done | bytes 262176 | tf_op jit(solution)/shard_map/ppermute | solution.py:253
  31.9 3.5 %collective-permute-done.3 = bf16[512,256]{1,0:T(8,128)(2,1)S(1)} collective-permute-done((bf16[512,256]{1,0:T(8,128)(2,1)}, bf16[512,256]{1,0:T(8,128)(2,1)S(1)}, u32[]{:S(2)}, u32[]{:S(2)}) %collective-permute-start.3) | collective-permute-done | bytes 262176 | tf_op jit(solution)/shard_map/ppermute | solution.py:253
  35.4 12.9 %all_to_all.15.kv = bf16[8,128,256]{2,1,0:T(8,128)(2,1)S(1)} all-to-all(bf16[8,128,256]{2,1,0:T(8,128)(2,1)S(1)} %reshape.28), channel_id=1, replica_groups=mesh['x'=4,'zl'=4,'zh'=2,'y'=4,'c'=2] {'y','c'}, dimensions={0} | all-to-all | bytes 1048576 | tf_op jit(solution)/shard_map/all_to_all | solution.py:292
  49.1 3.2 %collective-permute-start.9 = (bf16[256,1024]{1,0:T(8,128)(2,1)S(1)}, bf16[256,1024]{1,0:T(8,128)(2,1)S(1)}, u32[]{:S(2)}, u32[]{:S(2)}) collective-permute-start(bf16[256,1024]{1,0:T(8,128)(2,1)S(1)} %pad_maximum_fusion.3.refs_4_), channel_id=1, source_target_pairs={{0,2},{2,4},{4,6},{6,0},{1,3},{3,5},{5,7},{7,1},{8,10},{10,12},{12... | collective-permute-start | bytes 1572872 | tf_op jit(solution)/shard_map/ppermute | solution.py:253
  55.3 14.2 %attention_backward.1 = (bf16[1024,256]{1,0:T(8,128)(2,1)}, bf16[2048,128]{1,0:T(8,128)(2,1)}, bf16[2048,128]{1,0:T(8,128)(2,1)}) custom-call(s32[5]{0:T(128)} %stack.47.ids, s32[32]{0:T(128)} %span.1, s32[1,8]{1,0:T(1,128)} %lens.1, bf16[8,128,512]{2,1,0:T(8,128)(2,1)} %copy-done.1, bf16[8,128,256]{2,1,0:T(8,128)(2,1)} %copy-done.5, ...), custom_call_target="tpu_custom_call" | custom-call | flops 14000000000 | bytes 28000000 | tf_op jit(solution)/shard_map/attention_backward/pallas_call | solution.py:123
  69.6 5.1 %collective-permute-done.6.refs_1_ = bf16[256,1024]{1,0:T(8,128)(2,1)S(1)} collective-permute-done((bf16[256,1024]{1,0:T(8,128)(2,1)S(1)}, bf16[256,1024]{1,0:T(8,128)(2,1)S(1)}, u32[]{:S(2)}, u32[]{:S(2)}) %collective-permute-start.6) | collective-permute-done | bytes 524320 | tf_op jit(solution)/shard_map/ppermute | solution.py:253
  81.8 3.2 %collective-permute-start.11 = (bf16[256,1024]{1,0:T(8,128)(2,1)S(1)}, bf16[256,1024]{1,0:T(8,128)(2,1)}, u32[]{:S(2)}, u32[]{:S(2)}) collective-permute-start(bf16[256,1024]{1,0:T(8,128)(2,1)S(1)} %collective-permute-done.6.refs_1_), channel_id=1, source_target_pairs={{0,2},{2,4},{4,6},{6,0},{1,3},{3,5},{5,7},{7,1},{8,10},{10,12},{12... | collective-permute-start | bytes 1572872 | tf_op jit(solution)/shard_map/ppermute | solution.py:253
  85.1 2.6 %collective-permute-start.12 = (bf16[1024,128]{1,0:T(8,128)(2,1)S(1)}, bf16[1024,128]{1,0:T(8,128)(2,1)S(1)}, u32[]{:S(2)}, u32[]{:S(2)}) collective-permute-start(bf16[1024,128]{1,0:T(8,128)(2,1)S(1)} %slice.98), channel_id=1, source_target_pairs={{0,8},{8,0},{1,9},{9,1},{2,10},{10,2},{3,11},{11,3},{4,12},{12,4},... | collective-permute-start | bytes 786440 | tf_op jit(solution)/shard_map/ppermute | solution.py:253
  87.7 3.5 %collective-permute-done.13.refs_9_ = bf16[1024,256]{1,0:T(8,128)(2,1)S(1)} collective-permute-done((bf16[1024,256]{1,0:T(8,128)(2,1)}, bf16[1024,256]{1,0:T(8,128)(2,1)S(1)}, u32[]{:S(2)}, u32[]{:S(2)}) %collective-permute-start.13) | collective-permute-done | bytes 524320 | tf_op jit(solution)/shard_map/ppermute | solution.py:253
  91.1 11.7 %collective-permute-done.14.refs_10_ = bf16[1024,256]{1,0:T(8,128)(2,1)S(1)} collective-permute-done((bf16[1024,256]{1,0:T(8,128)(2,1)}, bf16[1024,256]{1,0:T(8,128)(2,1)S(1)}, u32[]{:S(2)}, u32[]{:S(2)}) %collective-permute-start.14) | collective-permute-done | bytes 524320 | tf_op jit(solution)/shard_map/ppermute | solution.py:253
  111.3 8.2 %collective-permute-done.16.refs_7_ = bf16[256,1024]{1,0:T(8,128)(2,1)S(1)} collective-permute-done((bf16[256,1024]{1,0:T(8,128)(2,1)S(1)}, bf16[256,1024]{1,0:T(8,128)(2,1)S(1)}, u32[]{:S(2)}, u32[]{:S(2)}) %collective-permute-start.16) | collective-permute-done | bytes 524320 | tf_op jit(solution)/shard_map/ppermute | solution.py:253
  120.5 6.5 %weight_term.2.refs_16_ = bf16[2,4,4,16,512]{4,3,2,1,0:T(8,128)(2,1)} custom-call(s32[5]{0:T(128)} %stack.47.ids, bf16[256,1024]{1,0:T(8,128)(2,1)} %copy-done.4, bf16[256,1024]{1,0:T(8,128)(2,1)} %copy-done.21, bf16[256,1024]{1,0:T(8,128)(2,1)} %copy-done.22, bf16[256,1024]{1,0:T(8,128)(2,1)} %collective-permute-done.11.refs_3_, ...), custom_call_target="tpu_custom_call" | custom-call | flops 5000000000 | bytes 10000000 | tf_op jit(solution)/shard_map/weight_term/pallas_call | solution.py:204
  131.2 5.1 %weight_term.3 = bf16[2,4,4,16,768]{4,3,2,1,0:T(8,128)(2,1)} custom-call(s32[5]{0:T(128)} %stack.47.ids, bf16[256,1024]{1,0:T(8,128)(2,1)} %copy-done.4, bf16[256,1024]{1,0:T(8,128)(2,1)} %copy-done.21, bf16[256,1024]{1,0:T(8,128)(2,1)} %copy-done.22, bf16[256,1024]{1,0:T(8,128)(2,1)} %collective-permute-done.11.refs_3_, bf16[256,1024]{1,0:T(8,128)(2,1)} %copy-done.3, ...), custom_call_target="tpu_custom_call" | custom-call | flops 5000000000 | bytes 10000000 | tf_op jit(solution)/shard_map/weight_term/pallas_call | solution.py:204
  136.3 28.6 %all_to_all.16 = bf16[32,16,768]{2,1,0:T(8,128)(2,1)S(1)} all-to-all(bf16[32,16,768]{2,1,0:T(8,128)(2,1)} %bitcast.28), channel_id=1, replica_groups=mesh['x'=4,'zl'=4,'zh'=2,'y'=4,'c'=2] {'zh','zl','y'}, dimensions={0} | all-to-all | bytes 1572864 | tf_op jit(solution)/shard_map/all_to_all | solution.py:316
  165.2 3.7 %collective-permute-start.25 = (bf16[4,16,768]{2,1,0:T(8,128)(2,1)S(1)}, bf16[4,16,768]{2,1,0:T(8,128)(2,1)S(1)}, u32[]{:S(2)}, u32[]{:S(2)}) collective-permute-start(bf16[4,16,768]{2,1,0:T(8,128)(2,1)S(1)} %reduce_sum.12), channel_id=1, source_target_pairs={{0,32},{16,48},{32,0},{48,16},{1,33},{17,49},{33,1},{49,17},{2,34}... | collective-permute-start | bytes 294920 | tf_op jit(solution)/shard_map/ppermute | solution.py:253
  170.8 2.8 %collective-permute-done.25 = bf16[4,16,768]{2,1,0:T(8,128)(2,1)S(1)} collective-permute-done((bf16[4,16,768]{2,1,0:T(8,128)(2,1)S(1)}, bf16[4,16,768]{2,1,0:T(8,128)(2,1)S(1)}, u32[]{:S(2)}, u32[]{:S(2)}) %collective-permute-start.25) | collective-permute-done | bytes 98336 | tf_op jit(solution)/shard_map/ppermute | solution.py:253
  173.6 2.8 %collective-permute-done.26 = bf16[4,16,768]{2,1,0:T(8,128)(2,1)S(1)} collective-permute-done((bf16[4,16,768]{2,1,0:T(8,128)(2,1)S(1)}, bf16[4,16,768]{2,1,0:T(8,128)(2,1)S(1)}, u32[]{:S(2)}, u32[]{:S(2)}) %collective-permute-start.26) | collective-permute-done | bytes 98336 | tf_op jit(solution)/shard_map/ppermute | solution.py:253
  181.7 7.6 %collective-permute-done.27.refs_1_ = bf16[4,4,16,768]{3,2,1,0:T(8,128)(2,1)S(1)} collective-permute-done((bf16[4,4,16,768]{3,2,1,0:T(8,128)(2,1)S(1)}, bf16[4,4,16,768]{3,2,1,0:T(8,128)(2,1)S(1)}, u32[]{:S(2)}, u32[]{:S(2)}) %collective-permute-start.27) | collective-permute-done | bytes 393248 | tf_op jit(solution)/shard_map/ppermute | solution.py:253
  189.3 8.5 %collective-permute-done.28.refs_2_ = bf16[4,4,16,768]{3,2,1,0:T(8,128)(2,1)S(1)} collective-permute-done((bf16[4,4,16,768]{3,2,1,0:T(8,128)(2,1)S(1)}, bf16[4,4,16,768]{3,2,1,0:T(8,128)(2,1)S(1)}, u32[]{:S(2)}, u32[]{:S(2)}) %collective-permute-start.28) | collective-permute-done | bytes 393248 | tf_op jit(solution)/shard_map/ppermute | solution.py:253
  199.3 3.3 %finish.1 = (f32[256,2048]{1,0:T(8,128)}, f32[256,512]{1,0:T(8,128)}, f32[256,512]{1,0:T(8,128)}) custom-call(s32[5]{0:T(128)} %stack.47.ids, bf16[4,4,16,768]{3,2,1,0:T(8,128)(2,1)} %copy-done, bf16[4,4,16,768]{3,2,1,0:T(8,128)(2,1)} %copy-done.10, bf16[4,4,16,768]{3,2,1,0:T(8,128)(2,1)} %copy-done.11, bf16[4,4,16,768]{3,2,1,0:T(8,128)(2,1)} %copy-done.12), custom_call_target="tpu_custom_call" | custom-call | tf_op jit(solution)/shard_map/finish/pallas_call | solution.py:238
  (130 shorter events, 42.9 us)
Async XLA Ops:
  7.0 11.2 %collective-permute-start.1 = (bf16[4,512,128]{2,1,0:T(8,128)(2,1)}, bf16[4,512,128]{2,1,0:T(8,128)(2,1)S(1)}, u32[]{:S(2)}, u32[]{:S(2)}) collective-permute-start(bf16[4,512,128]{2,1,0:T(8,128)(2,1)} %get-tuple-element.46), channel_id=1, source_target_pairs={{0,1},{1,0},{2,3},{3,2},{4,5},{5,4},{6,7},{7,6},{8,9},{9,8},{10,11... | collective-permute-start | bytes 1572872 | tf_op jit(solution)/shard_map/ppermute | solution.py:253
  7.0 28.4 %all-to-all-start = ((bf16[8,128,512]{2,1,0:T(8,128)(2,1)}), bf16[8,128,512]{2,1,0:T(8,128)(2,1)S(1)}, u32[]{:S(2)}, u32[]{:S(2)}) async-start(bf16[8,128,512]{2,1,0:T(8,128)(2,1)} %maximum_bitcast_fusion), calls=%async_computation | async-start | bytes 2097152 | tf_op jit(solution)/shard_map/all_to_all | solution.py:280
  11.9 18.6 %collective-permute-start = (bf16[128,1024]{1,0:T(8,128)(2,1)S(1)}, bf16[128,1024]{1,0:T(8,128)(2,1)S(1)}, u32[]{:S(2)}, u32[]{:S(2)}) collective-permute-start(bf16[128,1024]{1,0:T(8,128)(2,1)S(1)} %pad_maximum_fusion.5), channel_id=1, source_target_pairs={{0,8},{8,0},{1,9},{9,1},{2,10},{10,2},{3,11},{11,3},{4,12},{12,4},... | collective-permute-start | bytes 786440 | tf_op jit(solution)/shard_map/ppermute | solution.py:253
  19.3 12.6 %collective-permute-start.2 = (bf16[512,256]{1,0:T(8,128)(2,1)}, bf16[512,256]{1,0:T(8,128)(2,1)S(1)}, u32[]{:S(2)}, u32[]{:S(2)}) collective-permute-start(bf16[512,256]{1,0:T(8,128)(2,1)} %get-tuple-element.86), channel_id=1, source_target_pairs={{0,64},{64,128},{128,192},{192,0},{1,65},{65,129},{129,193},{193,1... | collective-permute-start | bytes 786440 | tf_op jit(solution)/shard_map/ppermute | solution.py:253
  20.8 14.6 %collective-permute-start.3 = (bf16[512,256]{1,0:T(8,128)(2,1)}, bf16[512,256]{1,0:T(8,128)(2,1)S(1)}, u32[]{:S(2)}, u32[]{:S(2)}) collective-permute-start(bf16[512,256]{1,0:T(8,128)(2,1)} %get-tuple-element.85), channel_id=1, source_target_pairs={{0,128},{64,192},{128,0},{192,64},{1,129},{65,193},{129,1},{193,65... | collective-permute-start | bytes 786440 | tf_op jit(solution)/shard_map/ppermute | solution.py:253
  23.5 11.9 %collective-permute-start.4 = (bf16[512,256]{1,0:T(8,128)(2,1)}, bf16[512,256]{1,0:T(8,128)(2,1)S(1)}, u32[]{:S(2)}, u32[]{:S(2)}) collective-permute-start(bf16[512,256]{1,0:T(8,128)(2,1)} %get-tuple-element.84), channel_id=1, source_target_pairs={{0,192},{64,0},{128,64},{192,128},{1,193},{65,1},{129,65},{193,129... | collective-permute-start | bytes 786440 | tf_op jit(solution)/shard_map/ppermute | solution.py:253
  49.1 20.4 %collective-permute-start.7 = (bf16[256,1024]{1,0:T(8,128)(2,1)S(1)}, bf16[256,1024]{1,0:T(8,128)(2,1)S(1)}, u32[]{:S(2)}, u32[]{:S(2)}) collective-permute-start(bf16[256,1024]{1,0:T(8,128)(2,1)S(1)} %pad_maximum_fusion.3.refs_4_), channel_id=1, source_target_pairs={{0,6},{2,0},{4,2},{6,4},{1,7},{3,1},{5,3},{7,5},{8,14},{10,8},{12,... | collective-permute-start | bytes 1572872 | tf_op jit(solution)/shard_map/ppermute | solution.py:253
  49.1 20.4 %collective-permute-start.9 = (bf16[256,1024]{1,0:T(8,128)(2,1)S(1)}, bf16[256,1024]{1,0:T(8,128)(2,1)S(1)}, u32[]{:S(2)}, u32[]{:S(2)}) collective-permute-start(bf16[256,1024]{1,0:T(8,128)(2,1)S(1)} %pad_maximum_fusion.3.refs_4_), channel_id=1, source_target_pairs={{0,2},{2,4},{4,6},{6,0},{1,3},{3,5},{5,7},{7,1},{8,10},{10,12},{12... | collective-permute-start | bytes 1572872 | tf_op jit(solution)/shard_map/ppermute | solution.py:253
  52.4 22.2 %collective-permute-start.6 = (bf16[256,1024]{1,0:T(8,128)(2,1)S(1)}, bf16[256,1024]{1,0:T(8,128)(2,1)S(1)}, u32[]{:S(2)}, u32[]{:S(2)}) collective-permute-start(bf16[256,1024]{1,0:T(8,128)(2,1)S(1)} %pad_maximum_fusion.2.refs_0_), channel_id=1, source_target_pairs={{0,2},{2,4},{4,6},{6,0},{1,3},{3,5},{5,7},{7,1},{8,10},{10,12},{12... | collective-permute-start | bytes 1572872 | tf_op jit(solution)/shard_map/ppermute | solution.py:253
  53.4 22.0 %collective-permute-start.8 = (bf16[256,1024]{1,0:T(8,128)(2,1)S(1)}, bf16[256,1024]{1,0:T(8,128)(2,1)S(1)}, u32[]{:S(2)}, u32[]{:S(2)}) collective-permute-start(bf16[256,1024]{1,0:T(8,128)(2,1)S(1)} %pad_maximum_fusion.2.refs_0_), channel_id=1, source_target_pairs={{0,6},{2,0},{4,2},{6,4},{1,7},{3,1},{5,3},{7,5},{8,14},{10,8},{12,... | collective-permute-start | bytes 1572872 | tf_op jit(solution)/shard_map/ppermute | solution.py:253
  75.4 15.8 %collective-permute-start.13 = (bf16[1024,256]{1,0:T(8,128)(2,1)}, bf16[1024,256]{1,0:T(8,128)(2,1)S(1)}, u32[]{:S(2)}, u32[]{:S(2)}) collective-permute-start(bf16[1024,256]{1,0:T(8,128)(2,1)} %get-tuple-element.71.refs_8_), channel_id=1, source_target_pairs={{0,64},{64,128},{128,192},{192,0},{1,65},{65,129},{129,193},{193,1... | collective-permute-start | bytes 1572872 | tf_op jit(solution)/shard_map/ppermute | solution.py:253
  76.7 26.1 %collective-permute-start.14 = (bf16[1024,256]{1,0:T(8,128)(2,1)}, bf16[1024,256]{1,0:T(8,128)(2,1)S(1)}, u32[]{:S(2)}, u32[]{:S(2)}) collective-permute-start(bf16[1024,256]{1,0:T(8,128)(2,1)} %get-tuple-element.71.refs_8_), channel_id=1, source_target_pairs={{0,128},{64,192},{128,0},{192,64},{1,129},{65,193},{129,1},{193,65... | collective-permute-start | bytes 1572872 | tf_op jit(solution)/shard_map/ppermute | solution.py:253
  79.1 23.9 %collective-permute-start.15 = (bf16[1024,256]{1,0:T(8,128)(2,1)}, bf16[1024,256]{1,0:T(8,128)(2,1)S(1)}, u32[]{:S(2)}, u32[]{:S(2)}) collective-permute-start(bf16[1024,256]{1,0:T(8,128)(2,1)} %get-tuple-element.71.refs_8_), channel_id=1, source_target_pairs={{0,192},{64,0},{128,64},{192,128},{1,193},{65,1},{129,65},{193,129... | collective-permute-start | bytes 1572872 | tf_op jit(solution)/shard_map/ppermute | solution.py:253
  81.8 21.2 %collective-permute-start.11 = (bf16[256,1024]{1,0:T(8,128)(2,1)S(1)}, bf16[256,1024]{1,0:T(8,128)(2,1)}, u32[]{:S(2)}, u32[]{:S(2)}) collective-permute-start(bf16[256,1024]{1,0:T(8,128)(2,1)S(1)} %collective-permute-done.6.refs_1_), channel_id=1, source_target_pairs={{0,2},{2,4},{4,6},{6,0},{1,3},{3,5},{5,7},{7,1},{8,10},{10,12},{12... | collective-permute-start | bytes 1572872 | tf_op jit(solution)/shard_map/ppermute | solution.py:253
  85.1 17.9 %collective-permute-start.12 = (bf16[1024,128]{1,0:T(8,128)(2,1)S(1)}, bf16[1024,128]{1,0:T(8,128)(2,1)S(1)}, u32[]{:S(2)}, u32[]{:S(2)}) collective-permute-start(bf16[1024,128]{1,0:T(8,128)(2,1)S(1)} %slice.98), channel_id=1, source_target_pairs={{0,8},{8,0},{1,9},{9,1},{2,10},{10,2},{3,11},{11,3},{4,12},{12,4},... | collective-permute-start | bytes 786440 | tf_op jit(solution)/shard_map/ppermute | solution.py:253
  103.9 15.7 %collective-permute-start.16 = (bf16[256,1024]{1,0:T(8,128)(2,1)S(1)}, bf16[256,1024]{1,0:T(8,128)(2,1)S(1)}, u32[]{:S(2)}, u32[]{:S(2)}) collective-permute-start(bf16[256,1024]{1,0:T(8,128)(2,1)S(1)} %collective-permute-done.7.refs_6_), channel_id=1, source_target_pairs={{0,6},{2,0},{4,2},{6,4},{1,7},{3,1},{5,3},{7,5},{8,14},{10,8},{12,... | collective-permute-start | bytes 1572872 | tf_op jit(solution)/shard_map/ppermute | solution.py:253
  104.5 15.0 %collective-permute-start.17 = (bf16[1024,256]{1,0:T(8,128)(2,1)S(1)}, bf16[1024,256]{1,0:T(8,128)(2,1)S(1)}, u32[]{:S(2)}, u32[]{:S(2)}) collective-permute-start(bf16[1024,256]{1,0:T(8,128)(2,1)S(1)} %copy-done.23), channel_id=1, source_target_pairs={{0,1},{1,0},{2,3},{3,2},{4,5},{5,4},{6,7},{7,6},{8,9},{9,8},{10,11... | collective-permute-start | bytes 1572872 | tf_op jit(solution)/shard_map/ppermute | solution.py:253
  104.8 22.2 %collective-permute-start.19 = (bf16[1024,128]{1,0:T(8,128)(2,1)S(1)}, bf16[1024,128]{1,0:T(8,128)(2,1)S(1)}, u32[]{:S(2)}, u32[]{:S(2)}) collective-permute-start(bf16[1024,128]{1,0:T(8,128)(2,1)S(1)} %add_convert_fusion.refs_8_), channel_id=1, source_target_pairs={{0,64},{64,128},{128,192},{192,0},{1,65},{65,129},{129,193},{193,1... | collective-permute-start | bytes 786440 | tf_op jit(solution)/shard_map/ppermute | solution.py:253
  106.5 20.5 %collective-permute-start.20 = (bf16[1024,128]{1,0:T(8,128)(2,1)S(1)}, bf16[1024,128]{1,0:T(8,128)(2,1)S(1)}, u32[]{:S(2)}, u32[]{:S(2)}) collective-permute-start(bf16[1024,128]{1,0:T(8,128)(2,1)S(1)} %add_convert_fusion.refs_8_), channel_id=1, source_target_pairs={{0,128},{64,192},{128,0},{192,64},{1,129},{65,193},{129,1},{193,65... | collective-permute-start | bytes 786440 | tf_op jit(solution)/shard_map/ppermute | solution.py:253
  108.9 18.1 %collective-permute-start.21 = (bf16[1024,128]{1,0:T(8,128)(2,1)S(1)}, bf16[1024,128]{1,0:T(8,128)(2,1)S(1)}, u32[]{:S(2)}, u32[]{:S(2)}) collective-permute-start(bf16[1024,128]{1,0:T(8,128)(2,1)S(1)} %add_convert_fusion.refs_8_), channel_id=1, source_target_pairs={{0,192},{64,0},{128,64},{192,128},{1,193},{65,1},{129,65},{193,129... | collective-permute-start | bytes 786440 | tf_op jit(solution)/shard_map/ppermute | solution.py:253
  165.2 8.5 %collective-permute-start.25 = (bf16[4,16,768]{2,1,0:T(8,128)(2,1)S(1)}, bf16[4,16,768]{2,1,0:T(8,128)(2,1)S(1)}, u32[]{:S(2)}, u32[]{:S(2)}) collective-permute-start(bf16[4,16,768]{2,1,0:T(8,128)(2,1)S(1)} %reduce_sum.12), channel_id=1, source_target_pairs={{0,32},{16,48},{32,0},{48,16},{1,33},{17,49},{33,1},{49,17},{2,34}... | collective-permute-start | bytes 294920 | tf_op jit(solution)/shard_map/ppermute | solution.py:253
  176.5 12.7 %collective-permute-start.27 = (bf16[4,4,16,768]{3,2,1,0:T(8,128)(2,1)S(1)}, bf16[4,4,16,768]{3,2,1,0:T(8,128)(2,1)S(1)}, u32[]{:S(2)}, u32[]{:S(2)}) collective-permute-start(bf16[4,4,16,768]{3,2,1,0:T(8,128)(2,1)S(1)} %pad_maximum_fusion.4.refs_0_), channel_id=1, source_target_pairs={{0,64},{64,128},{128,192},{192,0},{1,65},{65,129},{129,193},{193,1... | collective-permute-start | bytes 1179656 | tf_op jit(solution)/shard_map/ppermute | solution.py:253
  178.0 19.8 %collective-permute-start.28 = (bf16[4,4,16,768]{3,2,1,0:T(8,128)(2,1)S(1)}, bf16[4,4,16,768]{3,2,1,0:T(8,128)(2,1)S(1)}, u32[]{:S(2)}, u32[]{:S(2)}) collective-permute-start(bf16[4,4,16,768]{3,2,1,0:T(8,128)(2,1)S(1)} %pad_maximum_fusion.4.refs_0_), channel_id=1, source_target_pairs={{0,128},{64,192},{128,0},{192,64},{1,129},{65,193},{129,1},{193,65... | collective-permute-start | bytes 1179656 | tf_op jit(solution)/shard_map/ppermute | solution.py:253
  180.4 17.5 %collective-permute-start.29 = (bf16[4,4,16,768]{3,2,1,0:T(8,128)(2,1)S(1)}, bf16[4,4,16,768]{3,2,1,0:T(8,128)(2,1)S(1)}, u32[]{:S(2)}, u32[]{:S(2)}) collective-permute-start(bf16[4,4,16,768]{3,2,1,0:T(8,128)(2,1)S(1)} %pad_maximum_fusion.4.refs_0_), channel_id=1, source_target_pairs={{0,192},{64,0},{128,64},{192,128},{1,193},{65,1},{129,65},{193,129... | collective-permute-start | bytes 1179656 | tf_op jit(solution)/shard_map/ppermute | solution.py:253
  (35 other events, 326.9 us)

commit v5 on v4

--- a/solution.py
+++ b/solution.py
@@ -303,8 +303,9 @@
     both, xa_up = lax.optimization_barrier((both, xa_up))
     xa_far = shift(xa_up, "y", NY, 1)
     got = shift(both[OWN:].astype(jnp.bfloat16), "zh", NZH, 1)
-    got, xb_down, *dqs = lax.optimization_barrier((got, xb_down, *dqs))
+    dqs[1], xb_down = lax.optimization_barrier((dqs[1], xb_down))
     xb_far = shift(xb_down, "y", NY, -1)
+    got, xb_far, *dqs = lax.optimization_barrier((got, xb_far, *dqs))
     xa_far, *dqs = lax.optimization_barrier((xa_far, *dqs))
     x_all = [xa, xa_up, xa_down, xa_far, xb, xb_up, xb_down, xb_far]
     mine = (both[:OWN] + got.astype(jnp.float32)).astype(jnp.bfloat16)

time: 203 us -> 204 us (level)
  starting transfers between devices: 49 us -> 45.9 us
  waiting for transfers between devices: 63.6 us -> 66 us
    ppermute x30, starting transfers between devices: 44.1 us -> 41.1 us  [shift(): return lax.ppermute(value, axis, [(i, (i + s) % n) for i in range(n)])]
    ppermute x30, waiting for transfers between devices: 63.6 us -> 66 us  [shift(): return lax.ppermute(value, axis, [(i, (i + s) % n) for i in range(n)])]
    unnamed x59 -> x61, local copies, waits for them, and re-layouts: 7.02 us -> 7.65 us
  transfers between devices with their start and end apart: 31 -> 31, of which waited for: 15 -> 16; matrix products, arithmetic and copies ran while one was open for 3% -> 3% of each run, Pallas kernels for 10% -> 10%
where the time goes in v5:
time: 204 us
  waiting for transfers between devices  66 us (32%)
  starting transfers between devices  45.9 us (22%)
  blocking collectives  42.3 us (21%)
  Pallas kernels  31.9 us (16%)
  local copies, waits for them, and re-layouts  13 us (6%)
  other arithmetic  3.42 us (2%)
    ppermute x30, waiting for transfers between devices, shift(): return lax.ppermute(value, axis, [(i, (i + s) % n) for i in range(n)])  66 us
    ppermute x30, starting transfers between devices, shift(): return lax.ppermute(value, axis, [(i, (i + s) % n) for i in range(n)])  41.1 us
    all_to_all x1, blocking collectives, shards(): lax.all_to_all(part.reshape(NZH * NZL * NY, sub, cols), ('zh', 'zl', 'y')...  29.4 us
    pallas_call x1, Pallas kernels, attention(): pl.pallas_call(attention_kernel, out_shape=(jax.ShapeDtypeStruct((OWN, 2...  14.5 us
    all_to_all x1, blocking collectives, shards(): kv = lax.all_to_all(send, ('y', 'c'), 0, 0, tiled=True)  12.9 us
    pallas_call x2, Pallas kernels, weight_term(): pl.pallas_call(functools.partial(weight_kernel, before is not None), out_...  11.6 us
    unnamed x61, local copies, waits for them, and re-layouts  7.65 us
    all_to_all x1, starting transfers between devices, shards(): own = lax.all_to_all(send, ('y', 'c'), 0, 0, tiled=True)  4.84 us
  transfers between devices with their start and end apart: 31, of which 16 were waited for; matrix products, arithmetic and copies ran while one was open for 3% of the time, Pallas kernels for 10%

profile of v5, /device:TPU:56, one launch (start us, length us, event | category | flops | bytes accessed | tf_op | source)
XLA Modules:
  0.0 203.6 jit_solution(15236758374526743625)
XLA Ops:
  7.1 4.8 %all-to-all-start = ((bf16[8,128,512]{2,1,0:T(8,128)(2,1)}), bf16[8,128,512]{2,1,0:T(8,128)(2,1)S(1)}, u32[]{:S(2)}, u32[]{:S(2)}) async-start(bf16[8,128,512]{2,1,0:T(8,128)(2,1)} %maximum_bitcast_fusion), calls=%async_computation | async-start | bytes 2097152 | tf_op jit(solution)/shard_map/all_to_all | solution.py:280
  11.9 6.3 %collective-permute-start = (bf16[128,1024]{1,0:T(8,128)(2,1)S(1)}, bf16[128,1024]{1,0:T(8,128)(2,1)S(1)}, u32[]{:S(2)}, u32[]{:S(2)}) collective-permute-start(bf16[128,1024]{1,0:T(8,128)(2,1)S(1)} %pad_maximum_fusion.5), channel_id=1, source_target_pairs={{0,8},{8,0},{1,9},{9,1},{2,10},{10,2},{3,11},{11,3},{4,12},{12,4},... | collective-permute-start | bytes 786440 | tf_op jit(solution)/shard_map/ppermute | solution.py:253
  20.8 2.7 %collective-permute-start.3 = (bf16[512,256]{1,0:T(8,128)(2,1)}, bf16[512,256]{1,0:T(8,128)(2,1)S(1)}, u32[]{:S(2)}, u32[]{:S(2)}) collective-permute-start(bf16[512,256]{1,0:T(8,128)(2,1)} %get-tuple-element.89), channel_id=1, source_target_pairs={{0,128},{64,192},{128,0},{192,64},{1,129},{65,193},{129,1},{193,65... | collective-permute-start | bytes 786440 | tf_op jit(solution)/shard_map/ppermute | solution.py:253
  25.4 5.1 %collective-permute-done = bf16[128,1024]{1,0:T(8,128)(2,1)S(1)} collective-permute-done((bf16[128,1024]{1,0:T(8,128)(2,1)S(1)}, bf16[128,1024]{1,0:T(8,128)(2,1)S(1)}, u32[]{:S(2)}, u32[]{:S(2)}) %collective-permute-start) | collective-permute-done | bytes 262176 | tf_op jit(solution)/shard_map/ppermute | solution.py:253
  32.0 3.5 %collective-permute-done.3 = bf16[512,256]{1,0:T(8,128)(2,1)S(1)} collective-permute-done((bf16[512,256]{1,0:T(8,128)(2,1)}, bf16[512,256]{1,0:T(8,128)(2,1)S(1)}, u32[]{:S(2)}, u32[]{:S(2)}) %collective-permute-start.3) | collective-permute-done | bytes 262176 | tf_op jit(solution)/shard_map/ppermute | solution.py:253
  35.4 12.9 %all_to_all.15.kv = bf16[8,128,256]{2,1,0:T(8,128)(2,1)S(1)} all-to-all(bf16[8,128,256]{2,1,0:T(8,128)(2,1)S(1)} %reshape.28), channel_id=1, replica_groups=mesh['x'=4,'zl'=4,'zh'=2,'y'=4,'c'=2] {'y','c'}, dimensions={0} | all-to-all | bytes 1048576 | tf_op jit(solution)/shard_map/all_to_all | solution.py:292
  49.2 3.2 %collective-permute-start.9 = (bf16[256,1024]{1,0:T(8,128)(2,1)S(1)}, bf16[256,1024]{1,0:T(8,128)(2,1)S(1)}, u32[]{:S(2)}, u32[]{:S(2)}) collective-permute-start(bf16[256,1024]{1,0:T(8,128)(2,1)S(1)} %pad_maximum_fusion.3.refs_4_), channel_id=1, source_target_pairs={{0,2},{2,4},{4,6},{6,0},{1,3},{3,5},{5,7},{7,1},{8,10},{10,12},{12... | collective-permute-start | bytes 1572872 | tf_op jit(solution)/shard_map/ppermute | solution.py:253
  55.4 14.5 %attention_backward.1 = (bf16[1024,256]{1,0:T(8,128)(2,1)}, bf16[2048,128]{1,0:T(8,128)(2,1)}, bf16[2048,128]{1,0:T(8,128)(2,1)}) custom-call(s32[5]{0:T(128)} %stack.47.ids, s32[32]{0:T(128)} %span.1, s32[1,8]{1,0:T(1,128)} %lens.1, bf16[8,128,512]{2,1,0:T(8,128)(2,1)} %copy-done.1, bf16[8,128,256]{2,1,0:T(8,128)(2,1)} %copy-done.5, ...), custom_call_target="tpu_custom_call" | custom-call | flops 14000000000 | bytes 28000000 | tf_op jit(solution)/shard_map/attention_backward/pallas_call | solution.py:123
  69.9 4.8 %collective-permute-done.6.refs_1_ = bf16[256,1024]{1,0:T(8,128)(2,1)S(1)} collective-permute-done((bf16[256,1024]{1,0:T(8,128)(2,1)S(1)}, bf16[256,1024]{1,0:T(8,128)(2,1)S(1)}, u32[]{:S(2)}, u32[]{:S(2)}) %collective-permute-start.6) | collective-permute-done | bytes 524320 | tf_op jit(solution)/shard_map/ppermute | solution.py:253
  80.7 10.5 %collective-permute-done.13.refs_9_ = bf16[1024,256]{1,0:T(8,128)(2,1)S(1)} collective-permute-done((bf16[1024,256]{1,0:T(8,128)(2,1)}, bf16[1024,256]{1,0:T(8,128)(2,1)S(1)}, u32[]{:S(2)}, u32[]{:S(2)}) %collective-permute-start.13) | collective-permute-done | bytes 524320 | tf_op jit(solution)/shard_map/ppermute | solution.py:253
  93.0 2.7 %collective-permute-start.11 = (bf16[256,1024]{1,0:T(8,128)(2,1)S(1)}, bf16[256,1024]{1,0:T(8,128)(2,1)S(1)}, u32[]{:S(2)}, u32[]{:S(2)}) collective-permute-start(bf16[256,1024]{1,0:T(8,128)(2,1)S(1)} %collective-permute-done.6.refs_1_), channel_id=1, source_target_pairs={{0,2},{2,4},{4,6},{6,0},{1,3},{3,5},{5,7},{7,1},{8,10},{10,12},{12... | collective-permute-start | bytes 1572872 | tf_op jit(solution)/shard_map/ppermute | solution.py:253
  97.4 4.1 %collective-permute-done.15.refs_10_ = bf16[1024,256]{1,0:T(8,128)(2,1)S(1)} collective-permute-done((bf16[1024,256]{1,0:T(8,128)(2,1)}, bf16[1024,256]{1,0:T(8,128)(2,1)S(1)}, u32[]{:S(2)}, u32[]{:S(2)}) %collective-permute-start.15) | collective-permute-done | bytes 524320 | tf_op jit(solution)/shard_map/ppermute | solution.py:253
  103.3 5.8 %collective-permute-done.12 = bf16[1024,128]{1,0:T(8,128)(2,1)S(1)} collective-permute-done((bf16[1024,128]{1,0:T(8,128)(2,1)S(1)}, bf16[1024,128]{1,0:T(8,128)(2,1)S(1)}, u32[]{:S(2)}, u32[]{:S(2)}) %collective-permute-start.12) | collective-permute-done | bytes 262176 | tf_op jit(solution)/shard_map/ppermute | solution.py:253
  117.2 6.5 %weight_term.2.refs_16_ = bf16[2,4,4,16,512]{4,3,2,1,0:T(8,128)(2,1)} custom-call(s32[5]{0:T(128)} %stack.47.ids, bf16[256,1024]{1,0:T(8,128)(2,1)} %copy-done.4, bf16[256,1024]{1,0:T(8,128)(2,1)} %copy-done.21, bf16[256,1024]{1,0:T(8,128)(2,1)} %copy-done.22, bf16[256,1024]{1,0:T(8,128)(2,1)} %copy-done.25, bf16[256,1024]{1,0:T(8,128)(2,1)} %copy-done.3, ...), custom_call_target="tpu_custom_call" | custom-call | flops 5000000000 | bytes 10000000 | tf_op jit(solution)/shard_map/weight_term/pallas_call | solution.py:204
  123.8 2.6 %collective-permute-done.19.refs_9_ = bf16[1024,128]{1,0:T(8,128)(2,1)S(1)} collective-permute-done((bf16[1024,128]{1,0:T(8,128)(2,1)S(1)}, bf16[1024,128]{1,0:T(8,128)(2,1)S(1)}, u32[]{:S(2)}, u32[]{:S(2)}) %collective-permute-start.19) | collective-permute-done | bytes 262176 | tf_op jit(solution)/shard_map/ppermute | solution.py:253
  131.1 5.1 %weight_term.3 = bf16[2,4,4,16,768]{4,3,2,1,0:T(8,128)(2,1)} custom-call(s32[5]{0:T(128)} %stack.47.ids, bf16[256,1024]{1,0:T(8,128)(2,1)} %copy-done.4, bf16[256,1024]{1,0:T(8,128)(2,1)} %copy-done.21, bf16[256,1024]{1,0:T(8,128)(2,1)} %copy-done.22, bf16[256,1024]{1,0:T(8,128)(2,1)} %copy-done.25, bf16[256,1024]{1,0:T(8,128)(2,1)} %copy-done.3, ...), custom_call_target="tpu_custom_call" | custom-call | flops 5000000000 | bytes 10000000 | tf_op jit(solution)/shard_map/weight_term/pallas_call | solution.py:204
  136.2 29.4 %all_to_all.16 = bf16[32,16,768]{2,1,0:T(8,128)(2,1)S(1)} all-to-all(bf16[32,16,768]{2,1,0:T(8,128)(2,1)} %bitcast.28), channel_id=1, replica_groups=mesh['x'=4,'zl'=4,'zh'=2,'y'=4,'c'=2] {'zh','zl','y'}, dimensions={0} | all-to-all | bytes 1572864 | tf_op jit(solution)/shard_map/all_to_all | solution.py:317
  165.9 3.7 %collective-permute-start.25 = (bf16[4,16,768]{2,1,0:T(8,128)(2,1)S(1)}, bf16[4,16,768]{2,1,0:T(8,128)(2,1)S(1)}, u32[]{:S(2)}, u32[]{:S(2)}) collective-permute-start(bf16[4,16,768]{2,1,0:T(8,128)(2,1)S(1)} %reduce_sum.12), channel_id=1, source_target_pairs={{0,32},{16,48},{32,0},{48,16},{1,33},{17,49},{33,1},{49,17},{2,34}... | collective-permute-start | bytes 294920 | tf_op jit(solution)/shard_map/ppermute | solution.py:253
  171.5 2.8 %collective-permute-done.25 = bf16[4,16,768]{2,1,0:T(8,128)(2,1)S(1)} collective-permute-done((bf16[4,16,768]{2,1,0:T(8,128)(2,1)S(1)}, bf16[4,16,768]{2,1,0:T(8,128)(2,1)S(1)}, u32[]{:S(2)}, u32[]{:S(2)}) %collective-permute-start.25) | collective-permute-done | bytes 98336 | tf_op jit(solution)/shard_map/ppermute | solution.py:253
  174.3 2.8 %collective-permute-done.26 = bf16[4,16,768]{2,1,0:T(8,128)(2,1)S(1)} collective-permute-done((bf16[4,16,768]{2,1,0:T(8,128)(2,1)S(1)}, bf16[4,16,768]{2,1,0:T(8,128)(2,1)S(1)}, u32[]{:S(2)}, u32[]{:S(2)}) %collective-permute-start.26) | collective-permute-done | bytes 98336 | tf_op jit(solution)/shard_map/ppermute | solution.py:253
  178.5 2.9 %collective-permute-start.28 = (bf16[4,4,16,768]{3,2,1,0:T(8,128)(2,1)S(1)}, bf16[4,4,16,768]{3,2,1,0:T(8,128)(2,1)S(1)}, u32[]{:S(2)}, u32[]{:S(2)}) collective-permute-start(bf16[4,4,16,768]{3,2,1,0:T(8,128)(2,1)S(1)} %pad_maximum_fusion.4.refs_0_), channel_id=1, source_target_pairs={{0,128},{64,192},{128,0},{192,64},{1,129},{65,193},{129,1},{193,65... | collective-permute-start | bytes 1179656 | tf_op jit(solution)/shard_map/ppermute | solution.py:253
  181.8 7.8 %collective-permute-done.27.refs_1_ = bf16[4,4,16,768]{3,2,1,0:T(8,128)(2,1)S(1)} collective-permute-done((bf16[4,4,16,768]{3,2,1,0:T(8,128)(2,1)S(1)}, bf16[4,4,16,768]{3,2,1,0:T(8,128)(2,1)S(1)}, u32[]{:S(2)}, u32[]{:S(2)}) %collective-permute-start.27) | collective-permute-done | bytes 393248 | tf_op jit(solution)/shard_map/ppermute | solution.py:253
  189.6 9.2 %collective-permute-done.28.refs_2_ = bf16[4,4,16,768]{3,2,1,0:T(8,128)(2,1)S(1)} collective-permute-done((bf16[4,4,16,768]{3,2,1,0:T(8,128)(2,1)S(1)}, bf16[4,4,16,768]{3,2,1,0:T(8,128)(2,1)S(1)}, u32[]{:S(2)}, u32[]{:S(2)}) %collective-permute-start.28) | collective-permute-done | bytes 393248 | tf_op jit(solution)/shard_map/ppermute | solution.py:253
  200.3 3.3 %finish.1 = (f32[256,2048]{1,0:T(8,128)}, f32[256,512]{1,0:T(8,128)}, f32[256,512]{1,0:T(8,128)}) custom-call(s32[5]{0:T(128)} %stack.47.ids, bf16[4,4,16,768]{3,2,1,0:T(8,128)(2,1)} %copy-done, bf16[4,4,16,768]{3,2,1,0:T(8,128)(2,1)} %copy-done.10, bf16[4,4,16,768]{3,2,1,0:T(8,128)(2,1)} %copy-done.11, bf16[4,4,16,768]{3,2,1,0:T(8,128)(2,1)} %copy-done.12), custom_call_target="tpu_custom_call" | custom-call | tf_op jit(solution)/shard_map/finish/pallas_call | solution.py:238
  (132 shorter events, 45.5 us)
Async XLA Ops:
  7.0 11.2 %collective-permute-start.1 = (bf16[4,512,128]{2,1,0:T(8,128)(2,1)}, bf16[4,512,128]{2,1,0:T(8,128)(2,1)S(1)}, u32[]{:S(2)}, u32[]{:S(2)}) collective-permute-start(bf16[4,512,128]{2,1,0:T(8,128)(2,1)} %get-tuple-element.48), channel_id=1, source_target_pairs={{0,1},{1,0},{2,3},{3,2},{4,5},{5,4},{6,7},{7,6},{8,9},{9,8},{10,11... | collective-permute-start | bytes 1572872 | tf_op jit(solution)/shard_map/ppermute | solution.py:253
  7.1 28.4 %all-to-all-start = ((bf16[8,128,512]{2,1,0:T(8,128)(2,1)}), bf16[8,128,512]{2,1,0:T(8,128)(2,1)S(1)}, u32[]{:S(2)}, u32[]{:S(2)}) async-start(bf16[8,128,512]{2,1,0:T(8,128)(2,1)} %maximum_bitcast_fusion), calls=%async_computation | async-start | bytes 2097152 | tf_op jit(solution)/shard_map/all_to_all | solution.py:280
  11.9 18.6 %collective-permute-start = (bf16[128,1024]{1,0:T(8,128)(2,1)S(1)}, bf16[128,1024]{1,0:T(8,128)(2,1)S(1)}, u32[]{:S(2)}, u32[]{:S(2)}) collective-permute-start(bf16[128,1024]{1,0:T(8,128)(2,1)S(1)} %pad_maximum_fusion.5), channel_id=1, source_target_pairs={{0,8},{8,0},{1,9},{9,1},{2,10},{10,2},{3,11},{11,3},{4,12},{12,4},... | collective-permute-start | bytes 786440 | tf_op jit(solution)/shard_map/ppermute | solution.py:253
  19.3 12.6 %collective-permute-start.2 = (bf16[512,256]{1,0:T(8,128)(2,1)}, bf16[512,256]{1,0:T(8,128)(2,1)S(1)}, u32[]{:S(2)}, u32[]{:S(2)}) collective-permute-start(bf16[512,256]{1,0:T(8,128)(2,1)} %get-tuple-element.90), channel_id=1, source_target_pairs={{0,64},{64,128},{128,192},{192,0},{1,65},{65,129},{129,193},{193,1... | collective-permute-start | bytes 786440 | tf_op jit(solution)/shard_map/ppermute | solution.py:253
  20.8 14.6 %collective-permute-start.3 = (bf16[512,256]{1,0:T(8,128)(2,1)}, bf16[512,256]{1,0:T(8,128)(2,1)S(1)}, u32[]{:S(2)}, u32[]{:S(2)}) collective-permute-start(bf16[512,256]{1,0:T(8,128)(2,1)} %get-tuple-element.89), channel_id=1, source_target_pairs={{0,128},{64,192},{128,0},{192,64},{1,129},{65,193},{129,1},{193,65... | collective-permute-start | bytes 786440 | tf_op jit(solution)/shard_map/ppermute | solution.py:253
  23.6 11.9 %collective-permute-start.4 = (bf16[512,256]{1,0:T(8,128)(2,1)}, bf16[512,256]{1,0:T(8,128)(2,1)S(1)}, u32[]{:S(2)}, u32[]{:S(2)}) collective-permute-start(bf16[512,256]{1,0:T(8,128)(2,1)} %get-tuple-element.88), channel_id=1, source_target_pairs={{0,192},{64,0},{128,64},{192,128},{1,193},{65,1},{129,65},{193,129... | collective-permute-start | bytes 786440 | tf_op jit(solution)/shard_map/ppermute | solution.py:253
  49.2 20.7 %collective-permute-start.7 = (bf16[256,1024]{1,0:T(8,128)(2,1)S(1)}, bf16[256,1024]{1,0:T(8,128)(2,1)S(1)}, u32[]{:S(2)}, u32[]{:S(2)}) collective-permute-start(bf16[256,1024]{1,0:T(8,128)(2,1)S(1)} %pad_maximum_fusion.3.refs_4_), channel_id=1, source_target_pairs={{0,6},{2,0},{4,2},{6,4},{1,7},{3,1},{5,3},{7,5},{8,14},{10,8},{12,... | collective-permute-start | bytes 1572872 | tf_op jit(solution)/shard_map/ppermute | solution.py:253
  49.2 20.7 %collective-permute-start.9 = (bf16[256,1024]{1,0:T(8,128)(2,1)S(1)}, bf16[256,1024]{1,0:T(8,128)(2,1)S(1)}, u32[]{:S(2)}, u32[]{:S(2)}) collective-permute-start(bf16[256,1024]{1,0:T(8,128)(2,1)S(1)} %pad_maximum_fusion.3.refs_4_), channel_id=1, source_target_pairs={{0,2},{2,4},{4,6},{6,0},{1,3},{3,5},{5,7},{7,1},{8,10},{10,12},{12... | collective-permute-start | bytes 1572872 | tf_op jit(solution)/shard_map/ppermute | solution.py:253
  52.5 22.2 %collective-permute-start.6 = (bf16[256,1024]{1,0:T(8,128)(2,1)S(1)}, bf16[256,1024]{1,0:T(8,128)(2,1)S(1)}, u32[]{:S(2)}, u32[]{:S(2)}) collective-permute-start(bf16[256,1024]{1,0:T(8,128)(2,1)S(1)} %pad_maximum_fusion.2.refs_0_), channel_id=1, source_target_pairs={{0,2},{2,4},{4,6},{6,0},{1,3},{3,5},{5,7},{7,1},{8,10},{10,12},{12... | collective-permute-start | bytes 1572872 | tf_op jit(solution)/shard_map/ppermute | solution.py:253
  53.4 22.0 %collective-permute-start.8 = (bf16[256,1024]{1,0:T(8,128)(2,1)S(1)}, bf16[256,1024]{1,0:T(8,128)(2,1)S(1)}, u32[]{:S(2)}, u32[]{:S(2)}) collective-permute-start(bf16[256,1024]{1,0:T(8,128)(2,1)S(1)} %pad_maximum_fusion.2.refs_0_), channel_id=1, source_target_pairs={{0,6},{2,0},{4,2},{6,4},{1,7},{3,1},{5,3},{7,5},{8,14},{10,8},{12,... | collective-permute-start | bytes 1572872 | tf_op jit(solution)/shard_map/ppermute | solution.py:253
  75.4 15.8 %collective-permute-start.13 = (bf16[1024,256]{1,0:T(8,128)(2,1)}, bf16[1024,256]{1,0:T(8,128)(2,1)S(1)}, u32[]{:S(2)}, u32[]{:S(2)}) collective-permute-start(bf16[1024,256]{1,0:T(8,128)(2,1)} %get-tuple-element.75.refs_8_), channel_id=1, source_target_pairs={{0,64},{64,128},{128,192},{192,0},{1,65},{65,129},{129,193},{193,1... | collective-permute-start | bytes 1572872 | tf_op jit(solution)/shard_map/ppermute | solution.py:253
  76.7 15.1 %collective-permute-start.10 = (bf16[2048,128]{1,0:T(8,128)(2,1)}, bf16[2048,128]{1,0:T(8,128)(2,1)S(1)}, u32[]{:S(2)}, u32[]{:S(2)}) collective-permute-start(bf16[2048,128]{1,0:T(8,128)(2,1)} %get-tuple-element.59), channel_id=1, source_target_pairs={{0,1},{1,0},{2,3},{3,2},{4,5},{5,4},{6,7},{7,6},{8,9},{9,8},{10,11... | collective-permute-start | bytes 1572872 | tf_op jit(solution)/shard_map/ppermute | solution.py:253
  76.7 24.7 %collective-permute-start.15 = (bf16[1024,256]{1,0:T(8,128)(2,1)}, bf16[1024,256]{1,0:T(8,128)(2,1)S(1)}, u32[]{:S(2)}, u32[]{:S(2)}) collective-permute-start(bf16[1024,256]{1,0:T(8,128)(2,1)} %get-tuple-element.75.refs_8_), channel_id=1, source_target_pairs={{0,128},{64,192},{128,0},{192,64},{1,129},{65,193},{129,1},{193,65... | collective-permute-start | bytes 1572872 | tf_op jit(solution)/shard_map/ppermute | solution.py:253
  79.1 24.2 %collective-permute-start.16 = (bf16[1024,256]{1,0:T(8,128)(2,1)}, bf16[1024,256]{1,0:T(8,128)(2,1)S(1)}, u32[]{:S(2)}, u32[]{:S(2)}) collective-permute-start(bf16[1024,256]{1,0:T(8,128)(2,1)} %get-tuple-element.75.refs_8_), channel_id=1, source_target_pairs={{0,192},{64,0},{128,64},{192,128},{1,193},{65,1},{129,65},{193,129... | collective-permute-start | bytes 1572872 | tf_op jit(solution)/shard_map/ppermute | solution.py:253
  91.2 17.9 %collective-permute-start.14 = (bf16[256,1024]{1,0:T(8,128)(2,1)S(1)}, bf16[256,1024]{1,0:T(8,128)(2,1)S(1)}, u32[]{:S(2)}, u32[]{:S(2)}) collective-permute-start(bf16[256,1024]{1,0:T(8,128)(2,1)S(1)} %collective-permute-done.7.refs_6_), channel_id=1, source_target_pairs={{0,6},{2,0},{4,2},{6,4},{1,7},{3,1},{5,3},{7,5},{8,14},{10,8},{12,... | collective-permute-start | bytes 1572872 | tf_op jit(solution)/shard_map/ppermute | solution.py:253
  93.0 16.9 %collective-permute-start.11 = (bf16[256,1024]{1,0:T(8,128)(2,1)S(1)}, bf16[256,1024]{1,0:T(8,128)(2,1)S(1)}, u32[]{:S(2)}, u32[]{:S(2)}) collective-permute-start(bf16[256,1024]{1,0:T(8,128)(2,1)S(1)} %collective-permute-done.6.refs_1_), channel_id=1, source_target_pairs={{0,2},{2,4},{4,6},{6,0},{1,3},{3,5},{5,7},{7,1},{8,10},{10,12},{12... | collective-permute-start | bytes 1572872 | tf_op jit(solution)/shard_map/ppermute | solution.py:253
  95.7 13.4 %collective-permute-start.12 = (bf16[1024,128]{1,0:T(8,128)(2,1)S(1)}, bf16[1024,128]{1,0:T(8,128)(2,1)S(1)}, u32[]{:S(2)}, u32[]{:S(2)}) collective-permute-start(bf16[1024,128]{1,0:T(8,128)(2,1)S(1)} %slice.98), channel_id=1, source_target_pairs={{0,8},{8,0},{1,9},{9,1},{2,10},{10,2},{3,11},{11,3},{4,12},{12,4},... | collective-permute-start | bytes 786440 | tf_op jit(solution)/shard_map/ppermute | solution.py:253
  111.3 15.1 %collective-permute-start.19 = (bf16[1024,128]{1,0:T(8,128)(2,1)S(1)}, bf16[1024,128]{1,0:T(8,128)(2,1)S(1)}, u32[]{:S(2)}, u32[]{:S(2)}) collective-permute-start(bf16[1024,128]{1,0:T(8,128)(2,1)S(1)} %add_convert_fusion.refs_8_), channel_id=1, source_target_pairs={{0,64},{64,128},{128,192},{192,0},{1,65},{65,129},{129,193},{193,1... | collective-permute-start | bytes 786440 | tf_op jit(solution)/shard_map/ppermute | solution.py:253
  111.4 15.0 %collective-permute-start.20 = (bf16[1024,128]{1,0:T(8,128)(2,1)S(1)}, bf16[1024,128]{1,0:T(8,128)(2,1)S(1)}, u32[]{:S(2)}, u32[]{:S(2)}) collective-permute-start(bf16[1024,128]{1,0:T(8,128)(2,1)S(1)} %add_convert_fusion.refs_8_), channel_id=1, source_target_pairs={{0,128},{64,192},{128,0},{192,64},{1,129},{65,193},{129,1},{193,65... | collective-permute-start | bytes 786440 | tf_op jit(solution)/shard_map/ppermute | solution.py:253
  113.5 13.5 %collective-permute-start.21 = (bf16[1024,128]{1,0:T(8,128)(2,1)S(1)}, bf16[1024,128]{1,0:T(8,128)(2,1)S(1)}, u32[]{:S(2)}, u32[]{:S(2)}) collective-permute-start(bf16[1024,128]{1,0:T(8,128)(2,1)S(1)} %add_convert_fusion.refs_8_), channel_id=1, source_target_pairs={{0,192},{64,0},{128,64},{192,128},{1,193},{65,1},{129,65},{193,129... | collective-permute-start | bytes 786440 | tf_op jit(solution)/shard_map/ppermute | solution.py:253
  165.9 8.5 %collective-permute-start.25 = (bf16[4,16,768]{2,1,0:T(8,128)(2,1)S(1)}, bf16[4,16,768]{2,1,0:T(8,128)(2,1)S(1)}, u32[]{:S(2)}, u32[]{:S(2)}) collective-permute-start(bf16[4,16,768]{2,1,0:T(8,128)(2,1)S(1)} %reduce_sum.12), channel_id=1, source_target_pairs={{0,32},{16,48},{32,0},{48,16},{1,33},{17,49},{33,1},{49,17},{2,34}... | collective-permute-start | bytes 294920 | tf_op jit(solution)/shard_map/ppermute | solution.py:253
  177.2 12.4 %collective-permute-start.27 = (bf16[4,4,16,768]{3,2,1,0:T(8,128)(2,1)S(1)}, bf16[4,4,16,768]{3,2,1,0:T(8,128)(2,1)S(1)}, u32[]{:S(2)}, u32[]{:S(2)}) collective-permute-start(bf16[4,4,16,768]{3,2,1,0:T(8,128)(2,1)S(1)} %pad_maximum_fusion.4.refs_0_), channel_id=1, source_target_pairs={{0,64},{64,128},{128,192},{192,0},{1,65},{65,129},{129,193},{193,1... | collective-permute-start | bytes 1179656 | tf_op jit(solution)/shard_map/ppermute | solution.py:253
  178.5 20.3 %collective-permute-start.28 = (bf16[4,4,16,768]{3,2,1,0:T(8,128)(2,1)S(1)}, bf16[4,4,16,768]{3,2,1,0:T(8,128)(2,1)S(1)}, u32[]{:S(2)}, u32[]{:S(2)}) collective-permute-start(bf16[4,4,16,768]{3,2,1,0:T(8,128)(2,1)S(1)} %pad_maximum_fusion.4.refs_0_), channel_id=1, source_target_pairs={{0,128},{64,192},{128,0},{192,64},{1,129},{65,193},{129,1},{193,65... | collective-permute-start | bytes 1179656 | tf_op jit(solution)/shard_map/ppermute | solution.py:253
  181.4 17.4 %collective-permute-start.29 = (bf16[4,4,16,768]{3,2,1,0:T(8,128)(2,1)S(1)}, bf16[4,4,16,768]{3,2,1,0:T(8,128)(2,1)S(1)}, u32[]{:S(2)}, u32[]{:S(2)}) collective-permute-start(bf16[4,4,16,768]{3,2,1,0:T(8,128)(2,1)S(1)} %pad_maximum_fusion.4.refs_0_), channel_id=1, source_target_pairs={{0,192},{64,0},{128,64},{192,128},{1,193},{65,1},{129,65},{193,129... | collective-permute-start | bytes 1179656 | tf_op jit(solution)/shard_map/ppermute | solution.py:253
  (36 other events, 365.6 us)
